TPU v7x, 32 devices: a whole 2x2x4 slice. The times are simulated.
32 devices in a mesh: dp: 8 (over z, x), tensor: 4 (over y, core).
Axes of the slice: x: 2, y: 2, z: 4, core: 2. Of those that a mesh axis runs over, the one named last changes fastest.
Arguments:
- image_tokens: bfloat16 [8, 768, 1536], P('dp', 'tensor'), may hold values from -6 to 6
- text_tokens: bfloat16 [8, 128, 1536], P('dp', 'tensor'), may hold values from -6 to 6
- condition: bfloat16 [8, 1536], replicated, may hold values from -6 to 6
- image_cot: bfloat16 [8, 768, 1536], P('dp', 'tensor'), may hold values from -6 to 6
- text_cot: bfloat16 [8, 128, 1536], P('dp', 'tensor'), may hold values from -6 to 6
- ada_w: bfloat16 [1, 2, 1536, 9216], P(None, None, 'dp', 'tensor'), may hold values from -3 to 3
- ada_b: bfloat16 [1, 2, 9216], P(None, None, 'tensor'), may hold values from -3 to 3
- qkv_w: bfloat16 [1, 2, 1536, 3, 1536], P(None, None, 'dp', None, 'tensor'), may hold values from -0.15625 to 0.15625
- qv_b: bfloat16 [1, 2, 2, 1536], P(None, None, None, 'tensor'), may hold values from -1 to 1
- out_w: bfloat16 [1, 2, 1536, 1536], P(None, None, 'tensor', 'dp'), may hold values from -1.25 to 1.25
- out_b: bfloat16 [1, 2, 1536], replicated, may hold values from -3 to 3
- up_w: bfloat16 [1, 2, 1536, 6144], P(None, None, 'dp', 'tensor'), may hold values from -0.15625 to 0.15625
- up_b: bfloat16 [1, 2, 6144], P(None, None, 'tensor'), may hold values from -3 to 3
- down_w: bfloat16 [1, 2, 6144, 1536], P(None, None, 'tensor', 'dp'), may hold values from -0.078125 to 0.078125
- down_b: bfloat16 [1, 2, 1536], replicated, may hold values from -3 to 3
Outputs:
- image_out: bfloat16 [8, 768, 1536], P('dp', 'tensor')
- text_out: bfloat16 [8, 128, 1536], P('dp', 'tensor')
- image_grad: float32 [8, 768, 1536], P('dp', 'tensor')
- text_grad: float32 [8, 128, 1536], P('dp', 'tensor')
- cond_grad: float32 [8, 1536], P('dp')
- ada_w_grad: float32 [1, 2, 1536, 9216], P(None, None, 'dp', 'tensor')
- ada_b_grad: float32 [1, 2, 9216], P(None, None, ('tensor', 'dp'))
- qkv_w_grad: float32 [1, 2, 1536, 3, 1536], P(None, None, 'dp', None, 'tensor')
- qv_b_grad: float32 [1, 2, 2, 1536], P(None, None, None, ('tensor', 'dp'))
- out_w_grad: float32 [1, 2, 1536, 1536], P(None, None, 'tensor', 'dp')
- out_b_grad: float32 [1, 2, 1536], P(None, None, ('tensor', 'dp'))
- up_w_grad: float32 [1, 2, 1536, 6144], P(None, None, 'dp', 'tensor')
- up_b_grad: float32 [1, 2, 6144], P(None, None, ('tensor', 'dp'))
- down_w_grad: float32 [1, 2, 6144, 1536], P(None, None, 'tensor', 'dp')
- down_b_grad: float32 [1, 2, 1536], P(None, None, ('tensor', 'dp'))
All inputs are finite; a program needn't handle non-finite values.
Results may differ from a plain program's by a relative error of at most 0.0109.
The roundings to bfloat16 on the way count: a program that leaves them out, or rounds other values in their place, can miss the bound.
Values may be sent and summed in bfloat16 or wider, within the bound.
No kernel may reach another device: no remote copies, remote signals or barrier semaphores. Data moves between devices by JAX's collectives and lax.ppermute only.
A program may use at most 320 MiB of HBM per device.

v0:
```python
import jax
import jax.numpy as jnp
from jax import lax
from jax.sharding import PartitionSpec as P

HEAD = 64
LAYERS = 1


NORM_EPS = 1e-06


def layer_norm(value):
    centered = value - jnp.mean(value, axis=-1, keepdims=True)
    inv_std = lax.rsqrt(jnp.mean(centered * centered, axis=-1, keepdims=True) + NORM_EPS)
    return (centered * inv_std, inv_std)


def norm_back(upstream, normed, inv_std):
    mean_grad = jnp.mean(upstream, axis=-1, keepdims=True)
    mean_proj = jnp.mean(upstream * normed, axis=-1, keepdims=True)
    return inv_std * (upstream - mean_grad - normed * mean_proj)


def gelu_tanh(value):
    return jax.nn.gelu(value, approximate=True)


def gather_rows(first_rows, second_rows):
    return (
        lax.all_gather(first_rows, "tensor", axis=1, tiled=True),
        lax.all_gather(second_rows, "tensor", axis=1, tiled=True),
    )


def gather_grads(first_rows, second_rows):
    return (
        lax.all_gather(first_rows, "tensor", axis=1, tiled=True),
        lax.all_gather(second_rows, "tensor", axis=1, tiled=True),
    )


def reduce_branch(first_rows, second_rows):
    return (
        lax.psum_scatter(first_rows, "tensor", scatter_dimension=1, tiled=True),
        lax.psum_scatter(second_rows, "tensor", scatter_dimension=1, tiled=True),
    )


def reduce_inputs(first_rows, second_rows):
    return (
        lax.psum_scatter(first_rows, "tensor", scatter_dimension=1, tiled=True),
        lax.psum_scatter(second_rows, "tensor", scatter_dimension=1, tiled=True),
    )


def to_heads(packed, head_size):
    batch_size, seq_len, local_width = (packed.shape[0], packed.shape[1], packed.shape[3])
    split_heads = packed.reshape(batch_size, seq_len, 3, local_width // head_size, head_size)
    return split_heads.transpose(2, 3, 0, 1, 4)


def attend(packed, head_size):
    score_scale = head_size ** (-0.5)
    heads_q, heads_k, heads_v = to_heads(packed, head_size)

    def one_head(pieces):
        query_by_head, key_by_head, value_by_head = pieces
        scores = (
            jnp.einsum(
                "cpv,czv->cpz", query_by_head, key_by_head, preferred_element_type=jnp.float32
            )
            * score_scale
        )
        maximum = jnp.max(scores, axis=-1, keepdims=True)
        weights = jnp.exp(scores - maximum)
        totals = jnp.sum(weights, axis=-1, keepdims=True)
        probability_reduced = (weights / totals).astype(jnp.bfloat16)
        attended_output = jnp.einsum(
            "mjg,mgr->mjr", probability_reduced, value_by_head, preferred_element_type=jnp.float32
        )
        return (attended_output.astype(jnp.bfloat16), (maximum + jnp.log(totals))[..., 0])

    attended_output, log_sums = lax.map(one_head, (heads_q, heads_k, heads_v))
    count_heads, batch_size, seq_len = (
        attended_output.shape[0],
        attended_output.shape[1],
        attended_output.shape[2],
    )
    return (
        attended_output.transpose(1, 2, 0, 3).reshape(batch_size, seq_len, count_heads * head_size),
        log_sums,
    )


def attend_back(packed, log_sums, mixed_grad, head_size):
    score_scale = head_size ** (-0.5)
    heads_q, heads_k, heads_v = to_heads(packed, head_size)
    batch_size, seq_len, local_width = mixed_grad.shape
    grad_heads = mixed_grad.reshape(
        batch_size, seq_len, local_width // head_size, head_size
    ).transpose(2, 0, 1, 3)

    def one_head(pieces):
        query_by_head, key_by_head, value_by_head, gradient_by_head, head_lse = pieces
        scores = (
            jnp.einsum(
                "cpv,czv->cpz", query_by_head, key_by_head, preferred_element_type=jnp.float32
            )
            * score_scale
        )
        attention_probs = jnp.exp(scores - head_lse[..., None])
        v_grad = jnp.einsum(
            "yel,yen->yln",
            attention_probs.astype(jnp.bfloat16),
            gradient_by_head,
            preferred_element_type=jnp.float32,
        )
        probability_grad = jnp.einsum(
            "cpv,czv->cpz", gradient_by_head, value_by_head, preferred_element_type=jnp.float32
        )
        row_dots = jnp.sum(probability_grad * attention_probs, axis=-1, keepdims=True)
        score_grad = (attention_probs * (probability_grad - row_dots)).astype(jnp.bfloat16)
        q_grad = (
            jnp.einsum("mjg,mgr->mjr", score_grad, key_by_head, preferred_element_type=jnp.float32)
            * score_scale
        )
        k_grad = (
            jnp.einsum(
                "yel,yen->yln", score_grad, query_by_head, preferred_element_type=jnp.float32
            )
            * score_scale
        )
        return jnp.stack([q_grad, k_grad, v_grad]).astype(jnp.bfloat16)

    stacked = lax.map(one_head, (heads_q, heads_k, heads_v, grad_heads, log_sums))
    count_heads = stacked.shape[0]
    return stacked.transpose(2, 3, 1, 0, 4).reshape(batch_size, seq_len, 3, count_heads * head_size)


def layer_forward(streams, modulation, gathered, biases, head_size):
    w_qkv, w_out, w_up, w_down = gathered
    qv_bias, out_bias, up_bias, down_bias = biases
    normed_one, inv_one, lowered = ([], [], [])
    for stream in range(2):
        normed, inv_std = layer_norm(streams[stream])
        normed_one.append(normed)
        inv_one.append(inv_std)
        shifted = (
            normed * (1.0 + modulation[:, stream, 1][:, None]) + modulation[:, stream, 0][:, None]
        )
        lowered.append(shifted.astype(jnp.bfloat16))
    full_one = gather_rows(lowered[0], lowered[1])
    packed_list = []
    for stream in range(2):
        projected = jnp.einsum(
            "bnd,dkc->bnkc", full_one[stream], w_qkv[stream], preferred_element_type=jnp.float32
        )
        qkv_bias = jnp.stack(
            [qv_bias[stream, 0], jnp.zeros_like(qv_bias[stream, 0]), qv_bias[stream, 1]]
        )
        packed_list.append(projected + qkv_bias)
    packed = jnp.concatenate(packed_list, axis=1).astype(jnp.bfloat16)
    attended_output, log_sums = attend(packed, head_size)
    split_at = full_one[0].shape[1]
    attn_rows = (attended_output[:, :split_at], attended_output[:, split_at:])
    attn_terms = [
        jnp.einsum(
            "bnc,cd->bnd", attn_rows[stream], w_out[stream], preferred_element_type=jnp.float32
        )
        for stream in range(2)
    ]
    attn_sums = reduce_branch(attn_terms[0], attn_terms[1])
    attn_bias, residuals, normed_two, inv_two, lowered_two = ([], [], [], [], [])
    for stream in range(2):
        attn_bias.append(attn_sums[stream] + out_bias[stream])
        residual = streams[stream] + modulation[:, stream, 2][:, None] * attn_bias[stream]
        residuals.append(residual)
        normed, inv_std = layer_norm(residual)
        normed_two.append(normed)
        inv_two.append(inv_std)
        shifted = (
            normed * (1.0 + modulation[:, stream, 4][:, None]) + modulation[:, stream, 3][:, None]
        )
        lowered_two.append(shifted.astype(jnp.bfloat16))
    full_two = gather_rows(lowered_two[0], lowered_two[1])
    pre_acts, act_lows, mlp_terms = ([], [], [])
    for stream in range(2):
        pre_act = (
            jnp.einsum(
                "bnd,df->bnf", full_two[stream], w_up[stream], preferred_element_type=jnp.float32
            )
            + up_bias[stream]
        )
        act_low = gelu_tanh(pre_act).astype(jnp.bfloat16)
        pre_acts.append(pre_act)
        act_lows.append(act_low)
        mlp_terms.append(
            jnp.einsum("bnf,fd->bnd", act_low, w_down[stream], preferred_element_type=jnp.float32)
        )
    mlp_sums = reduce_branch(mlp_terms[0], mlp_terms[1])
    mlp_bias = [mlp_sums[stream] + down_bias[stream] for stream in range(2)]
    outputs = [
        residuals[stream] + modulation[:, stream, 5][:, None] * mlp_bias[stream]
        for stream in range(2)
    ]
    stored = {
        "normed_one": normed_one,
        "inv_one": inv_one,
        "full_one": full_one,
        "packed": packed,
        "log_sums": log_sums,
        "attn_rows": attn_rows,
        "attn_bias": attn_bias,
        "normed_two": normed_two,
        "inv_two": inv_two,
        "full_two": full_two,
        "pre_act": pre_acts,
        "act_low": act_lows,
        "mlp_bias": mlp_bias,
    }
    return (outputs, stored)


def layer_backward(gradients, modulation, gathered, stored, head_size):
    w_qkv, w_out, w_up, w_down = gathered
    gate_two_grad, down_bias_grad, dy_lows = ([], [], [])
    for stream in range(2):
        gate_two_grad.append(jnp.sum(gradients[stream] * stored["mlp_bias"][stream], axis=1))
        scaled = modulation[:, stream, 5][:, None] * gradients[stream]
        down_bias_grad.append(jnp.sum(scaled, axis=(0, 1)))
        dy_lows.append(scaled.astype(jnp.bfloat16))
    dy_full = gather_grads(dy_lows[0], dy_lows[1])
    down_w_grad, up_w_grad, up_b_grad, hidden_terms = ([], [], [], [])
    for stream in range(2):
        down_w_grad.append(
            jnp.einsum(
                "bnf,bnd->fd",
                stored["act_low"][stream],
                dy_full[stream],
                preferred_element_type=jnp.float32,
            )
        )
        act_grad = jnp.einsum(
            "bnd,fd->bnf", dy_full[stream], w_down[stream], preferred_element_type=jnp.float32
        )
        gelu_back = jax.vjp(gelu_tanh, stored["pre_act"][stream])[1]
        pre_grad = gelu_back(act_grad)[0].astype(jnp.bfloat16)
        up_b_grad.append(jnp.sum(pre_grad, axis=(0, 1), dtype=jnp.float32))
        up_w_grad.append(
            jnp.einsum(
                "bnd,bnf->df",
                stored["full_two"][stream],
                pre_grad,
                preferred_element_type=jnp.float32,
            )
        )
        hidden_terms.append(
            jnp.einsum("bnf,df->bnd", pre_grad, w_up[stream], preferred_element_type=jnp.float32)
        )
    hidden_two = reduce_inputs(hidden_terms[0], hidden_terms[1])
    shift_two_grad, scale_two_grad, mid_grads = ([], [], [])
    for stream in range(2):
        shift_two_grad.append(jnp.sum(hidden_two[stream], axis=1))
        scale_two_grad.append(jnp.sum(hidden_two[stream] * stored["normed_two"][stream], axis=1))
        upstream = hidden_two[stream] * (1.0 + modulation[:, stream, 4][:, None])
        mid_grads.append(
            gradients[stream]
            + norm_back(upstream, stored["normed_two"][stream], stored["inv_two"][stream])
        )
    gate_one_grad, out_bias_grad, dz_lows = ([], [], [])
    for stream in range(2):
        gate_one_grad.append(jnp.sum(mid_grads[stream] * stored["attn_bias"][stream], axis=1))
        scaled = modulation[:, stream, 2][:, None] * mid_grads[stream]
        out_bias_grad.append(jnp.sum(scaled, axis=(0, 1)))
        dz_lows.append(scaled.astype(jnp.bfloat16))
    dz_full = gather_grads(dz_lows[0], dz_lows[1])
    out_w_grad, attn_grads = ([], [])
    for stream in range(2):
        out_w_grad.append(
            jnp.einsum(
                "bnc,bnd->cd",
                stored["attn_rows"][stream],
                dz_full[stream],
                preferred_element_type=jnp.float32,
            )
        )
        attn_grads.append(
            jnp.einsum(
                "bnd,cd->bnc", dz_full[stream], w_out[stream], preferred_element_type=jnp.float32
            )
        )
    mixed_grad = jnp.concatenate(attn_grads, axis=1).astype(jnp.bfloat16)
    packed_grad = attend_back(stored["packed"], stored["log_sums"], mixed_grad, head_size)
    split_at = stored["full_one"][0].shape[1]
    stream_grads = (packed_grad[:, :split_at], packed_grad[:, split_at:])
    qkv_w_grad, qv_b_grad, input_terms = ([], [], [])
    for stream in range(2):
        part_grad = stream_grads[stream]
        qkv_w_grad.append(
            jnp.einsum(
                "bnd,bnkc->dkc",
                stored["full_one"][stream],
                part_grad,
                preferred_element_type=jnp.float32,
            )
        )
        summed = jnp.sum(part_grad, axis=(0, 1), dtype=jnp.float32)
        qv_b_grad.append(jnp.stack([summed[0], summed[2]]))
        input_terms.append(
            jnp.einsum(
                "bnkc,dkc->bnd", part_grad, w_qkv[stream], preferred_element_type=jnp.float32
            )
        )
    hidden_one = reduce_inputs(input_terms[0], input_terms[1])
    shift_one_grad, scale_one_grad, new_grads = ([], [], [])
    for stream in range(2):
        shift_one_grad.append(jnp.sum(hidden_one[stream], axis=1))
        scale_one_grad.append(jnp.sum(hidden_one[stream] * stored["normed_one"][stream], axis=1))
        upstream = hidden_one[stream] * (1.0 + modulation[:, stream, 1][:, None])
        new_grads.append(
            mid_grads[stream]
            + norm_back(upstream, stored["normed_one"][stream], stored["inv_one"][stream])
        )
    mod_grad = jnp.stack(
        [
            jnp.stack(
                [
                    shift_one_grad[stream],
                    scale_one_grad[stream],
                    gate_one_grad[stream],
                    shift_two_grad[stream],
                    scale_two_grad[stream],
                    gate_two_grad[stream],
                ],
                axis=1,
            )
            for stream in range(2)
        ],
        axis=1,
    )
    bias_grad = jnp.stack([jnp.stack(out_bias_grad), jnp.stack(down_bias_grad)])
    grad_parts = (
        jnp.stack(qkv_w_grad),
        jnp.stack(out_w_grad),
        up_w_grad[0],
        up_w_grad[1],
        down_w_grad[0],
        down_w_grad[1],
        jnp.stack(qv_b_grad),
        jnp.stack(up_b_grad),
    )
    return (new_grads, grad_parts, mod_grad, bias_grad)


def per_device(
    image_tokens,
    text_tokens,
    condition,
    image_cot,
    text_cot,
    ada_w,
    ada_b,
    qkv_w,
    qv_b,
    out_w,
    out_b,
    up_w,
    up_b,
    down_w,
    down_b,
):
    head_size = HEAD
    batch_size = image_tokens.shape[0]
    model_width = image_tokens.shape[2]
    dp_rank = lax.axis_index("dp")
    cond_full = condition.astype(jnp.float32)
    silu_low = jax.nn.silu(cond_full).astype(jnp.bfloat16)
    own_cond = lax.dynamic_slice_in_dim(cond_full, dp_rank * batch_size, batch_size, 0)
    row_block = ada_w.shape[2]
    own_cols = lax.dynamic_slice_in_dim(silu_low, dp_rank * row_block, row_block, 1)
    streams = [image_tokens.astype(jnp.float32), text_tokens.astype(jnp.float32)]
    layer_num = 0
    kept_ada = None
    mod_terms = jnp.einsum(
        "sr,krc->skc", own_cols, ada_w[layer_num], preferred_element_type=jnp.float32
    )
    mod_local = lax.psum_scatter(mod_terms, "dp", scatter_dimension=0, tiled=True)
    mod_local = mod_local + ada_b[layer_num].astype(jnp.float32)
    mod_full = lax.all_gather(mod_local, "tensor", axis=2, tiled=True)
    modulation = mod_full.reshape(batch_size, 2, 6, model_width)
    gathered = (
        lax.all_gather(qkv_w[layer_num], "dp", axis=1, tiled=True),
        lax.all_gather(out_w[layer_num], "dp", axis=2, tiled=True),
        lax.all_gather(up_w[layer_num], "dp", axis=1, tiled=True),
        lax.all_gather(down_w[layer_num], "dp", axis=2, tiled=True),
    )
    biases = (
        qv_b[layer_num].astype(jnp.float32),
        out_b[layer_num].astype(jnp.float32),
        up_b[layer_num].astype(jnp.float32),
        down_b[layer_num].astype(jnp.float32),
    )
    streams, stored = layer_forward(streams, modulation, gathered, biases, head_size)
    records = [(modulation, gathered, stored, kept_ada)]
    gradients = [image_cot.astype(jnp.float32), text_cot.astype(jnp.float32)]
    layer_grads = [None] * LAYERS
    mod_list = [None] * LAYERS
    bias_list = [None] * LAYERS
    for layer_num in reversed(range(LAYERS)):
        modulation, gathered, stored, kept_ada = records[layer_num]
        gradients, grad_parts, mod_grad, bias_grad = layer_backward(
            gradients, modulation, gathered, stored, head_size
        )
        layer_grads[layer_num] = (
            lax.psum_scatter(grad_parts[0], "dp", scatter_dimension=1, tiled=True),
            lax.psum_scatter(grad_parts[1], "dp", scatter_dimension=2, tiled=True),
            lax.psum_scatter(grad_parts[2], "dp", scatter_dimension=0, tiled=True),
            lax.psum_scatter(grad_parts[3], "dp", scatter_dimension=0, tiled=True),
            lax.psum_scatter(grad_parts[4], "dp", scatter_dimension=1, tiled=True),
            lax.psum_scatter(grad_parts[5], "dp", scatter_dimension=1, tiled=True),
            lax.psum_scatter(grad_parts[6], "dp", scatter_dimension=2, tiled=True),
            lax.psum_scatter(grad_parts[7], "dp", scatter_dimension=1, tiled=True),
        )
        mod_list[layer_num] = mod_grad
        bias_list[layer_num] = bias_grad
    mod_all = jnp.stack(mod_list).reshape(LAYERS, batch_size, 2, 6 * model_width)
    bias_all = jnp.stack(bias_list)
    mod_shard, bias_shard = (
        lax.psum_scatter(mod_all, "tensor", scatter_dimension=3, tiled=True),
        lax.psum_scatter(bias_all, "tensor", scatter_dimension=3, tiled=True),
    )
    mod_low = mod_shard.astype(jnp.bfloat16)
    every_mod, every_bias = (
        lax.all_gather(mod_low.astype(jnp.float32), "dp", axis=1, tiled=True),
        lax.all_gather(bias_shard[:, None], "dp", axis=1, tiled=True),
    )
    every_low = every_mod.astype(jnp.bfloat16)
    ada_w_grad = jnp.einsum(
        "sr,lskc->lkrc", own_cols, every_low, preferred_element_type=jnp.float32
    )
    piece_len = mod_shard.shape[3] // lax.axis_size("dp")
    ada_b_grad = lax.dynamic_slice_in_dim(
        jnp.sum(every_mod, axis=1), dp_rank * piece_len, piece_len, 2
    )
    bias_len = bias_shard.shape[3] // lax.axis_size("dp")
    bias_sum = lax.dynamic_slice_in_dim(
        jnp.sum(every_bias, axis=1), dp_rank * bias_len, bias_len, 3
    )
    cond_terms = jnp.einsum("lskc,lkrc->sr", every_low, ada_w, preferred_element_type=jnp.float32)
    cond_part = lax.all_to_all(cond_terms, "dp", split_axis=0, concat_axis=1, tiled=True)
    cond_sum = lax.psum(cond_part, "tensor")
    sigmoid = jax.nn.sigmoid(own_cond)
    cond_grad = cond_sum * sigmoid * (1.0 + own_cond * (1.0 - sigmoid))
    qkv_w_grad = jnp.stack([member[0] for member in layer_grads])
    out_w_grad = jnp.stack([member[1] for member in layer_grads])
    up_w_grad = jnp.stack([jnp.stack([member[2], member[3]]) for member in layer_grads])
    down_w_grad = jnp.stack([jnp.stack([member[4], member[5]]) for member in layer_grads])
    qv_b_grad = jnp.stack([member[6] for member in layer_grads])
    up_b_grad = jnp.stack([member[7] for member in layer_grads])
    return (
        streams[0].astype(jnp.bfloat16),
        streams[1].astype(jnp.bfloat16),
        gradients[0],
        gradients[1],
        cond_grad,
        ada_w_grad,
        ada_b_grad,
        qkv_w_grad,
        qv_b_grad,
        out_w_grad,
        bias_sum[:, 0],
        up_w_grad,
        up_b_grad,
        down_w_grad,
        bias_sum[:, 1],
    )


def solution(mesh):
    in_specs = (
        P("dp", "tensor", None),
        P("dp", "tensor", None),
        P(),
        P("dp", "tensor", None),
        P("dp", "tensor", None),
        P(None, None, "dp", "tensor"),
        P(None, None, "tensor"),
        P(None, None, "dp", None, "tensor"),
        P(None, None, None, "tensor"),
        P(None, None, "tensor", "dp"),
        P(),
        P(None, None, "dp", "tensor"),
        P(None, None, "tensor"),
        P(None, None, "tensor", "dp"),
        P(),
    )
    out_specs = (
        P("dp", "tensor", None),
        P("dp", "tensor", None),
        P("dp", "tensor", None),
        P("dp", "tensor", None),
        P("dp", None),
        P(None, None, "dp", "tensor"),
        P(None, None, ("tensor", "dp")),
        P(None, None, "dp", None, "tensor"),
        P(None, None, None, ("tensor", "dp")),
        P(None, None, "tensor", "dp"),
        P(None, None, ("tensor", "dp")),
        P(None, None, "dp", "tensor"),
        P(None, None, ("tensor", "dp")),
        P(None, None, "tensor", "dp"),
        P(None, None, ("tensor", "dp")),
    )
    return jax.shard_map(
        per_device, mesh=mesh, in_specs=in_specs, out_specs=out_specs, check_vma=False
    )
```

profile of v0, /device:TPU:0, one launch (start us, length us, event | category | flops | bytes accessed | tf_op | source)
XLA Modules:
  0.0 2285.3 jit_solution(2849697293516069158)
XLA Ops:
  12.9 71.6 %all-reduce.5.cloned.1.call-done = f32[8,2,2304]{2,1,0:T(2,128)} async-done(((f32[8,2,2304]{2,1,0:T(2,128)}), f32[8,2,2304]{2,1,0:T(2,128)}) %all-reduce.5.cloned.1.call-update) | async-done | bytes 147472
  95.2 6.7 all_gather.48
  101.9 93.4 %all-gather.22.cloned.1.call-done = bf16[1,2,1536,3,384]{4,1,3,0,2:T(2,128)(2,1)} async-done(((bf16[1,2,192,3,384]{4,1,3,0,2:T(2,128)(2,1)}), bf16[1,2,1536,3,384]{4,1,3,0,2:T(2,128)(2,1)}) %all-gather.22.cloned.1.call-update) | async-done | bytes 7077904 | tf_op jit(solution)/shard_map/all_gather | solution.py:393
  195.4 15.1 fusion.180
  214.6 17.0 copy.102
  231.5 6.9 add_convert_fusion
  248.1 27.5 %while.22 = (s32[]{:T(128)}, bf16[6,1,896,64]{2,3,1,0:T(8,128)(2,1)S(1)}, f32[6,1,896]{2,1,0:T(1,128)}, bf16[6,1,896,64]{3,2,1,0:T(8,128)(2,1)}, bf16[6,1,896,64...) while((s32[]{:T(128)}, bf16[6,1,896,64]{2,3,1,0:T(8,128)(2,1)S(1)}, ...), condition=%wide.region_8.9_spmd, body=%wide.region_5.8_spmd.sunk | while | flops 212802688 | bytes 10475609 | solution.py:84
  282.1 45.1 %reduce-scatter.26.cloned.1.call-done = f32[1,192,1536]{2,1,0:T(8,128)} async-done(((f32[1,768,1536]{2,1,0:T(8,128)}), f32[1,192,1536]{2,1,0:T(8,128)}) %reduce-scatter.26.cloned.1.call-update) | async-done | bytes 1179664 | tf_op jit(solution)/shard_map/reduce_scatter | solution.py:45
  337.6 129.6 %all-gather.26.cloned.1.call-done = bf16[1,2,1536,1536]{3,2,1,0:T(8,128)(2,1)} async-done(((bf16[1,2,192,1536]{3,2,1,0:T(8,128)(2,1)}), bf16[1,2,1536,1536]{3,2,1,0:T(8,128)(2,1)}) %all-gather.26.cloned.1.call-update) | async-done | bytes 9437200 | tf_op jit(solution)/shard_map/all_gather | solution.py:395
  467.3 24.4 %all-gather.16.cloned.1.call-done = bf16[1,768,1536]{2,1,0:T(8,128)(2,1)} async-done(((bf16[1,192,1536]{2,1,0:T(8,128)(2,1)}), bf16[1,768,1536]{2,1,0:T(8,128)(2,1)}) %all-gather.16.cloned.1.call-update) | async-done | bytes 2359312 | tf_op jit(solution)/shard_map/all_gather | solution.py:31
  491.7 9.0 fusion.59
  500.7 17.3 all-gather.18.cloned.1.call-done
  517.9 140.3 %all-gather.28.cloned.1.call-done = bf16[1,2,1536,1536]{2,3,1,0:T(8,128)(2,1)} async-done(((bf16[1,2,1536,192]{2,3,1,0:T(8,128)(2,1)}), bf16[1,2,1536,1536]{2,3,1,0:T(8,128)(2,1)}) %all-gather.28.cloned.1.call-update) | async-done | bytes 9437200 | tf_op jit(solution)/shard_map/all_gather | solution.py:396
  658.2 10.2 convert_reduce_fusion
  669.9 5.5 fusion.67
  675.4 10.3 fusion.66
  686.7 6.9 all_gather.56
  695.1 6.7 all_gather.53
  720.7 12.6 reduce-scatter.34.cloned.1.call-done
  735.7 47.8 %reduce-scatter.28.cloned.1.call-done = f32[1,192,1536]{2,1,0:T(8,128)} async-done(((f32[1,768,1536]{2,1,0:T(8,128)}), f32[1,192,1536]{2,1,0:T(8,128)}) %reduce-scatter.28.cloned.1.call-update) | async-done | bytes 1179664 | tf_op jit(solution)/shard_map/reduce_scatter | solution.py:45
  797.8 11.7 reduce-scatter.36.cloned.1.call-done
  811.2 24.0 %reduce-scatter.32.cloned.1.call-done = f32[1,32,1536]{2,1,0:T(8,128)} async-done(((f32[1,128,1536]{2,1,0:T(8,128)}), f32[1,32,1536]{2,1,0:T(8,128)}) %reduce-scatter.32.cloned.1.call-update) | async-done | bytes 196624 | tf_op jit(solution)/shard_map/reduce_scatter | solution.py:46
  838.3 6.1 all_gather.57
  844.9 16.4 all-gather.20.cloned.1.call-done
  864.5 55.2 %while.23 = (s32[]{:T(128)}, bf16[6,3,1,896,64]{3,4,0,1,2:T(8,128)(2,1)}, bf16[6,1,896,64]{3,2,1,0:T(8,128)(2,1)}, bf16[6,1,896,64]{3,2,1,0:T(8,128)(2,1)}, f32[...) while((s32[]{:T(128)}, ...), condition=%wide.region_25.26_spmd, body=%wide.region_23.25_spmd.sunk | while | flops 524754048 | bytes 26521200 | solution.py:136
  919.7 5.3 convolution_bitcast_fusion.7
  925.3 7.9 convolution_bitcast_fusion.4
  957.7 8.4 copy.83
  967.2 5.3 fusion.139
  972.6 9.8 fusion.80
  989.4 10.7 fusion.77
  1015.2 8.9 copy.90
  1024.0 18.9 bitcast_reduce_fusion
  1043.0 11.0 pad_maximum_fusion
  1054.8 10.0 reduce-scatter.58.cloned.1.call-done
  1066.3 23.9 %reduce-scatter.56.cloned.1.call-done = f32[384,4]{1,0:T(8,128)} async-done(((f32[1536,4]{1,0:T(8,128)}), f32[384,4]{1,0:T(8,128)}) %reduce-scatter.56.cloned.1.call-update) | async-done | bytes 6160
  1091.5 30.7 %all-gather.4 = f32[8,2,2,384]{3,2,1,0:T(2,128)S(1)} all-gather(f32[1,2,2,384]{3,2,1,0:T(2,128)S(1)} %copy.95), channel_id=6, replica_groups=mesh['dp'=8,'tensor'=4] {'dp'}, dimensions={0}, use_global_device_ids=true | all-gather | bytes 55296 | tf_op jit(solution)/shard_map/all_gather | solution.py:436
  1122.9 32.4 %reduce-scatter.54.cloned.1.call-done = f32[48,4]{1,0:T(8,128)} async-done(((f32[384,4]{1,0:T(8,128)}), f32[48,4]{1,0:T(8,128)}) %reduce-scatter.54.cloned.1.call-update) | async-done | bytes 784
  1157.6 170.5 %all-reduce.7.cloned.1.call-done = f32[2,384,1536]{1,0,2:T(2,128)} async-done(((f32[2,384,1536]{1,0,2:T(2,128)}), f32[2,384,1536]{1,0,2:T(2,128)}) %all-reduce.7.cloned.1.call-update) | async-done | bytes 4718608
  1330.2 164.4 %reduce-scatter.46.cloned.1.call-done = f32[192,1536]{1,0:T(8,128)} async-done(((f32[1536,1536]{1,0:T(8,128)}), f32[192,1536]{1,0:T(8,128)}) %reduce-scatter.46.cloned.1.call-update) | async-done | bytes 1179664 | tf_op jit(solution)/shard_map/reduce_scatter | solution.py:419
  1494.6 166.6 %reduce-scatter.44.cloned.1.call-done = f32[192,1536]{1,0:T(8,128)} async-done(((f32[1536,1536]{1,0:T(8,128)}), f32[192,1536]{1,0:T(8,128)}) %reduce-scatter.44.cloned.1.call-update) | async-done | bytes 1179664 | tf_op jit(solution)/shard_map/reduce_scatter | solution.py:418
  1664.3 163.3 %reduce-scatter.50.cloned.1.call-done = f32[1536,192]{0,1:T(8,128)} async-done(((f32[1536,1536]{0,1:T(8,128)}), f32[1536,192]{0,1:T(8,128)}) %reduce-scatter.50.cloned.1.call-update) | async-done | bytes 1179664 | tf_op jit(solution)/shard_map/reduce_scatter | solution.py:421
  1827.6 166.4 %reduce-scatter.48.cloned.1.call-done = f32[1536,192]{0,1:T(8,128)} async-done(((f32[1536,1536]{0,1:T(8,128)}), f32[1536,192]{0,1:T(8,128)}) %reduce-scatter.48.cloned.1.call-update) | async-done | bytes 1179664 | tf_op jit(solution)/shard_map/reduce_scatter | solution.py:420
  1998.9 44.7 %reduce-scatter.52.cloned.1.call-done = f32[2304,2]{1,0:T(8,128)} async-done(((f32[9216,2]{1,0:T(8,128)}), f32[2304,2]{1,0:T(8,128)}) %reduce-scatter.52.cloned.1.call-update) | async-done | bytes 18448
  2049.8 31.8 %all_gather.58 = f32[1,8,2,2304]{3,2,0,1:T(2,128)S(1)} all-gather(f32[1,1,2,2304]{3,2,0,1:T(2,128)S(1)} %copy.78), channel_id=1, replica_groups=mesh['dp'=8,'tensor'=4] {'dp'}, dimensions={1}, use_global_device_ids=true | all-gather | bytes 165888 | tf_op jit(solution)/shard_map/all_gather | solution.py:435
  2082.8 5.6 all-to-all-start
  2095.7 6.1 psum.7
  2103.3 175.0 %reduce-scatter.42.cloned.1.call-done = f32[2,192,3,384]{3,1,2,0:T(8,128)} async-done(((f32[2,1536,3,384]{3,1,2,0:T(8,128)}), f32[2,192,3,384]{3,1,2,0:T(8,128)}) %reduce-scatter.42.cloned.1.call-update) | async-done | bytes 1769488 | tf_op jit(solution)/shard_map/reduce_scatter | solution.py:416
  (453 shorter events, 256.5 us)
Async XLA Ops:
  7.2 77.3 %all-reduce.5.cloned.1.call-start = ((), (), s32[]{:S(2)}) async-start(), calls=%async_computation.43 | async-start | bytes 294912
  9.1 75.4 %copy-start.60 = (bf16[1,2,2304]{2,1,0:T(2,128)(2,1)S(1)}, bf16[1,2,2304]{2,1,0:T(2,128)(2,1)}, u32[]{:S(2)}) copy-start(bf16[1,2,2304]{2,1,0:T(2,128)(2,1)} %param.25) | copy-start | bytes 27652
  9.9 185.5 %all-gather.22.cloned.1.call-start = ((), (), s32[]{:S(2)}) async-start(), calls=%async_computation.35 | async-start | bytes 7962624 | tf_op jit(solution)/shard_map/all_gather | solution.py:393
  11.7 82.2 %copy-start.8 = (bf16[1,32,1536]{2,1,0:T(8,128)(2,1)S(1)}, bf16[1,32,1536]{2,1,0:T(8,128)(2,1)}, u32[]{:S(2)}) copy-start(bf16[1,32,1536]{2,1,0:T(8,128)(2,1)} %param.20) | copy-start | bytes 294916
  11.7 82.5 %copy-start.74 = (bf16[1,2,2,384]{3,2,1,0:T(2,128)(2,1)S(1)}, bf16[1,2,2,384]{3,2,1,0:T(2,128)(2,1)}, u32[]{:S(2)}) copy-start(bf16[1,2,2,384]{3,2,1,0:T(2,128)(2,1)} %param.27) | copy-start | bytes 9220
  11.8 219.8 %all-gather.14.cloned.1.call-start = ((), (), s32[]{:S(2)}) async-start(), calls=%async_computation.18 | async-start | bytes 2949120 | tf_op jit(solution)/shard_map/all_gather | solution.py:31
  12.6 82.5 %copy-start.52 = (f32[192]{0:T(256)}, f32[192]{0:T(256)S(1)}, u32[]{:S(2)}) copy-start(f32[192]{0:T(256)S(1)} %broadcast_multiply_fusion.5) | copy-start | bytes 2308
  12.9 82.1 %copy-start.56 = (f32[192]{0:T(256)}, f32[192]{0:T(256)S(1)}, u32[]{:S(2)}) copy-start(f32[192]{0:T(256)S(1)} %add_rsqrt_fusion.1) | copy-start | bytes 2308
  93.3 182.3 %all-gather.24.cloned.1.call-start = ((), (), s32[]{:S(2)}) async-start(), calls=%async_computation.36 | async-start | bytes 2654208 | tf_op jit(solution)/shard_map/all_gather | solution.py:394
  93.8 233.3 %reduce-scatter.26.cloned.1.call-start = ((), (), s32[]{:S(2)}) async-start(), calls=%async_computation.19 | async-start | bytes 5898240 | tf_op jit(solution)/shard_map/reduce_scatter | solution.py:45
  101.9 108.5 %copy-start.19 = (bf16[1,128,1536]{2,1,0:T(8,128)(2,1)}, bf16[1,128,1536]{2,1,0:T(8,128)(2,1)S(1)}, u32[]{:S(2)}) copy-start(bf16[1,128,1536]{2,1,0:T(8,128)(2,1)S(1)} %all_gather.48) | copy-start | bytes 1179652
  214.6 17.0 copy-start.69
  280.8 186.5 %all-gather.26.cloned.1.call-start = ((), (), s32[]{:S(2)}) async-start(), calls=%async_computation.37 | async-start | bytes 10616832 | tf_op jit(solution)/shard_map/all_gather | solution.py:395
  281.4 210.3 %all-gather.16.cloned.1.call-start = ((), (), s32[]{:S(2)}) async-start(), calls=%async_computation.20 | async-start | bytes 2949120 | tf_op jit(solution)/shard_map/all_gather | solution.py:31
  331.4 186.5 %all-gather.18.cloned.1.call-start = ((), (), s32[]{:S(2)}) async-start(), calls=%async_computation.24 | async-start | bytes 2949120 | tf_op jit(solution)/shard_map/all_gather | solution.py:38
  333.1 325.1 %all-gather.28.cloned.1.call-start = ((), (), s32[]{:S(2)}) async-start(), calls=%async_computation.38 | async-start | bytes 10616832 | tf_op jit(solution)/shard_map/all_gather | solution.py:396
  333.8 359.8 %reduce-scatter.30.cloned.1.call-start = ((), (), s32[]{:S(2)}) async-start(), calls=%async_computation.22 | async-start | bytes 983040 | tf_op jit(solution)/shard_map/reduce_scatter | solution.py:46
  334.6 340.8 %copy-start.61 = (f32[1536]{0:T(1024)}, f32[1536]{0:T(1024)S(1)}, u32[]{:S(2)}) copy-start(f32[1536]{0:T(1024)S(1)} %get-tuple-element.193) | copy-start | bytes 18436
  337.4 395.9 %reduce-scatter.34.cloned.1.call-start = ((), (), s32[]{:S(2)}) async-start(), calls=%async_computation.25 | async-start | bytes 5898240 | tf_op jit(solution)/shard_map/reduce_scatter | solution.py:52
  658.2 11.6 copy-start.75
  675.4 108.1 %reduce-scatter.28.cloned.1.call-start = ((), (), s32[]{:S(2)}) async-start(), calls=%async_computation.21 | async-start | bytes 5898240 | tf_op jit(solution)/shard_map/reduce_scatter | solution.py:45
  685.8 123.7 %reduce-scatter.36.cloned.1.call-start = ((), (), s32[]{:S(2)}) async-start(), calls=%async_computation.27 | async-start | bytes 983040 | tf_op jit(solution)/shard_map/reduce_scatter | solution.py:53
  694.9 11.4 copy-start.70
  714.9 18.4 copy-start.37
  714.9 18.4 copy-start.55
  714.9 18.3 copy-start.59
  714.9 120.2 %reduce-scatter.32.cloned.1.call-start = ((), (), s32[]{:S(2)}) async-start(), calls=%async_computation.23 | async-start | bytes 983040 | tf_op jit(solution)/shard_map/reduce_scatter | solution.py:46
  720.5 63.0 %copy-start.36 = (f32[1536]{0:T(1024)S(1)}, f32[1536]{0:T(1024)}, u32[]{:S(2)}) copy-start(f32[1536]{0:T(1024)} %get-tuple-element.189) | copy-start | bytes 18436
  720.5 63.0 %copy-start.41 = (f32[1536]{0:T(1024)S(1)}, f32[1536]{0:T(1024)}, u32[]{:S(2)}) copy-start(f32[1536]{0:T(1024)} %get-tuple-element.195) | copy-start | bytes 18436
  720.5 63.0 %copy-start.42 = (f32[1536]{0:T(1024)S(1)}, f32[1536]{0:T(1024)}, u32[]{:S(2)}) copy-start(f32[1536]{0:T(1024)} %get-tuple-element.184) | copy-start | bytes 18436
  720.6 140.8 %all-gather.20.cloned.1.call-start = ((), (), s32[]{:S(2)}) async-start(), calls=%async_computation.26 | async-start | bytes 2949120 | tf_op jit(solution)/shard_map/all_gather | solution.py:38
  790.3 221.4 %reduce-scatter.40.cloned.1.call-start = ((), (), s32[]{:S(2)}) async-start(), calls=%async_computation.29 | async-start | bytes 983040 | tf_op jit(solution)/shard_map/reduce_scatter | solution.py:53
  793.8 15.7 copy-start.71
  793.8 41.4 %copy-start.27 = (f32[1,32,1536]{2,1,0:T(8,128)S(1)}, f32[1,32,1536]{2,1,0:T(8,128)}, u32[]{:S(2)}) copy-start(f32[1,32,1536]{2,1,0:T(8,128)} %reduce-scatter.30.cloned.1.call-done) | copy-start | bytes 589828
  925.0 88.0 %reduce-scatter.38.cloned.1.call-start = ((), (), s32[]{:S(2)}) async-start(), calls=%async_computation.28 | async-start | bytes 5898240 | tf_op jit(solution)/shard_map/reduce_scatter | solution.py:52
  933.2 131.5 %reduce-scatter.58.cloned.1.call-start = ((), (), s32[]{:S(2)}) async-start(), calls=%async_computation.42 | async-start | bytes 884736
  937.9 152.3 %reduce-scatter.56.cloned.1.call-start = ((), (), s32[]{:S(2)}) async-start(), calls=%async_computation.41 | async-start | bytes 983040
  940.7 214.6 %reduce-scatter.54.cloned.1.call-start = ((), (), s32[]{:S(2)}) async-start(), calls=%async_computation.40 | async-start | bytes 221184
  952.2 375.9 %all-reduce.7.cloned.1.call-start = ((), (), s32[]{:S(2)}) async-start(), calls=%async_computation.44 | async-start | bytes 9437184
  966.1 528.5 %reduce-scatter.46.cloned.1.call-start = ((), (), s32[]{:S(2)}) async-start(), calls=%async_computation.32 | async-start | bytes 10616832 | tf_op jit(solution)/shard_map/reduce_scatter | solution.py:419
  972.5 688.6 %reduce-scatter.44.cloned.1.call-start = ((), (), s32[]{:S(2)}) async-start(), calls=%async_computation.31 | async-start | bytes 10616832 | tf_op jit(solution)/shard_map/reduce_scatter | solution.py:418
  982.4 845.2 %reduce-scatter.50.cloned.1.call-start = ((), (), s32[]{:S(2)}) async-start(), calls=%async_computation.34 | async-start | bytes 10616832 | tf_op jit(solution)/shard_map/reduce_scatter | solution.py:421
  988.7 1005.3 %reduce-scatter.48.cloned.1.call-start = ((), (), s32[]{:S(2)}) async-start(), calls=%async_computation.33 | async-start | bytes 10616832 | tf_op jit(solution)/shard_map/reduce_scatter | solution.py:420
  1000.2 1043.4 %reduce-scatter.52.cloned.1.call-start = ((), (), s32[]{:S(2)}) async-start(), calls=%async_computation.39 | async-start | bytes 5898240
  1043.0 1235.3 %reduce-scatter.42.cloned.1.call-start = ((), (), s32[]{:S(2)}) async-start(), calls=%async_computation.30 | async-start | bytes 15925248 | tf_op jit(solution)/shard_map/reduce_scatter | solution.py:416
  1054.0 102.8 %copy-start.16 = (f32[1,32,1536]{2,1,0:T(8,128)S(1)}, f32[1,32,1536]{2,1,0:T(8,128)}, u32[]{:S(2)}) copy-start(f32[1,32,1536]{2,1,0:T(8,128)} %copy-done.15) | copy-start | bytes 589828
  1054.0 102.8 %copy-start.28 = (f32[1,32,1536]{2,1,0:T(8,128)S(1)}, f32[1,32,1536]{2,1,0:T(8,128)}, u32[]{:S(2)}) copy-start(f32[1,32,1536]{2,1,0:T(8,128)} %reduce-scatter.40.cloned.1.call-done) | copy-start | bytes 589828
  2082.8 12.7 all-to-all-start
  (62 other events, 196.8 us)
Sparse Core Ops, SparseCore 0:
  11.9 72.5 all-reduce.4
  87.5 107.8 all-gather.21
  197.6 22.2 all-gather.13
  222.2 52.0 all-gather.23
  280.9 46.1 reduce-scatter.25
  329.2 138.0 all-gather.25
  469.4 22.2 all-gather.15
  493.8 24.0 all-gather.17
  520.1 138.0 all-gather.27
  661.2 21.4 reduce-scatter.29
  685.4 47.8 reduce-scatter.33
  735.6 47.8 reduce-scatter.27
  786.2 23.2 reduce-scatter.35
  811.9 23.2 reduce-scatter.31
  837.2 24.0 all-gather.19
  925.2 23.2 reduce-scatter.39
  950.9 47.8 reduce-scatter.37
  1002.2 62.4 reduce-scatter.57
  1067.9 22.2 reduce-scatter.55
  1094.2 61.0 reduce-scatter.53
  1159.3 168.6 all-reduce.6
  1332.1 162.4 reduce-scatter.45
  1498.6 162.5 reduce-scatter.43
  1665.0 162.5 reduce-scatter.49
  1831.6 162.3 reduce-scatter.47
  1996.6 46.9 reduce-scatter.51
  2047.6 230.5 reduce-scatter.41
where the time goes:
time: 2290 us
  waiting for transfers between devices  1760 us (77%)
  matrix products  197 us (9%)
  local copies, waits for them, and re-layouts  136 us (6%)
  blocking collectives  100 us (4%)
  other arithmetic  71.1 us (3%)
    unnamed x33, waiting for transfers between devices  355 us
    reduce_scatter x1, waiting for transfers between devices, per_device(): lax.psum_scatter(grad_parts[0], 'dp', scatter_dimension=1, tiled=True)  175 us
    reduce_scatter x1, waiting for transfers between devices, per_device(): lax.psum_scatter(grad_parts[2], 'dp', scatter_dimension=0, tiled=True)  167 us
    reduce_scatter x1, waiting for transfers between devices, per_device(): lax.psum_scatter(grad_parts[4], 'dp', scatter_dimension=1, tiled=True)  166 us
    reduce_scatter x1, waiting for transfers between devices, per_device(): lax.psum_scatter(grad_parts[3], 'dp', scatter_dimension=0, tiled=True)  164 us
    reduce_scatter x1, waiting for transfers between devices, per_device(): lax.psum_scatter(grad_parts[5], 'dp', scatter_dimension=1, tiled=True)  163 us
    all_gather x1, waiting for transfers between devices, per_device(): lax.all_gather(down_w[layer_num], 'dp', axis=2, tiled=True)  140 us
    all_gather x1, waiting for transfers between devices, per_device(): lax.all_gather(up_w[layer_num], 'dp', axis=1, tiled=True)  130 us
  transfers between devices with their start and end apart: 28, of which 23 were waited for; matrix products, arithmetic and copies ran while one was open for 14% of the time, Pallas kernels for 0%

commit v1 on v0

v1 whole, which is shorter than its diff:
```python
import jax
import jax.numpy as jnp
from jax import lax
from jax.experimental import pallas as pl
from jax.experimental.pallas import tpu as pltpu
from jax.sharding import PartitionSpec as P

HEAD = 64
NORM_EPS = 1e-06
F32 = jnp.float32
BF16 = jnp.bfloat16


def layer_norm(value):
    centered = value - jnp.mean(value, axis=-1, keepdims=True)
    inv_std = lax.rsqrt(jnp.mean(centered * centered, axis=-1, keepdims=True) + NORM_EPS)
    return (centered * inv_std, inv_std)


def norm_back(upstream, normed, inv_std):
    mean_grad = jnp.mean(upstream, axis=-1, keepdims=True)
    mean_proj = jnp.mean(upstream * normed, axis=-1, keepdims=True)
    return inv_std * (upstream - mean_grad - normed * mean_proj)


def gelu_tanh(value):
    return jax.nn.gelu(value, approximate=True)


def dot(left, right, dims):
    return lax.dot_general(left, right, (dims, ((), ())), preferred_element_type=F32)


def mm(left, right):
    return dot(left, right, ((1,), (0,)))


def mm_nt(left, right):
    return dot(left, right, ((1,), (1,)))


def mm_tn(left, right):
    return dot(left, right, ((0,), (0,)))


def ring_place(count, position):
    position = position % count
    if isinstance(position, int):
        return 2 * position if position < count // 2 else 2 * (count - 1 - position) + 1
    return jnp.where(position < count // 2, 2 * position, 2 * (count - 1 - position) + 1)


class Ring:
    def __init__(self, count):
        self.count = count
        self.half = count // 2
        index = lax.axis_index("dp")
        self.position = jnp.where(index % 2 == 0, index // 2, count - 1 - index // 2)
        places = [ring_place(count, p) for p in range(count)]
        self.right_pairs = [(places[p], places[(p + 1) % count]) for p in range(count)]
        self.left_pairs = [(places[p], places[(p - 1) % count]) for p in range(count)]

    def right(self, value):
        return lax.ppermute(value, "dp", self.right_pairs)

    def left(self, value):
        return lax.ppermute(value, "dp", self.left_pairs)

    def owner(self, offset):
        return ring_place(self.count, self.position + offset)

    def gather(self, shard):
        streams, rows, width = shard.shape
        cut = rows // 2
        whole = jnp.zeros((streams, self.count * rows, width), shard.dtype)

        def put(whole, piece, offset, start=0):
            return lax.dynamic_update_slice(whole, piece, (0, self.owner(offset) * rows + start, 0))

        whole = put(whole, shard, 0)
        forward, backward = (shard, shard)
        marks = []
        for step in range(1, self.half):
            forward = self.right(forward)
            backward = self.left(backward)
            marks.append((forward, backward))
            whole = put(whole, forward, -step)
            whole = put(whole, backward, step)
        forward = self.right(forward[:, :cut])
        backward = self.left(backward[:, cut:])
        whole = put(whole, forward, -self.half)
        whole = put(whole, backward, self.half, cut)
        return (whole, marks)

    def scatter(self, whole):
        streams, all_rows, width = whole.shape
        rows = all_rows // self.count
        cut = rows // 2

        def block(offset, start=0, size=rows):
            return lax.dynamic_slice(
                whole, (0, self.owner(offset) * rows + start, 0), (streams, size, width)
            )

        forward = self.right(block(self.half, 0, cut))
        backward = self.left(block(-self.half, cut, rows - cut))
        forward = jnp.pad(forward.astype(F32), ((0, 0), (0, rows - cut), (0, 0)))
        backward = jnp.pad(backward.astype(F32), ((0, 0), (cut, 0), (0, 0)))
        for step in range(self.half - 1, 0, -1):
            forward = self.right((block(step).astype(F32) + forward).astype(BF16)).astype(F32)
            backward = self.left((block(-step).astype(F32) + backward).astype(BF16)).astype(F32)
        return block(0).astype(F32) + forward + backward


def flip_pairs(count, bit):
    return [(i, i ^ bit) for i in range(count)]


def pick(pair, flag):
    return jnp.where(flag == 0, pair[0], pair[1])


def small_scatter(value, axis, count):
    index = lax.axis_index(axis)
    bit = count // 2
    bits = []
    width = 1
    while width < count:
        bits.append(width)
        width *= 2
    rest = value
    for bit in bits:
        pairs = rest.reshape((rest.shape[0] // 2, 2) + rest.shape[1:])
        flag = (index // bit) % 2
        mine = jnp.where(flag == 0, pairs[:, 0], pairs[:, 1])
        other = jnp.where(flag == 0, pairs[:, 1], pairs[:, 0])
        rest = mine + lax.ppermute(other, axis, flip_pairs(count, bit))
    return rest[0]


def small_gather(value, axis, count):
    index = lax.axis_index(axis)
    rest = value[None]
    bit = 1
    while bit < count:
        got = lax.ppermute(rest, axis, flip_pairs(count, bit))
        flag = (index // bit) % 2
        rest = jnp.where(
            flag == 0, jnp.concatenate([rest, got]), jnp.concatenate([got, rest])
        )
        bit *= 2
    return rest


def small_sum(value, axis, count):
    bit = 1
    while bit < count:
        value = value + lax.ppermute(value, axis, flip_pairs(count, bit))
        bit *= 2
    return value


def small_exchange(value, axis, count):
    index = lax.axis_index(axis)
    tail = value.shape[1:]
    bit = 1
    rest = value
    while bit < count:
        pairs = rest.reshape((count // (2 * bit), 2, bit) + tail)
        flag = (index // bit) % 2
        mine = jnp.where(flag == 0, pairs[:, 0], pairs[:, 1])
        other = jnp.where(flag == 0, pairs[:, 1], pairs[:, 0])
        got = lax.ppermute(other, axis, flip_pairs(count, bit))
        rest = jnp.where(
            flag == 0, jnp.stack([mine, got], axis=1), jnp.stack([got, mine], axis=1)
        ).reshape((count,) + tail)
        bit *= 2
    return rest


def swap_core(value):
    return lax.ppermute(value, "tensor", flip_pairs(4, 1))


def swap_y(value):
    return lax.ppermute(value, "tensor", flip_pairs(4, 2))


def gather_rows(first, second):
    split = first.shape[0]
    own = jnp.concatenate([first, second])
    over_y = swap_y(own)
    core = swap_core(own)
    both = swap_core(over_y)
    pieces = (own, over_y, core, both)
    return (
        jnp.concatenate([piece[:split] for piece in pieces]),
        jnp.concatenate([piece[split:] for piece in pieces]),
    )


def reduce_rows(factors, products):
    away, kept = ([], [])
    for factor, product in zip(factors, products):
        rows = factor.shape[0] // 2
        away.append(product(factor[rows:]))
    for factor, product in zip(factors, products):
        rows = factor.shape[0] // 2
        kept.append(product(factor[:rows]))
    sums = [keep + swap_core(send) for keep, send in zip(kept, away)]
    quarter = [total.shape[0] // 2 for total in sums]
    crossing = jnp.concatenate(
        [total[size:].astype(BF16) for total, size in zip(sums, quarter)]
    )
    got = swap_y(crossing).astype(F32)
    return [
        sums[0][: quarter[0]] + got[: quarter[0]],
        sums[1][: quarter[1]] + got[quarter[0] :],
    ]


CHUNK = 128


def attend_kernel(qi, qt, ki, kt, vi, vt, oi, ot, lse, weights):
    rows_i = qi.shape[0]
    rows = rows_i + qt.shape[0]
    keys = jnp.concatenate([ki[...], kt[...]])
    queries = jnp.concatenate([qi[...], qt[...]])
    queries = (queries.astype(F32) * (HEAD**-0.5)).astype(BF16)
    values_t = jnp.concatenate([vi[...], vt[...]]).T
    outs = []
    for head in range(2):
        lanes = slice(head * HEAD, (head + 1) * HEAD)
        key = keys[:, lanes]
        query = queries[:, lanes]
        totals = []
        for start in range(0, rows, CHUNK):
            scores = mm_nt(key, query[start : start + CHUNK])
            maximum = jnp.max(scores, axis=0, keepdims=True)
            weight = jnp.exp(scores - maximum)
            total = jnp.sum(weight, axis=0, keepdims=True)
            weights[:, start : start + CHUNK] = weight.astype(BF16)
            lse[0, head : head + 1, start : start + CHUNK] = maximum + jnp.log(total)
            totals.append(total)
        out_t = mm(values_t[lanes], weights[...])
        outs.append(out_t / jnp.concatenate(totals, axis=1))
    result = jnp.concatenate(outs).T.astype(BF16)
    oi[...] = result[:rows_i]
    ot[...] = result[rows_i:]


def attend(packed_image, packed_text):
    rows_i, width = packed_image.shape
    rows_t = packed_text.shape[0]
    rows = rows_i + rows_t
    pairs = width // 3 // 128

    def spec(count, part):
        return pl.BlockSpec((count, 128), lambda i, part=part: (0, part * pairs + i))

    return pl.pallas_call(
        attend_kernel,
        grid=(pairs,),
        in_specs=[spec(count, part) for part in range(3) for count in (rows_i, rows_t)],
        out_specs=[
            pl.BlockSpec((rows_i, 128), lambda i: (0, i)),
            pl.BlockSpec((rows_t, 128), lambda i: (0, i)),
            pl.BlockSpec((1, 2, rows), lambda i: (i, 0, 0)),
        ],
        out_shape=[
            jax.ShapeDtypeStruct((rows_i, pairs * 128), BF16),
            jax.ShapeDtypeStruct((rows_t, pairs * 128), BF16),
            jax.ShapeDtypeStruct((pairs, 2, rows), F32),
        ],
        scratch_shapes=[pltpu.VMEM((rows, rows), BF16)],
        compiler_params=pltpu.CompilerParams(vmem_limit_bytes=40 * 2**20),
        cost_estimate=pl.CostEstimate(
            flops=pairs * 2 * 4 * rows * rows * 256,
            bytes_accessed=rows * width * 3,
            transcendentals=pairs * 2 * rows * rows,
        ),
    )(*([packed_image, packed_text] * 3))


def attend_back_kernel(qi, qt, ki, kt, vi, vt, gi, gt, lse, di, dt, probs, grads):
    rows_i = qi.shape[0]
    rows = rows_i + qt.shape[0]
    pair = pl.program_id(0)
    pairs = pl.num_programs(0)
    scale = HEAD**-0.5
    keys = jnp.concatenate([ki[...], kt[...]])
    queries = jnp.concatenate([qi[...], qt[...]])
    queries = (queries.astype(F32) * scale).astype(BF16)
    values = jnp.concatenate([vi[...], vt[...]])
    outer = jnp.concatenate([gi[...], gt[...]])
    keys_t = keys.T
    dq, dk, dv = ([], [], [])
    for head in range(2):
        lanes = slice(head * HEAD, (head + 1) * HEAD)
        key, query, value, grad = (keys[:, lanes], queries[:, lanes], values[:, lanes], outer[:, lanes])
        for start in range(0, rows, CHUNK):
            piece = slice(start, start + CHUNK)
            scores = mm_nt(key, query[piece])
            prob = jnp.exp(scores - lse[0, head : head + 1, piece])
            prob_grad = mm_nt(value, grad[piece])
            row_dot = jnp.sum(prob_grad * prob, axis=0, keepdims=True)
            probs[:, piece] = prob.astype(BF16)
            grads[:, piece] = (prob * (prob_grad - row_dot)).astype(BF16)
        dv.append(mm(probs[...], grad))
        dk.append(mm(grads[...], query))
        dq.append(mm(keys_t[lanes], grads[...]) * scale)
    results = (
        jnp.concatenate(dq).T.astype(BF16),
        jnp.concatenate(dk, axis=1).astype(BF16),
        jnp.concatenate(dv, axis=1).astype(BF16),
    )
    for part, result in enumerate(results):
        lanes = pl.ds(pl.multiple_of((part * pairs + pair) * 128, 128), 128)
        di[:, lanes] = result[:rows_i]
        dt[:, lanes] = result[rows_i:]


def attend_back(packed_image, packed_text, grad_image, grad_text, lse):
    rows_i, width = packed_image.shape
    rows_t = packed_text.shape[0]
    rows = rows_i + rows_t
    pairs = width // 3 // 128

    def spec(count, part):
        return pl.BlockSpec((count, 128), lambda i, part=part: (0, part * pairs + i))

    return pl.pallas_call(
        attend_back_kernel,
        grid=(pairs,),
        in_specs=[spec(count, part) for part in range(3) for count in (rows_i, rows_t)]
        + [
            pl.BlockSpec((rows_i, 128), lambda i: (0, i)),
            pl.BlockSpec((rows_t, 128), lambda i: (0, i)),
            pl.BlockSpec((1, 2, rows), lambda i: (i, 0, 0)),
        ],
        out_specs=[
            pl.BlockSpec((rows_i, width), lambda i: (0, 0)),
            pl.BlockSpec((rows_t, width), lambda i: (0, 0)),
        ],
        out_shape=[
            jax.ShapeDtypeStruct((rows_i, width), BF16),
            jax.ShapeDtypeStruct((rows_t, width), BF16),
        ],
        scratch_shapes=[pltpu.VMEM((rows, rows), BF16), pltpu.VMEM((rows, rows), BF16)],
        compiler_params=pltpu.CompilerParams(vmem_limit_bytes=48 * 2**20),
        cost_estimate=pl.CostEstimate(
            flops=pairs * 2 * 10 * rows * rows * 256,
            bytes_accessed=rows * width * 5,
            transcendentals=pairs * 2 * rows * rows,
        ),
    )(*([packed_image, packed_text] * 3), grad_image, grad_text, lse)


def after(value, *marks):
    return lax.optimization_barrier((value,) + marks)[0]


def per_device(
    image_tokens,
    text_tokens,
    condition,
    image_cot,
    text_cot,
    ada_w,
    ada_b,
    qkv_w,
    qv_b,
    out_w,
    out_b,
    up_w,
    up_b,
    down_w,
    down_b,
):
    both = range(2)
    count = lax.axis_size("dp")
    members = lax.axis_size("tensor")
    ring = Ring(count)
    dp_rank = lax.axis_index("dp")
    width = image_tokens.shape[2]
    row_block = ada_w.shape[2]
    heads_width = qkv_w.shape[4]

    qkv_shard = qkv_w[0].reshape(2, row_block, 3 * heads_width)
    out_shard = out_w[0].transpose(0, 2, 1)
    up_shard = up_w[0]
    down_shard = down_w[0].transpose(0, 2, 1)
    w_qkv, marks = ring.gather(qkv_shard)
    w_out, marks = ring.gather(after(out_shard, *marks[-1]))
    w_up, marks = ring.gather(after(up_shard, *marks[0]))
    w_down, marks = ring.gather(after(down_shard, *marks[-1]))

    cond_full = condition.astype(F32)
    silu_low = jax.nn.silu(cond_full).astype(BF16)
    own_cond = lax.dynamic_slice_in_dim(cond_full, dp_rank, 1, 0)
    own_cols = lax.dynamic_slice_in_dim(silu_low, dp_rank * row_block, row_block, 1)
    mod_terms = jnp.einsum("sr,krc->skc", own_cols, ada_w[0], preferred_element_type=F32)
    mod_local = small_scatter(mod_terms, "dp", count) + ada_b[0].astype(F32)
    mod_full = small_gather(mod_local, "tensor", members)
    mods = mod_full.transpose(1, 0, 2).reshape(2, 6, 1, width)

    biases_out = out_b[0].astype(F32)
    biases_down = down_b[0].astype(F32)
    biases_up = up_b[0].astype(F32)
    biases_qv = qv_b[0].astype(F32)

    streams = [image_tokens[0].astype(F32), text_tokens[0].astype(F32)]
    normed_one, inv_one, lowered = ([], [], [])
    for s in both:
        normed, inv_std = layer_norm(streams[s])
        normed_one.append(normed)
        inv_one.append(inv_std)
        lowered.append((normed * (1.0 + mods[s, 1]) + mods[s, 0]).astype(BF16))
    full_one = gather_rows(*lowered)
    packed = []
    for s in both:
        bias = jnp.concatenate(
            [biases_qv[s, 0], jnp.zeros_like(biases_qv[s, 0]), biases_qv[s, 1]]
        )
        packed.append((mm(full_one[s], w_qkv[s]) + bias).astype(BF16))
    attn_image, attn_text, lse = attend(*packed)
    attn = (attn_image, attn_text)
    attn_sums = reduce_rows(attn, [lambda rows, s=s: mm_nt(rows, w_out[s]) for s in both])
    attn_bias, residuals, normed_two, inv_two, lowered = ([], [], [], [], [])
    for s in both:
        attn_bias.append(attn_sums[s] + biases_out[s])
        residuals.append(streams[s] + mods[s, 2] * attn_bias[s])
        normed, inv_std = layer_norm(residuals[s])
        normed_two.append(normed)
        inv_two.append(inv_std)
        lowered.append((normed * (1.0 + mods[s, 4]) + mods[s, 3]).astype(BF16))
    full_two = gather_rows(*lowered)

    gradients = [image_cot[0].astype(F32), text_cot[0].astype(F32)]
    scaled = [mods[s, 5] * gradients[s] for s in both]
    down_bias_grad = [jnp.sum(scaled[s], axis=0) for s in both]
    dy_full = gather_rows(*[value.astype(BF16) for value in scaled])
    pre_acts, acts, down_w_grad = ([], [], [])
    for s in both:
        pre_acts.append(mm(full_two[s], w_up[s]) + biases_up[s])
        acts.append(gelu_tanh(pre_acts[s]).astype(BF16))
    for s in both:
        down_w_grad.append(mm_tn(dy_full[s], acts[s]).astype(BF16))
    down_grad = ring.scatter(jnp.stack(down_w_grad))

    up_w_grad, up_b_grad, pre_grads = ([], [], [])
    for s in both:
        act_grad = mm(dy_full[s], w_down[s])
        gelu_back = jax.vjp(gelu_tanh, pre_acts[s])[1]
        pre_grad = gelu_back(act_grad)[0].astype(BF16)
        pre_grads.append(pre_grad)
        up_b_grad.append(jnp.sum(pre_grad, axis=0, dtype=F32))
    hidden_two = reduce_rows(pre_grads, [lambda rows, s=s: mm_nt(rows, w_up[s]) for s in both])
    for s in both:
        up_w_grad.append(mm_tn(full_two[s], pre_grads[s]).astype(BF16))
    up_grad = ring.scatter(jnp.stack(up_w_grad))

    mlp_sums = reduce_rows(acts, [lambda rows, s=s: mm_nt(rows, w_down[s]) for s in both])
    outputs, gate_two_grad = ([], [])
    for s in both:
        mlp_bias = mlp_sums[s] + biases_down[s]
        outputs.append((residuals[s] + mods[s, 5] * mlp_bias).astype(BF16))
        gate_two_grad.append(jnp.sum(gradients[s] * mlp_bias, axis=0))

    shift_two_grad, scale_two_grad, mid_grads = ([], [], [])
    gate_one_grad, out_bias_grad, dz_lows = ([], [], [])
    for s in both:
        shift_two_grad.append(jnp.sum(hidden_two[s], axis=0))
        scale_two_grad.append(jnp.sum(hidden_two[s] * normed_two[s], axis=0))
        upstream = hidden_two[s] * (1.0 + mods[s, 4])
        mid_grads.append(gradients[s] + norm_back(upstream, normed_two[s], inv_two[s]))
        gate_one_grad.append(jnp.sum(mid_grads[s] * attn_bias[s], axis=0))
        scaled = mods[s, 2] * mid_grads[s]
        out_bias_grad.append(jnp.sum(scaled, axis=0))
        dz_lows.append(scaled.astype(BF16))
    dz_full = gather_rows(*dz_lows)
    attn_grads = [mm(dz_full[s], w_out[s]).astype(BF16) for s in both]
    out_w_grad = [mm_tn(dz_full[s], attn[s]).astype(BF16) for s in both]
    out_grad = ring.scatter(jnp.stack(out_w_grad))

    packed_grad = attend_back(*packed, *attn_grads, lse)
    hidden_one = reduce_rows(packed_grad, [lambda rows, s=s: mm_nt(rows, w_qkv[s]) for s in both])
    qkv_w_grad, qv_b_grad = ([], [])
    for s in both:
        qkv_w_grad.append(mm_tn(full_one[s], packed_grad[s]).astype(BF16))
        summed = jnp.sum(packed_grad[s], axis=0, dtype=F32).reshape(3, heads_width)
        qv_b_grad.append(jnp.stack([summed[0], summed[2]]))
    qkv_grad = ring.scatter(jnp.stack(qkv_w_grad))
    shift_one_grad, scale_one_grad, new_grads = ([], [], [])
    for s in both:
        shift_one_grad.append(jnp.sum(hidden_one[s], axis=0))
        scale_one_grad.append(jnp.sum(hidden_one[s] * normed_one[s], axis=0))
        upstream = hidden_one[s] * (1.0 + mods[s, 1])
        new_grads.append(mid_grads[s] + norm_back(upstream, normed_one[s], inv_one[s]))

    mod_grad = jnp.stack(
        [
            jnp.concatenate(
                [
                    shift_one_grad[s],
                    scale_one_grad[s],
                    gate_one_grad[s],
                    shift_two_grad[s],
                    scale_two_grad[s],
                    gate_two_grad[s],
                ]
            )
            for s in both
        ]
    )
    bias_grad = jnp.stack(out_bias_grad + down_bias_grad)
    mod_cols = mod_grad.shape[1] // members
    bias_cols = width // members
    by_member = jnp.concatenate(
        [
            mod_grad.reshape(2, members, mod_cols).transpose(1, 0, 2).reshape(members, -1),
            bias_grad.reshape(4, members, bias_cols).transpose(1, 0, 2).reshape(members, -1),
        ],
        axis=1,
    )
    own_part = small_scatter(by_member, "tensor", members)
    mod_part = own_part[: 2 * mod_cols].astype(BF16).astype(F32)
    qv_part = jnp.stack(qv_b_grad).reshape(-1)
    up_part = jnp.stack(up_b_grad).reshape(-1)
    message = jnp.concatenate([mod_part, own_part[2 * mod_cols :], qv_part, up_part])
    every = small_gather(message, "dp", count)
    every_mod = every[:, : 2 * mod_cols].reshape(count, 2, mod_cols)
    every_low = every_mod.astype(BF16)
    summed = jnp.sum(every, axis=0)

    def own_piece(value):
        piece = value.shape[-1] // count
        return lax.dynamic_slice_in_dim(value, dp_rank * piece, piece, value.ndim - 1)

    ends = [2 * mod_cols]
    for size in (4 * bias_cols, qv_part.shape[0], up_part.shape[0]):
        ends.append(ends[-1] + size)
    ada_b_grad = own_piece(summed[: ends[0]].reshape(2, mod_cols))
    bias_sum = own_piece(summed[ends[0] : ends[1]].reshape(2, 2, bias_cols))
    qv_sum = own_piece(summed[ends[1] : ends[2]].reshape(2, 2, heads_width))
    up_sum = own_piece(summed[ends[2] : ends[3]].reshape(2, -1))

    ada_w_grad = jnp.einsum("sr,skc->krc", own_cols, every_low, preferred_element_type=F32)
    cond_terms = jnp.einsum("skc,krc->sr", every_low, ada_w[0], preferred_element_type=F32)
    cond_sum = small_exchange(small_sum(cond_terms, "tensor", members), "dp", count).reshape(1, width)
    sigmoid = jax.nn.sigmoid(own_cond)
    cond_grad = cond_sum * sigmoid * (1.0 + own_cond * (1.0 - sigmoid))
    return (
        outputs[0][None],
        outputs[1][None],
        new_grads[0][None],
        new_grads[1][None],
        cond_grad,
        ada_w_grad[None],
        ada_b_grad[None],
        qkv_grad.reshape(1, 2, row_block, 3, heads_width),
        qv_sum[None],
        out_grad.transpose(0, 2, 1)[None],
        bias_sum[0][None],
        up_grad[None],
        up_sum[None],
        down_grad.transpose(0, 2, 1)[None],
        bias_sum[1][None],
    )


def solution(mesh):
    in_specs = (
        P("dp", "tensor", None),
        P("dp", "tensor", None),
        P(),
        P("dp", "tensor", None),
        P("dp", "tensor", None),
        P(None, None, "dp", "tensor"),
        P(None, None, "tensor"),
        P(None, None, "dp", None, "tensor"),
        P(None, None, None, "tensor"),
        P(None, None, "tensor", "dp"),
        P(),
        P(None, None, "dp", "tensor"),
        P(None, None, "tensor"),
        P(None, None, "tensor", "dp"),
        P(),
    )
    out_specs = (
        P("dp", "tensor", None),
        P("dp", "tensor", None),
        P("dp", "tensor", None),
        P("dp", "tensor", None),
        P("dp", None),
        P(None, None, "dp", "tensor"),
        P(None, None, ("tensor", "dp")),
        P(None, None, "dp", None, "tensor"),
        P(None, None, None, ("tensor", "dp")),
        P(None, None, "tensor", "dp"),
        P(None, None, ("tensor", "dp")),
        P(None, None, "dp", "tensor"),
        P(None, None, ("tensor", "dp")),
        P(None, None, "tensor", "dp"),
        P(None, None, ("tensor", "dp")),
    )
    return jax.shard_map(
        per_device, mesh=mesh, in_specs=in_specs, out_specs=out_specs, check_vma=False
    )
```

time: 2290 us -> 778 us (0.34)
  waiting for transfers between devices: 1760 us -> 387 us
  blocking collectives: 100 us -> 0 us
  starting transfers between devices: 7.69 us -> 101 us
  matrix products: 197 us -> 112 us
  local copies, waits for them, and re-layouts: 136 us -> 79.3 us
  Pallas kernels: 0 us -> 25.5 us
    reduce_scatter x13 -> x0, waiting for transfers between devices: 977 us -> none  [the longest x1 175 us: per_device(): lax.psum_scatter(grad_parts[0], 'dp', scatter_dimension=1, tiled=True)]
    all_gather x8 -> x0, waiting for transfers between devices: 421 us -> none  [the longest x1 140 us: per_device(): lax.all_gather(down_w[layer_num], 'dp', axis=2, tiled=True)]
    ppermute x0 -> x103, waiting for transfers between devices: none -> 387 us  [the longest x32 222 us: right(): return lax.ppermute(value, 'dp', self.right_pairs)]
    unnamed x33 -> x0, waiting for transfers between devices: 355 us -> none
    ppermute x0 -> x103, starting transfers between devices: none -> 101 us  [the longest x32 34.7 us: left(): return lax.ppermute(value, 'dp', self.left_pairs)]
    all_gather x7 -> x0, blocking collectives: 94.3 us -> none  [the longest x1 31.8 us: per_device(): lax.all_gather(mod_low.astype(jnp.float32), 'dp', axis=1, tiled=True)]
    dot_general x69 -> x35, matrix products: 197 us -> 112 us  [the longest x32 109 us: dot(): lax.dot_general(left, right, (dims, ((), ())), preferred_element_type=F32)]
    unnamed x184 -> x352, local copies, waits for them, and re-layouts: 81.3 us -> 11.1 us
  transfers between devices with their start and end apart: 28 -> 103, of which waited for: 23 -> 47; matrix products, arithmetic and copies ran while one was open for 14% -> 28% of each run, Pallas kernels for 0% -> 1%
where the time goes in v1:
time: 778 us; the launch traced here: 769 us
  waiting for transfers between devices  387 us (50%)
  matrix products  112 us (14%)
  starting transfers between devices  101 us (13%)
  local copies, waits for them, and re-layouts  79.3 us (10%)
  other arithmetic  60 us (8%)
  Pallas kernels  25.5 us (3%)
    ppermute x32, waiting for transfers between devices, right(): return lax.ppermute(value, 'dp', self.right_pairs)  222 us
    dot_general x32, matrix products, dot(): lax.dot_general(left, right, (dims, ((), ())), preferred_element_type=F32)  109 us
    ppermute x32, waiting for transfers between devices, left(): return lax.ppermute(value, 'dp', self.left_pairs)  84.4 us
    ppermute x8, waiting for transfers between devices, swap_y(): return lax.ppermute(value, 'tensor', flip_pairs(4, 2))  38.6 us
    ppermute x32, starting transfers between devices, left(): return lax.ppermute(value, 'dp', self.left_pairs)  34.7 us
    ppermute x32, starting transfers between devices, right(): return lax.ppermute(value, 'dp', self.right_pairs)  32.5 us
    dynamic_update_slice x36, local copies, waits for them, and re-layouts, put(): lax.dynamic_update_slice(whole, piece, (0, self.owner(offset) * rows + st...  25.8 us
    ppermute x5, waiting for transfers between devices, small_scatter(): rest = mine + lax.ppermute(other, axis, flip_pairs(count, bit))  24.9 us
  transfers between devices with their start and end apart: 103, of which 47 were waited for; matrix products, arithmetic and copies ran while one was open for 28% of the time, Pallas kernels for 1%

profile of v1, /device:TPU:0, one launch (start us, length us, event | category | flops | bytes accessed | tf_op | source)
XLA Modules:
  0.0 768.7 jit_solution(12588314015207938828)
XLA Ops:
  12.1 17.0 %collective-permute-done = f32[4,2,2304]{2,0,1:T(4,128)S(1)} collective-permute-done((f32[4,2,2304]{2,0,1:T(4,128)S(1)}, f32[4,2,2304]{2,0,1:T(4,128)S(1)}, u32[]{:S(2)}, u32[]{:S(2)}) %collective-permute-start) | collective-permute-done | bytes 73760 | tf_op jit(solution)/shard_map/ppermute | solution.py:137
  29.5 3.8 collective-permute-done.1
  33.4 3.7 collective-permute-start.2
  49.6 3.4 broadcast_in_dim.28
  54.0 8.6 %collective-permute-done.5 = bf16[224,1536]{1,0:T(8,128)(2,1)} collective-permute-done((bf16[224,1536]{1,0:T(8,128)(2,1)}, bf16[224,1536]{1,0:T(8,128)(2,1)}, u32[]{:S(2)}, u32[]{:S(2)}) %collective-permute-start.5) | collective-permute-done | bytes 688160 | tf_op jit(solution)/shard_map/ppermute | solution.py:186
  79.8 9.6 %collective-permute-done.12 = bf16[2,192,1152]{2,1,0:T(8,128)(2,1)S(1)} collective-permute-done((bf16[2,192,1152]{2,1,0:T(8,128)(2,1)S(1)}, bf16[2,192,1152]{2,1,0:T(8,128)(2,1)S(1)}, u32[]{:S(2)}, u32[]{:S(2)}) %collective-permute-start.12) | collective-permute-done | bytes 884768 | tf_op jit(solution)/shard_map/ppermute | solution.py:64
  97.9 3.5 collective-permute-done.16
  103.5 7.3 collective-permute-done.14
  113.4 5.2 fusion.25.qi.ki.vi
  124.5 8.7 %shard_map.262 = (bf16[768,384]{1,0:T(8,128)(2,1)S(1)}, bf16[128,384]{1,0:T(8,128)(2,1)S(1)}, f32[3,2,896]{2,1,0:T(2,128)S(1)}) custom-call(bf16[768,1152]{1,0:T(8,128)(2,1)S(1)} %fusion.25.qi.ki.vi, bf16[128,1152]{1,0:T(8,128)(2,1)S(1)} %fusion.36.qt.kt.vt, bf16[768,1152]{1,0:T(8,128)(2,1)S(1)} %fusion.25.qi.ki.vi, bf16[128,1152]{1,0:T(8,128)(2,1)S(1)} %fusion.36.qt.kt.vt, ...), custom_call_target="tpu_custom_call" | custom-call | flops 4932501504 | bytes 3096576 | tf_op jit(solution)/shard_map/pallas_call | solution.py:262
  146.7 14.2 %collective-permute-done.49 = bf16[224,1536]{1,0:T(8,128)(2,1)} collective-permute-done((bf16[224,1536]{1,0:T(8,128)(2,1)S(1)}, bf16[224,1536]{1,0:T(8,128)(2,1)}, u32[]{:S(2)}, u32[]{:S(2)}) %collective-permute-start.49) | collective-permute-done | bytes 688160 | tf_op jit(solution)/shard_map/ppermute | solution.py:186
  184.4 17.1 %collective-permute-done.32 = bf16[2,192,1536]{2,1,0:T(8,128)(2,1)} collective-permute-done((bf16[2,192,1536]{2,1,0:T(8,128)(2,1)}, bf16[2,192,1536]{2,1,0:T(8,128)(2,1)}, u32[]{:S(2)}, u32[]{:S(2)}) %collective-permute-start.32) | collective-permute-done | bytes 1179680 | tf_op jit(solution)/shard_map/ppermute | solution.py:64
  208.6 20.1 %collective-permute-done.34 = bf16[2,192,1536]{2,1,0:T(8,128)(2,1)S(1)} collective-permute-done((bf16[2,192,1536]{2,1,0:T(8,128)(2,1)}, bf16[2,192,1536]{2,1,0:T(8,128)(2,1)S(1)}, u32[]{:S(2)}, u32[]{:S(2)}) %collective-permute-start.34) | collective-permute-done | bytes 1179680 | tf_op jit(solution)/shard_map/ppermute | solution.py:64
  234.0 33.7 %collective-permute-done.36 = bf16[2,96,1536]{2,1,0:T(8,128)(2,1)S(1)} collective-permute-done((bf16[2,96,1536]{2,1,0:T(8,128)(2,1)S(1)}, bf16[2,96,1536]{2,1,0:T(8,128)(2,1)S(1)}, u32[]{:S(2)}, u32[]{:S(2)}) %collective-permute-start.36) | collective-permute-done | bytes 589856 | tf_op jit(solution)/shard_map/ppermute | solution.py:64
  270.4 6.7 multiply_convert_fusion
  277.2 4.1 fusion.5
  289.9 6.9 collective-permute-done.39
  298.0 9.1 %collective-permute-done.95 = bf16[2,96,1536]{2,1,0:T(8,128)(2,1)} collective-permute-done((bf16[2,96,1536]{2,1,0:T(8,128)(2,1)}, bf16[2,96,1536]{2,1,0:T(8,128)(2,1)}, u32[]{:S(2)}, u32[]{:S(2)}) %collective-permute-start.95) | collective-permute-done | bytes 589856 | tf_op jit(solution)/shard_map/ppermute | solution.py:64
  316.7 18.0 %collective-permute-done.41 = bf16[2,192,1536]{2,1,0:T(8,128)(2,1)} collective-permute-done((bf16[2,192,1536]{2,1,0:T(8,128)(2,1)}, bf16[2,192,1536]{2,1,0:T(8,128)(2,1)}, u32[]{:S(2)}, u32[]{:S(2)}) %collective-permute-start.41) | collective-permute-done | bytes 1179680 | tf_op jit(solution)/shard_map/ppermute | solution.py:67
  340.0 22.9 %collective-permute-done.42 = bf16[2,192,1536]{2,1,0:T(8,128)(2,1)S(1)} collective-permute-done((bf16[2,192,1536]{2,1,0:T(8,128)(2,1)}, bf16[2,192,1536]{2,1,0:T(8,128)(2,1)S(1)}, u32[]{:S(2)}, u32[]{:S(2)}) %collective-permute-start.42) | collective-permute-done | bytes 1179680 | tf_op jit(solution)/shard_map/ppermute | solution.py:64
  369.1 16.0 %collective-permute-done.43 = bf16[2,192,1536]{2,1,0:T(8,128)(2,1)S(1)} collective-permute-done((bf16[2,192,1536]{2,1,0:T(8,128)(2,1)}, bf16[2,192,1536]{2,1,0:T(8,128)(2,1)S(1)}, u32[]{:S(2)}, u32[]{:S(2)}) %collective-permute-start.43) | collective-permute-done | bytes 1179680 | tf_op jit(solution)/shard_map/ppermute | solution.py:67
  387.1 31.9 %collective-permute-done.45 = bf16[2,96,1536]{2,1,0:T(8,128)(2,1)S(1)} collective-permute-done((bf16[2,96,1536]{2,1,0:T(8,128)(2,1)S(1)}, bf16[2,96,1536]{2,1,0:T(8,128)(2,1)S(1)}, u32[]{:S(2)}, u32[]{:S(2)}) %collective-permute-start.45) | collective-permute-done | bytes 589856 | tf_op jit(solution)/shard_map/ppermute | solution.py:67
  419.1 3.4 fusion.17
  424.6 10.7 %convert_reduce_fusion = (f32[1536]{0:T(1024)S(1)}, bf16[768,1536]{1,0:T(8,128)(2,1)}) fusion(f32[768,1536]{1,0:T(8,128)} %get-tuple-element.196, f32[1536]{0:T(1024)S(1)} %copy-done.143, bf16[2,1536,1536]{2,1,0:T(8,128)(2,1)S(1)} %constant_dynamic-update-slice_fusion, bf16[192,1536]{1,0:T(8,128)(2,1)S(1)} %copy-done.75, ...), kind=kOutput, calls=%fused_computation.97 | convolution fusion | flops 3660446208 | bytes 14170112 | tf_op jit(solution)/shard_map/dot_general | solution.py:31
  435.3 6.1 fusion.4
  447.6 4.8 fusion.19
  455.3 6.1 fusion.13
  468.8 3.9 fusion.39
  473.5 3.7 add_convert_fusion.3
  478.3 13.2 %collective-permute-done.88 = bf16[2,192,1536]{2,1,0:T(8,128)(2,1)S(1)} collective-permute-done((bf16[2,192,1536]{2,1,0:T(8,128)(2,1)S(1)}, bf16[2,192,1536]{2,1,0:T(8,128)(2,1)S(1)}, u32[]{:S(2)}, u32[]{:S(2)}) %collective-permute-start.88) | collective-permute-done | bytes 1179680 | tf_op jit(solution)/shard_map/ppermute | solution.py:64
  497.0 5.5 fusion.26
  503.8 4.1 fusion.27
  509.7 34.4 %collective-permute-done.89 = bf16[2,192,1536]{2,1,0:T(8,128)(2,1)S(1)} collective-permute-done((bf16[2,192,1536]{2,1,0:T(8,128)(2,1)}, bf16[2,192,1536]{2,1,0:T(8,128)(2,1)S(1)}, u32[]{:S(2)}, u32[]{:S(2)}) %collective-permute-start.89) | collective-permute-done | bytes 1179680 | tf_op jit(solution)/shard_map/ppermute | solution.py:64
  545.6 3.3 add_convert_fusion.9
  553.2 6.7 collective-permute-done.48
  567.8 3.8 add_bitcast_fusion
  571.7 9.2 %collective-permute-done.55 = bf16[224,1536]{1,0:T(8,128)(2,1)} collective-permute-done((bf16[224,1536]{1,0:T(8,128)(2,1)}, bf16[224,1536]{1,0:T(8,128)(2,1)}, u32[]{:S(2)}, u32[]{:S(2)}) %collective-permute-start.55) | collective-permute-done | bytes 688160 | tf_op jit(solution)/shard_map/ppermute | solution.py:186
  585.6 3.9 add_bitcast_fusion.1
  593.6 16.8 %shard_map.263 = (bf16[768,1152]{1,0:T(8,128)(2,1)S(1)}, bf16[128,1152]{1,0:T(8,128)(2,1)S(1)}) custom-call(bf16[768,1152]{1,0:T(8,128)(2,1)S(1)} %copy-done.8, bf16[128,1152]{1,0:T(8,128)(2,1)S(1)} %fusion.36.qt.kt.vt, bf16[768,1152]{1,0:T(8,128)(2,1)S(1)} %copy-done.8, bf16[128,1152]{1,0:T(8,128)(2,1)S(1)} %fusion.36.qt.kt.vt, ...), custom_call_target="tpu_custom_call" | custom-call | flops 12331253760 | bytes 5160960 | tf_op jit(solution)/shard_map/pallas_call | solution.py:333
  610.4 4.6 fusion.29
  615.1 5.3 fusion.28
  620.7 3.5 fusion.2
  633.6 11.0 %collective-permute-done.79 = bf16[2,96,384]{2,1,0:T(8,128)(2,1)S(1)} collective-permute-done((bf16[2,96,384]{2,1,0:T(8,128)(2,1)S(1)}, bf16[2,96,384]{2,1,0:T(8,128)(2,1)S(1)}, u32[]{:S(2)}, u32[]{:S(2)}) %collective-permute-start.79) | collective-permute-done | bytes 147488 | tf_op jit(solution)/shard_map/ppermute | solution.py:64
  649.2 5.9 collective-permute-done.80
  660.8 3.4 fusion.37
  664.2 15.3 %collective-permute-done.81 = bf16[2,192,384]{2,1,0:T(8,128)(2,1)S(1)} collective-permute-done((bf16[2,192,384]{2,1,0:T(8,128)(2,1)S(1)}, bf16[2,192,384]{2,1,0:T(8,128)(2,1)S(1)}, u32[]{:S(2)}, u32[]{:S(2)}) %collective-permute-start.81) | collective-permute-done | bytes 294944 | tf_op jit(solution)/shard_map/ppermute | solution.py:64
  687.7 4.5 convolution_add_fusion.2
  694.6 12.8 %collective-permute-done.73 = bf16[2,192,1152]{2,1,0:T(8,128)(2,1)S(1)} collective-permute-done((bf16[2,192,1152]{2,1,0:T(8,128)(2,1)S(1)}, bf16[2,192,1152]{2,1,0:T(8,128)(2,1)S(1)}, u32[]{:S(2)}, u32[]{:S(2)}) %collective-permute-start.73) | collective-permute-done | bytes 884768 | tf_op jit(solution)/shard_map/ppermute | solution.py:64
  (794 shorter events, 286.9 us)
Async XLA Ops:
  4.7 42.8 %collective-permute-start.8 = (bf16[2,192,1152]{2,1,0:T(8,128)(2,1)}, bf16[2,192,1152]{2,1,0:T(8,128)(2,1)}, u32[]{:S(2)}, u32[]{:S(2)}) collective-permute-start(bf16[2,192,1152]{2,1,0:T(8,128)(2,1)} %reshape_squeeze.3), channel_id=1, source_target_pairs={{0,8},{8,16},{16,24},{24,28},{28,20},{20,12},{12,4},{4,0},{1,9},{9... | collective-permute-start | bytes 2654216 | tf_op jit(solution)/shard_map/ppermute | solution.py:64
  7.7 41.8 %collective-permute-start.9 = (bf16[2,192,1152]{2,1,0:T(8,128)(2,1)}, bf16[2,192,1152]{2,1,0:T(8,128)(2,1)}, u32[]{:S(2)}, u32[]{:S(2)}) collective-permute-start(bf16[2,192,1152]{2,1,0:T(8,128)(2,1)} %reshape_squeeze.3), channel_id=1, source_target_pairs={{0,4},{8,0},{16,8},{24,16},{28,24},{20,28},{12,20},{4,12},{1,5},{9... | collective-permute-start | bytes 2654216 | tf_op jit(solution)/shard_map/ppermute | solution.py:67
  68.0 21.4 %collective-permute-start.12 = (bf16[2,192,1152]{2,1,0:T(8,128)(2,1)S(1)}, bf16[2,192,1152]{2,1,0:T(8,128)(2,1)S(1)}, u32[]{:S(2)}, u32[]{:S(2)}) collective-permute-start(bf16[2,192,1152]{2,1,0:T(8,128)(2,1)S(1)} %collective-permute-done.10), channel_id=1, source_target_pairs={{0,8},{8,16},{16,24},{24,28},{28,20},{20,12},{12,4},{4,0},{1,9},{9... | collective-permute-start | bytes 2654216 | tf_op jit(solution)/shard_map/ppermute | solution.py:64
  70.1 21.3 %collective-permute-start.13 = (bf16[2,192,1152]{2,1,0:T(8,128)(2,1)}, bf16[2,192,1152]{2,1,0:T(8,128)(2,1)S(1)}, u32[]{:S(2)}, u32[]{:S(2)}) collective-permute-start(bf16[2,192,1152]{2,1,0:T(8,128)(2,1)} %collective-permute-done.11), channel_id=1, source_target_pairs={{0,4},{8,0},{16,8},{24,16},{28,24},{20,28},{12,20},{4,12},{1,5},{9... | collective-permute-start | bytes 2654216 | tf_op jit(solution)/shard_map/ppermute | solution.py:67
  142.7 32.6 %collective-permute-start.24 = (f32[384,1536]{1,0:T(8,128)}, f32[384,1536]{1,0:T(8,128)}, u32[]{:S(2)}, u32[]{:S(2)}) collective-permute-start(f32[384,1536]{1,0:T(8,128)} %fusion.87), channel_id=1, source_target_pairs={{0,1},{1,0},{2,3},{3,2},{4,5},{5,4},{6,7},{7,6},{8,9},{9,8},{10,11... | collective-permute-start | bytes 7077896 | tf_op jit(solution)/shard_map/ppermute | solution.py:182
  144.7 28.5 %collective-permute-start.30 = (bf16[2,192,1536]{2,1,0:T(8,128)(2,1)}, bf16[2,192,1536]{2,1,0:T(8,128)(2,1)}, u32[]{:S(2)}, u32[]{:S(2)}) collective-permute-start(bf16[2,192,1536]{2,1,0:T(8,128)(2,1)} %bitcast.21), channel_id=1, source_target_pairs={{0,8},{8,16},{16,24},{24,28},{28,20},{20,12},{12,4},{4,0},{1,9},{9... | collective-permute-start | bytes 3538952 | tf_op jit(solution)/shard_map/ppermute | solution.py:64
  145.5 28.6 %collective-permute-start.31 = (bf16[2,192,1536]{2,1,0:T(8,128)(2,1)}, bf16[2,192,1536]{2,1,0:T(8,128)(2,1)}, u32[]{:S(2)}, u32[]{:S(2)}) collective-permute-start(bf16[2,192,1536]{2,1,0:T(8,128)(2,1)} %bitcast.21), channel_id=1, source_target_pairs={{0,4},{8,0},{16,8},{24,16},{28,24},{20,28},{12,20},{4,12},{1,5},{9... | collective-permute-start | bytes 3538952 | tf_op jit(solution)/shard_map/ppermute | solution.py:67
  173.2 28.2 %collective-permute-start.32 = (bf16[2,192,1536]{2,1,0:T(8,128)(2,1)}, bf16[2,192,1536]{2,1,0:T(8,128)(2,1)}, u32[]{:S(2)}, u32[]{:S(2)}) collective-permute-start(bf16[2,192,1536]{2,1,0:T(8,128)(2,1)} %collective-permute-done.30), channel_id=1, source_target_pairs={{0,8},{8,16},{16,24},{24,28},{28,20},{20,12},{12,4},{4,0},{1,9},{9... | collective-permute-start | bytes 3538952 | tf_op jit(solution)/shard_map/ppermute | solution.py:64
  174.1 28.2 %collective-permute-start.33 = (bf16[2,192,1536]{2,1,0:T(8,128)(2,1)}, bf16[2,192,1536]{2,1,0:T(8,128)(2,1)}, u32[]{:S(2)}, u32[]{:S(2)}) collective-permute-start(bf16[2,192,1536]{2,1,0:T(8,128)(2,1)} %collective-permute-done.31), channel_id=1, source_target_pairs={{0,4},{8,0},{16,8},{24,16},{28,24},{20,28},{12,20},{4,12},{1,5},{9... | collective-permute-start | bytes 3538952 | tf_op jit(solution)/shard_map/ppermute | solution.py:67
  178.0 25.6 %collective-permute-start.26 = (bf16[224,1536]{1,0:T(8,128)(2,1)S(1)}, bf16[224,1536]{1,0:T(8,128)(2,1)S(1)}, u32[]{:S(2)}, u32[]{:S(2)}) collective-permute-start(bf16[224,1536]{1,0:T(8,128)(2,1)S(1)} %pad_maximum_fusion.5), channel_id=1, source_target_pairs={{0,2},{1,3},{2,0},{3,1},{4,6},{5,7},{6,4},{7,5},{8,10},{9,11},{10,... | collective-permute-start | bytes 2064392 | tf_op jit(solution)/shard_map/ppermute | solution.py:186
  201.5 27.2 %collective-permute-start.34 = (bf16[2,192,1536]{2,1,0:T(8,128)(2,1)}, bf16[2,192,1536]{2,1,0:T(8,128)(2,1)S(1)}, u32[]{:S(2)}, u32[]{:S(2)}) collective-permute-start(bf16[2,192,1536]{2,1,0:T(8,128)(2,1)} %collective-permute-done.32), channel_id=1, source_target_pairs={{0,8},{8,16},{16,24},{24,28},{28,20},{20,12},{12,4},{4,0},{1,9},{9... | collective-permute-start | bytes 3538952 | tf_op jit(solution)/shard_map/ppermute | solution.py:64
  202.3 27.0 %collective-permute-start.35 = (bf16[2,192,1536]{2,1,0:T(8,128)(2,1)}, bf16[2,192,1536]{2,1,0:T(8,128)(2,1)S(1)}, u32[]{:S(2)}, u32[]{:S(2)}) collective-permute-start(bf16[2,192,1536]{2,1,0:T(8,128)(2,1)} %collective-permute-done.33), channel_id=1, source_target_pairs={{0,4},{8,0},{16,8},{24,16},{28,24},{20,28},{12,20},{4,12},{1,5},{9... | collective-permute-start | bytes 3538952 | tf_op jit(solution)/shard_map/ppermute | solution.py:67
  205.6 27.8 %collective-permute-start.27 = (bf16[224,1536]{1,0:T(8,128)(2,1)S(1)}, bf16[224,1536]{1,0:T(8,128)(2,1)S(1)}, u32[]{:S(2)}, u32[]{:S(2)}) collective-permute-start(bf16[224,1536]{1,0:T(8,128)(2,1)S(1)} %pad_maximum_fusion.6), channel_id=1, source_target_pairs={{0,2},{1,3},{2,0},{3,1},{4,6},{5,7},{6,4},{7,5},{8,10},{9,11},{10,... | collective-permute-start | bytes 2064392 | tf_op jit(solution)/shard_map/ppermute | solution.py:186
  229.3 40.0 %collective-permute-start.38 = (bf16[2,192,1536]{2,1,0:T(8,128)(2,1)S(1)}, bf16[2,192,1536]{2,1,0:T(8,128)(2,1)}, u32[]{:S(2)}, u32[]{:S(2)}) collective-permute-start(bf16[2,192,1536]{2,1,0:T(8,128)(2,1)S(1)} %bitcast.310), channel_id=1, source_target_pairs={{0,8},{8,16},{16,24},{24,28},{28,20},{20,12},{12,4},{4,0},{1,9},{9... | collective-permute-start | bytes 3538952 | tf_op jit(solution)/shard_map/ppermute | solution.py:64
  229.7 38.1 %collective-permute-start.36 = (bf16[2,96,1536]{2,1,0:T(8,128)(2,1)S(1)}, bf16[2,96,1536]{2,1,0:T(8,128)(2,1)S(1)}, u32[]{:S(2)}, u32[]{:S(2)}) collective-permute-start(bf16[2,96,1536]{2,1,0:T(8,128)(2,1)S(1)} %slice.680), channel_id=1, source_target_pairs={{0,8},{8,16},{16,24},{24,28},{28,20},{20,12},{12,4},{4,0},{1,9},{9... | collective-permute-start | bytes 1769480 | tf_op jit(solution)/shard_map/ppermute | solution.py:64
  231.5 37.5 %collective-permute-start.37 = (bf16[2,96,1536]{2,1,0:T(8,128)(2,1)S(1)}, bf16[2,96,1536]{2,1,0:T(8,128)(2,1)S(1)}, u32[]{:S(2)}, u32[]{:S(2)}) collective-permute-start(bf16[2,96,1536]{2,1,0:T(8,128)(2,1)S(1)} %slice.681), channel_id=1, source_target_pairs={{0,4},{8,0},{16,8},{24,16},{28,24},{20,28},{12,20},{4,12},{1,5},{9... | collective-permute-start | bytes 1769480 | tf_op jit(solution)/shard_map/ppermute | solution.py:67
  233.3 35.7 %collective-permute-start.28 = (bf16[224,1536]{1,0:T(8,128)(2,1)S(1)}, bf16[224,1536]{1,0:T(8,128)(2,1)S(1)}, u32[]{:S(2)}, u32[]{:S(2)}) collective-permute-start(bf16[224,1536]{1,0:T(8,128)(2,1)S(1)} %pad_maximum_fusion.6), channel_id=1, source_target_pairs={{0,1},{1,0},{2,3},{3,2},{4,5},{5,4},{6,7},{7,6},{8,9},{9,8},{10,11... | collective-permute-start | bytes 2064392 | tf_op jit(solution)/shard_map/ppermute | solution.py:182
  233.4 36.9 %collective-permute-start.29 = (bf16[224,1536]{1,0:T(8,128)(2,1)S(1)}, bf16[224,1536]{1,0:T(8,128)(2,1)S(1)}, u32[]{:S(2)}, u32[]{:S(2)}) collective-permute-start(bf16[224,1536]{1,0:T(8,128)(2,1)S(1)} %collective-permute-done.27), channel_id=1, source_target_pairs={{0,1},{1,0},{2,3},{3,2},{4,5},{5,4},{6,7},{7,6},{8,9},{9,8},{10,11... | collective-permute-start | bytes 2064392 | tf_op jit(solution)/shard_map/ppermute | solution.py:182
  267.7 29.0 %collective-permute-start.39 = (bf16[2,192,1536]{2,1,0:T(8,128)(2,1)S(1)}, bf16[2,192,1536]{2,1,0:T(8,128)(2,1)}, u32[]{:S(2)}, u32[]{:S(2)}) collective-permute-start(bf16[2,192,1536]{2,1,0:T(8,128)(2,1)S(1)} %bitcast.311), channel_id=1, source_target_pairs={{0,4},{8,0},{16,8},{24,16},{28,24},{20,28},{12,20},{4,12},{1,5},{9... | collective-permute-start | bytes 3538952 | tf_op jit(solution)/shard_map/ppermute | solution.py:67
  269.2 44.5 %collective-permute-start.40 = (bf16[2,192,1536]{2,1,0:T(8,128)(2,1)}, bf16[2,192,1536]{2,1,0:T(8,128)(2,1)}, u32[]{:S(2)}, u32[]{:S(2)}) collective-permute-start(bf16[2,192,1536]{2,1,0:T(8,128)(2,1)} %collective-permute-done.38), channel_id=1, source_target_pairs={{0,8},{8,16},{16,24},{24,28},{28,20},{20,12},{12,4},{4,0},{1,9},{9... | collective-permute-start | bytes 3538952 | tf_op jit(solution)/shard_map/ppermute | solution.py:64
  296.7 37.9 %collective-permute-start.41 = (bf16[2,192,1536]{2,1,0:T(8,128)(2,1)}, bf16[2,192,1536]{2,1,0:T(8,128)(2,1)}, u32[]{:S(2)}, u32[]{:S(2)}) collective-permute-start(bf16[2,192,1536]{2,1,0:T(8,128)(2,1)} %collective-permute-done.39), channel_id=1, source_target_pairs={{0,4},{8,0},{16,8},{24,16},{28,24},{20,28},{12,20},{4,12},{1,5},{9... | collective-permute-start | bytes 3538952 | tf_op jit(solution)/shard_map/ppermute | solution.py:67
  311.7 51.9 %collective-permute-start.96 = (bf16[2,192,1536]{2,1,0:T(8,128)(2,1)S(1)}, bf16[2,192,1536]{2,1,0:T(8,128)(2,1)S(1)}, u32[]{:S(2)}, u32[]{:S(2)}) collective-permute-start(bf16[2,192,1536]{2,1,0:T(8,128)(2,1)S(1)} %get-tuple-element.138), channel_id=1, source_target_pairs={{0,8},{8,16},{16,24},{24,28},{28,20},{20,12},{12,4},{4,0},{1,9},{9... | collective-permute-start | bytes 3538952 | tf_op jit(solution)/shard_map/ppermute | solution.py:64
  312.3 51.3 %collective-permute-start.100 = (bf16[2,192,1536]{2,1,0:T(8,128)(2,1)S(1)}, bf16[2,192,1536]{2,1,0:T(8,128)(2,1)}, u32[]{:S(2)}, u32[]{:S(2)}) collective-permute-start(bf16[2,192,1536]{2,1,0:T(8,128)(2,1)S(1)} %get-tuple-element.139), channel_id=1, source_target_pairs={{0,4},{8,0},{16,8},{24,16},{28,24},{20,28},{12,20},{4,12},{1,5},{9... | collective-permute-start | bytes 3538952 | tf_op jit(solution)/shard_map/ppermute | solution.py:67
  313.8 49.2 %collective-permute-start.42 = (bf16[2,192,1536]{2,1,0:T(8,128)(2,1)}, bf16[2,192,1536]{2,1,0:T(8,128)(2,1)S(1)}, u32[]{:S(2)}, u32[]{:S(2)}) collective-permute-start(bf16[2,192,1536]{2,1,0:T(8,128)(2,1)} %collective-permute-done.40), channel_id=1, source_target_pairs={{0,8},{8,16},{16,24},{24,28},{28,20},{20,12},{12,4},{4,0},{1,9},{9... | collective-permute-start | bytes 3538952 | tf_op jit(solution)/shard_map/ppermute | solution.py:64
  334.7 50.5 %collective-permute-start.43 = (bf16[2,192,1536]{2,1,0:T(8,128)(2,1)}, bf16[2,192,1536]{2,1,0:T(8,128)(2,1)S(1)}, u32[]{:S(2)}, u32[]{:S(2)}) collective-permute-start(bf16[2,192,1536]{2,1,0:T(8,128)(2,1)} %collective-permute-done.41), channel_id=1, source_target_pairs={{0,4},{8,0},{16,8},{24,16},{28,24},{20,28},{12,20},{4,12},{1,5},{9... | collective-permute-start | bytes 3538952 | tf_op jit(solution)/shard_map/ppermute | solution.py:67
  363.0 24.0 %collective-permute-start.44 = (bf16[2,96,1536]{2,1,0:T(8,128)(2,1)S(1)}, bf16[2,96,1536]{2,1,0:T(8,128)(2,1)S(1)}, u32[]{:S(2)}, u32[]{:S(2)}) collective-permute-start(bf16[2,96,1536]{2,1,0:T(8,128)(2,1)S(1)} %slice.685), channel_id=1, source_target_pairs={{0,8},{8,16},{16,24},{24,28},{28,20},{20,12},{12,4},{4,0},{1,9},{9... | collective-permute-start | bytes 1769480 | tf_op jit(solution)/shard_map/ppermute | solution.py:64
  367.0 97.0 %collective-permute-start.97 = (bf16[2,192,1536]{2,1,0:T(8,128)(2,1)}, bf16[2,192,1536]{2,1,0:T(8,128)(2,1)}, u32[]{:S(2)}, u32[]{:S(2)}) collective-permute-start(bf16[2,192,1536]{2,1,0:T(8,128)(2,1)} %get-tuple-element.136), channel_id=1, source_target_pairs={{0,8},{8,16},{16,24},{24,28},{28,20},{20,12},{12,4},{4,0},{1,9},{9... | collective-permute-start | bytes 3538952 | tf_op jit(solution)/shard_map/ppermute | solution.py:64
  367.4 106.1 %collective-permute-start.101 = (bf16[2,192,1536]{2,1,0:T(8,128)(2,1)}, bf16[2,192,1536]{2,1,0:T(8,128)(2,1)}, u32[]{:S(2)}, u32[]{:S(2)}) collective-permute-start(bf16[2,192,1536]{2,1,0:T(8,128)(2,1)} %get-tuple-element.137), channel_id=1, source_target_pairs={{0,4},{8,0},{16,8},{24,16},{28,24},{20,28},{12,20},{4,12},{1,5},{9... | collective-permute-start | bytes 3538952 | tf_op jit(solution)/shard_map/ppermute | solution.py:67
  385.1 33.9 %collective-permute-start.45 = (bf16[2,96,1536]{2,1,0:T(8,128)(2,1)S(1)}, bf16[2,96,1536]{2,1,0:T(8,128)(2,1)S(1)}, u32[]{:S(2)}, u32[]{:S(2)}) collective-permute-start(bf16[2,96,1536]{2,1,0:T(8,128)(2,1)S(1)} %slice.686), channel_id=1, source_target_pairs={{0,4},{8,0},{16,8},{24,16},{28,24},{20,28},{12,20},{4,12},{1,5},{9... | collective-permute-start | bytes 1769480 | tf_op jit(solution)/shard_map/ppermute | solution.py:67
  454.5 40.8 %collective-permute-start.46 = (f32[384,1536]{1,0:T(8,128)S(1)}, f32[384,1536]{1,0:T(8,128)}, u32[]{:S(2)}, u32[]{:S(2)}) collective-permute-start(f32[384,1536]{1,0:T(8,128)S(1)} %copy-done.158), channel_id=1, source_target_pairs={{0,1},{1,0},{2,3},{3,2},{4,5},{5,4},{6,7},{7,6},{8,9},{9,8},{10,11... | collective-permute-start | bytes 7077896 | tf_op jit(solution)/shard_map/ppermute | solution.py:182
  463.0 40.8 %collective-permute-start.52 = (f32[384,1536]{1,0:T(8,128)}, f32[384,1536]{1,0:T(8,128)}, u32[]{:S(2)}, u32[]{:S(2)}) collective-permute-start(f32[384,1536]{1,0:T(8,128)} %fusion.13), channel_id=1, source_target_pairs={{0,1},{1,0},{2,3},{3,2},{4,5},{5,4},{6,7},{7,6},{8,9},{9,8},{10,11... | collective-permute-start | bytes 7077896 | tf_op jit(solution)/shard_map/ppermute | solution.py:182
  463.6 27.9 %collective-permute-start.88 = (bf16[2,192,1536]{2,1,0:T(8,128)(2,1)S(1)}, bf16[2,192,1536]{2,1,0:T(8,128)(2,1)S(1)}, u32[]{:S(2)}, u32[]{:S(2)}) collective-permute-start(bf16[2,192,1536]{2,1,0:T(8,128)(2,1)S(1)} %get-tuple-element.146), channel_id=1, source_target_pairs={{0,8},{8,16},{16,24},{24,28},{28,20},{20,12},{12,4},{4,0},{1,9},{9... | collective-permute-start | bytes 3538952 | tf_op jit(solution)/shard_map/ppermute | solution.py:64
  464.1 28.9 %collective-permute-start.92 = (bf16[2,192,1536]{2,1,0:T(8,128)(2,1)S(1)}, bf16[2,192,1536]{2,1,0:T(8,128)(2,1)S(1)}, u32[]{:S(2)}, u32[]{:S(2)}) collective-permute-start(bf16[2,192,1536]{2,1,0:T(8,128)(2,1)S(1)} %get-tuple-element.147), channel_id=1, source_target_pairs={{0,4},{8,0},{16,8},{24,16},{28,24},{20,28},{12,20},{4,12},{1,5},{9... | collective-permute-start | bytes 3538952 | tf_op jit(solution)/shard_map/ppermute | solution.py:67
  477.2 90.6 %collective-permute-start.102 = (bf16[2,192,1536]{2,1,0:T(8,128)(2,1)}, bf16[2,192,1536]{2,1,0:T(8,128)(2,1)}, u32[]{:S(2)}, u32[]{:S(2)}) collective-permute-start(bf16[2,192,1536]{2,1,0:T(8,128)(2,1)} %get-tuple-element.135), channel_id=1, source_target_pairs={{0,4},{8,0},{16,8},{24,16},{28,24},{20,28},{12,20},{4,12},{1,5},{9... | collective-permute-start | bytes 3538952 | tf_op jit(solution)/shard_map/ppermute | solution.py:67
  491.5 76.3 %collective-permute-start.98 = (bf16[2,192,1536]{2,1,0:T(8,128)(2,1)}, bf16[2,192,1536]{2,1,0:T(8,128)(2,1)}, u32[]{:S(2)}, u32[]{:S(2)}) collective-permute-start(bf16[2,192,1536]{2,1,0:T(8,128)(2,1)} %get-tuple-element.134), channel_id=1, source_target_pairs={{0,8},{8,16},{16,24},{24,28},{28,20},{20,12},{12,4},{4,0},{1,9},{9... | collective-permute-start | bytes 3538952 | tf_op jit(solution)/shard_map/ppermute | solution.py:64
  495.0 49.1 %collective-permute-start.89 = (bf16[2,192,1536]{2,1,0:T(8,128)(2,1)}, bf16[2,192,1536]{2,1,0:T(8,128)(2,1)S(1)}, u32[]{:S(2)}, u32[]{:S(2)}) collective-permute-start(bf16[2,192,1536]{2,1,0:T(8,128)(2,1)} %get-tuple-element.144), channel_id=1, source_target_pairs={{0,8},{8,16},{16,24},{24,28},{28,20},{20,12},{12,4},{4,0},{1,9},{9... | collective-permute-start | bytes 3538952 | tf_op jit(solution)/shard_map/ppermute | solution.py:64
  495.3 50.3 %collective-permute-start.93 = (bf16[2,192,1536]{2,1,0:T(8,128)(2,1)}, bf16[2,192,1536]{2,1,0:T(8,128)(2,1)}, u32[]{:S(2)}, u32[]{:S(2)}) collective-permute-start(bf16[2,192,1536]{2,1,0:T(8,128)(2,1)} %get-tuple-element.145), channel_id=1, source_target_pairs={{0,4},{8,0},{16,8},{24,16},{28,24},{20,28},{12,20},{4,12},{1,5},{9... | collective-permute-start | bytes 3538952 | tf_op jit(solution)/shard_map/ppermute | solution.py:67
  508.1 41.9 %collective-permute-start.54 = (bf16[224,1536]{1,0:T(8,128)(2,1)S(1)}, bf16[224,1536]{1,0:T(8,128)(2,1)S(1)}, u32[]{:S(2)}, u32[]{:S(2)}) collective-permute-start(bf16[224,1536]{1,0:T(8,128)(2,1)S(1)} %pad_maximum_fusion.9), channel_id=1, source_target_pairs={{0,2},{1,3},{2,0},{3,1},{4,6},{5,7},{6,4},{7,5},{8,10},{9,11},{10,... | collective-permute-start | bytes 2064392 | tf_op jit(solution)/shard_map/ppermute | solution.py:186
  549.0 36.6 %collective-permute-start.94 = (bf16[2,192,1536]{2,1,0:T(8,128)(2,1)}, bf16[2,192,1536]{2,1,0:T(8,128)(2,1)}, u32[]{:S(2)}, u32[]{:S(2)}) collective-permute-start(bf16[2,192,1536]{2,1,0:T(8,128)(2,1)} %get-tuple-element.143), channel_id=1, source_target_pairs={{0,4},{8,0},{16,8},{24,16},{28,24},{20,28},{12,20},{4,12},{1,5},{9... | collective-permute-start | bytes 3538952 | tf_op jit(solution)/shard_map/ppermute | solution.py:67
  550.1 35.5 %collective-permute-start.90 = (bf16[2,192,1536]{2,1,0:T(8,128)(2,1)}, bf16[2,192,1536]{2,1,0:T(8,128)(2,1)}, u32[]{:S(2)}, u32[]{:S(2)}) collective-permute-start(bf16[2,192,1536]{2,1,0:T(8,128)(2,1)} %get-tuple-element.142), channel_id=1, source_target_pairs={{0,8},{8,16},{16,24},{24,28},{28,20},{20,12},{12,4},{4,0},{1,9},{9... | collective-permute-start | bytes 3538952 | tf_op jit(solution)/shard_map/ppermute | solution.py:64
  627.2 60.5 %collective-permute-start.58 = (f32[384,1536]{1,0:T(8,128)}, f32[384,1536]{1,0:T(8,128)}, u32[]{:S(2)}, u32[]{:S(2)}) collective-permute-start(f32[384,1536]{1,0:T(8,128)} %fusion.28), channel_id=1, source_target_pairs={{0,1},{1,0},{2,3},{3,2},{4,5},{5,4},{6,7},{7,6},{8,9},{9,8},{10,11... | collective-permute-start | bytes 7077896 | tf_op jit(solution)/shard_map/ppermute | solution.py:182
  648.4 35.3 %collective-permute-start.72 = (bf16[2,192,1152]{2,1,0:T(8,128)(2,1)}, bf16[2,192,1152]{2,1,0:T(8,128)(2,1)}, u32[]{:S(2)}, u32[]{:S(2)}) collective-permute-start(bf16[2,192,1152]{2,1,0:T(8,128)(2,1)} %get-tuple-element.154), channel_id=1, source_target_pairs={{0,8},{8,16},{16,24},{24,28},{28,20},{20,12},{12,4},{4,0},{1,9},{9... | collective-permute-start | bytes 2654216 | tf_op jit(solution)/shard_map/ppermute | solution.py:64
  655.1 28.7 %collective-permute-start.76 = (bf16[2,192,1152]{2,1,0:T(8,128)(2,1)S(1)}, bf16[2,192,1152]{2,1,0:T(8,128)(2,1)}, u32[]{:S(2)}, u32[]{:S(2)}) collective-permute-start(bf16[2,192,1152]{2,1,0:T(8,128)(2,1)S(1)} %get-tuple-element.155), channel_id=1, source_target_pairs={{0,4},{8,0},{16,8},{24,16},{28,24},{20,28},{12,20},{4,12},{1,5},{9... | collective-permute-start | bytes 2654216 | tf_op jit(solution)/shard_map/ppermute | solution.py:67
  659.4 22.1 %collective-permute-start.85 = (bf16[2,192,384]{2,1,0:T(8,128)(2,1)S(1)}, bf16[2,192,384]{2,1,0:T(8,128)(2,1)S(1)}, u32[]{:S(2)}, u32[]{:S(2)}) collective-permute-start(bf16[2,192,384]{2,1,0:T(8,128)(2,1)S(1)} %get-tuple-element.162), channel_id=1, source_target_pairs={{0,4},{8,0},{16,8},{24,16},{28,24},{20,28},{12,20},{4,12},{1,5},{9... | collective-permute-start | bytes 884744 | tf_op jit(solution)/shard_map/ppermute | solution.py:67
  685.6 21.8 %collective-permute-start.73 = (bf16[2,192,1152]{2,1,0:T(8,128)(2,1)S(1)}, bf16[2,192,1152]{2,1,0:T(8,128)(2,1)S(1)}, u32[]{:S(2)}, u32[]{:S(2)}) collective-permute-start(bf16[2,192,1152]{2,1,0:T(8,128)(2,1)S(1)} %get-tuple-element.152), channel_id=1, source_target_pairs={{0,8},{8,16},{16,24},{24,28},{28,20},{20,12},{12,4},{4,0},{1,9},{9... | collective-permute-start | bytes 2654216 | tf_op jit(solution)/shard_map/ppermute | solution.py:64
  686.3 21.2 %collective-permute-start.77 = (bf16[2,192,1152]{2,1,0:T(8,128)(2,1)S(1)}, bf16[2,192,1152]{2,1,0:T(8,128)(2,1)S(1)}, u32[]{:S(2)}, u32[]{:S(2)}) collective-permute-start(bf16[2,192,1152]{2,1,0:T(8,128)(2,1)S(1)} %get-tuple-element.153), channel_id=1, source_target_pairs={{0,4},{8,0},{16,8},{24,16},{28,24},{20,28},{12,20},{4,12},{1,5},{9... | collective-permute-start | bytes 2654216 | tf_op jit(solution)/shard_map/ppermute | solution.py:67
  709.2 29.4 %collective-permute-start.78 = (bf16[2,192,1152]{2,1,0:T(8,128)(2,1)}, bf16[2,192,1152]{2,1,0:T(8,128)(2,1)}, u32[]{:S(2)}, u32[]{:S(2)}) collective-permute-start(bf16[2,192,1152]{2,1,0:T(8,128)(2,1)} %get-tuple-element.151), channel_id=1, source_target_pairs={{0,4},{8,0},{16,8},{24,16},{28,24},{20,28},{12,20},{4,12},{1,5},{9... | collective-permute-start | bytes 2654216 | tf_op jit(solution)/shard_map/ppermute | solution.py:67
  710.5 28.1 %collective-permute-start.74 = (bf16[2,192,1152]{2,1,0:T(8,128)(2,1)}, bf16[2,192,1152]{2,1,0:T(8,128)(2,1)}, u32[]{:S(2)}, u32[]{:S(2)}) collective-permute-start(bf16[2,192,1152]{2,1,0:T(8,128)(2,1)} %get-tuple-element.150), channel_id=1, source_target_pairs={{0,8},{8,16},{16,24},{24,28},{28,20},{20,12},{12,4},{4,0},{1,9},{9... | collective-permute-start | bytes 2654216 | tf_op jit(solution)/shard_map/ppermute | solution.py:64
  (224 other events, 3542.7 us)

commit v2 on v1

--- a/solution.py
+++ b/solution.py
@@ -79,37 +79,73 @@
 
         whole = put(whole, shard, 0)
         forward, backward = (shard, shard)
-        marks = []
         for step in range(1, self.half):
-            forward = self.right(forward)
-            backward = self.left(backward)
-            marks.append((forward, backward))
+            forward, backward = yield (self.right(forward), self.left(backward))
             whole = put(whole, forward, -step)
             whole = put(whole, backward, step)
-        forward = self.right(forward[:, :cut])
-        backward = self.left(backward[:, cut:])
+        forward, backward = yield (self.right(forward[:, :cut]), self.left(backward[:, cut:]))
         whole = put(whole, forward, -self.half)
-        whole = put(whole, backward, self.half, cut)
-        return (whole, marks)
-
-    def scatter(self, whole):
-        streams, all_rows, width = whole.shape
-        rows = all_rows // self.count
+        return put(whole, backward, self.half, cut)
+
+    def scatter(self, wholes):
+        rows = wholes[0][0].shape[0] // self.count
         cut = rows // 2
 
         def block(offset, start=0, size=rows):
-            return lax.dynamic_slice(
-                whole, (0, self.owner(offset) * rows + start, 0), (streams, size, width)
+            at = (self.owner(offset) * rows + start, 0)
+            return jnp.stack(
+                [
+                    jnp.concatenate(
+                        [lax.dynamic_slice(part, at, (size, part.shape[1])) for part in parts],
+                        axis=1,
+                    )
+                    for parts in wholes
+                ]
             )
 
-        forward = self.right(block(self.half, 0, cut))
-        backward = self.left(block(-self.half, cut, rows - cut))
+        forward, backward = yield (
+            self.right(block(self.half, 0, cut)),
+            self.left(block(-self.half, cut, rows - cut)),
+        )
         forward = jnp.pad(forward.astype(F32), ((0, 0), (0, rows - cut), (0, 0)))
         backward = jnp.pad(backward.astype(F32), ((0, 0), (cut, 0), (0, 0)))
         for step in range(self.half - 1, 0, -1):
-            forward = self.right((block(step).astype(F32) + forward).astype(BF16)).astype(F32)
-            backward = self.left((block(-step).astype(F32) + backward).astype(BF16)).astype(F32)
+            forward, backward = yield (
+                self.right((block(step).astype(F32) + forward).astype(BF16)),
+                self.left((block(-step).astype(F32) + backward).astype(BF16)),
+            )
+            forward, backward = (forward.astype(F32), backward.astype(F32))
         return block(0).astype(F32) + forward + backward
+
+
+def fence(pending, values):
+    return lax.optimization_barrier((tuple(pending), tuple(values)))
+
+
+def later(values, mark):
+    values = tuple(values)
+    return lax.optimization_barrier((values, tuple(mark)))[0]
+
+
+class Lane:
+    def __init__(self):
+        self.last = ()
+
+    def add(self, make, source, hooks=None):
+        if self.last:
+            source = lax.optimization_barrier((self.last, source))[1]
+        steps = make(source)
+        received = None
+        marks = []
+        try:
+            while True:
+                received = lax.optimization_barrier(steps.send(received))
+                if hooks and len(marks) in hooks:
+                    received = hooks[len(marks)](received)
+                marks.append(received)
+                self.last = received
+        except StopIteration as end:
+            return (end.value, marks)
 
 
 def flip_pairs(count, bit):
@@ -120,36 +156,37 @@
     return jnp.where(flag == 0, pair[0], pair[1])
 
 
-def small_scatter(value, axis, count):
+def small_scatter(value, axis, count, hold=None):
     index = lax.axis_index(axis)
-    bit = count // 2
-    bits = []
-    width = 1
-    while width < count:
-        bits.append(width)
-        width *= 2
     rest = value
-    for bit in bits:
+    sent = []
+    bit = 1
+    while bit < count:
         pairs = rest.reshape((rest.shape[0] // 2, 2) + rest.shape[1:])
         flag = (index // bit) % 2
         mine = jnp.where(flag == 0, pairs[:, 0], pairs[:, 1])
         other = jnp.where(flag == 0, pairs[:, 1], pairs[:, 0])
+        if hold is not None:
+            other = hold(other, sent)
+        sent.append(other)
         rest = mine + lax.ppermute(other, axis, flip_pairs(count, bit))
+        bit *= 2
     return rest[0]
 
 
+def shift_pairs(count, offset):
+    return [(i, (i + offset) % count) for i in range(count)]
+
+
 def small_gather(value, axis, count):
-    index = lax.axis_index(axis)
-    rest = value[None]
-    bit = 1
-    while bit < count:
-        got = lax.ppermute(rest, axis, flip_pairs(count, bit))
-        flag = (index // bit) % 2
-        rest = jnp.where(
-            flag == 0, jnp.concatenate([rest, got]), jnp.concatenate([got, rest])
-        )
-        bit *= 2
-    return rest
+    return jnp.concatenate(
+        [value]
+        + [lax.ppermute(value, axis, shift_pairs(count, -offset)) for offset in range(1, count)]
+    )
+
+
+def in_order(value, axis):
+    return jnp.roll(value, lax.axis_index(axis), axis=0)
 
 
 def small_sum(value, axis, count):
@@ -161,21 +198,11 @@
 
 
 def small_exchange(value, axis, count):
-    index = lax.axis_index(axis)
-    tail = value.shape[1:]
-    bit = 1
-    rest = value
-    while bit < count:
-        pairs = rest.reshape((count // (2 * bit), 2, bit) + tail)
-        flag = (index // bit) % 2
-        mine = jnp.where(flag == 0, pairs[:, 0], pairs[:, 1])
-        other = jnp.where(flag == 0, pairs[:, 1], pairs[:, 0])
-        got = lax.ppermute(other, axis, flip_pairs(count, bit))
-        rest = jnp.where(
-            flag == 0, jnp.stack([mine, got], axis=1), jnp.stack([got, mine], axis=1)
-        ).reshape((count,) + tail)
-        bit *= 2
-    return rest
+    pieces = [value[:1]] + [
+        lax.ppermute(value[count - offset : count - offset + 1], axis, shift_pairs(count, -offset))
+        for offset in range(1, count)
+    ]
+    return jnp.concatenate(pieces)
 
 
 def swap_core(value):
@@ -184,6 +211,37 @@
 
 def swap_y(value):
     return lax.ppermute(value, "tensor", flip_pairs(4, 2))
+
+
+def assemble_kernel(own, over_y, core, both, first, second):
+    split = first.shape[0] // 4
+    rest = second.shape[0] // 4
+    for i, piece in enumerate((own, over_y, core, both)):
+        first[i * split : (i + 1) * split] = piece[:split]
+        second[i * rest : (i + 1) * rest] = piece[split:]
+
+
+def assemble(pieces, split):
+    rows, width = pieces[0].shape
+    half = width // 2
+
+    def spec(size):
+        return pl.BlockSpec((size, half), lambda i: (0, i))
+
+    return pl.pallas_call(
+        assemble_kernel,
+        grid=(2,),
+        in_specs=[spec(rows)] * 4,
+        out_specs=[spec(4 * split), spec(4 * (rows - split))],
+        out_shape=[
+            jax.ShapeDtypeStruct((4 * split, width), BF16),
+            jax.ShapeDtypeStruct((4 * (rows - split), width), BF16),
+        ],
+        cost_estimate=pl.CostEstimate(
+            flops=0, bytes_accessed=16 * rows * width, transcendentals=0
+        ),
+        compiler_params=pltpu.CompilerParams(vmem_limit_bytes=24 * 2**20),
+    )(*pieces)
 
 
 def gather_rows(first, second):
@@ -192,11 +250,7 @@
     over_y = swap_y(own)
     core = swap_core(own)
     both = swap_core(over_y)
-    pieces = (own, over_y, core, both)
-    return (
-        jnp.concatenate([piece[:split] for piece in pieces]),
-        jnp.concatenate([piece[split:] for piece in pieces]),
-    )
+    return (assemble((own, over_y, core, both), split), own)
 
 
 def reduce_rows(factors, products):
@@ -204,19 +258,13 @@
     for factor, product in zip(factors, products):
         rows = factor.shape[0] // 2
         away.append(product(factor[rows:]))
-    for factor, product in zip(factors, products):
-        rows = factor.shape[0] // 2
         kept.append(product(factor[:rows]))
-    sums = [keep + swap_core(send) for keep, send in zip(kept, away)]
+    sums = [keep + swap_core(piece) for keep, piece in zip(kept, away)]
     quarter = [total.shape[0] // 2 for total in sums]
-    crossing = jnp.concatenate(
-        [total[size:].astype(BF16) for total, size in zip(sums, quarter)]
-    )
+    crossing = jnp.concatenate([total[size:].astype(BF16) for total, size in zip(sums, quarter)])
     got = swap_y(crossing).astype(F32)
-    return [
-        sums[0][: quarter[0]] + got[: quarter[0]],
-        sums[1][: quarter[1]] + got[quarter[0] :],
-    ]
+    size = quarter[0]
+    return ([sums[0][:size] + got[:size], sums[1][:quarter[1]] + got[size:]], crossing)
 
 
 CHUNK = 128
@@ -357,8 +405,8 @@
     )(*([packed_image, packed_text] * 3), grad_image, grad_text, lse)
 
 
-def after(value, *marks):
-    return lax.optimization_barrier((value,) + marks)[0]
+def stack_rows(pair):
+    return jnp.concatenate([pair[0], pair[1]], axis=1)
 
 
 def per_device(
@@ -387,23 +435,36 @@
     row_block = ada_w.shape[2]
     heads_width = qkv_w.shape[4]
 
-    qkv_shard = qkv_w[0].reshape(2, row_block, 3 * heads_width)
-    out_shard = out_w[0].transpose(0, 2, 1)
-    up_shard = up_w[0]
-    down_shard = down_w[0].transpose(0, 2, 1)
-    w_qkv, marks = ring.gather(qkv_shard)
-    w_out, marks = ring.gather(after(out_shard, *marks[-1]))
-    w_up, marks = ring.gather(after(up_shard, *marks[0]))
-    w_down, marks = ring.gather(after(down_shard, *marks[-1]))
-
     cond_full = condition.astype(F32)
     silu_low = jax.nn.silu(cond_full).astype(BF16)
     own_cond = lax.dynamic_slice_in_dim(cond_full, dp_rank, 1, 0)
     own_cols = lax.dynamic_slice_in_dim(silu_low, dp_rank * row_block, row_block, 1)
+    near_cols = jnp.roll(own_cols, -dp_rank, axis=0)
     mod_terms = jnp.einsum("sr,krc->skc", own_cols, ada_w[0], preferred_element_type=F32)
-    mod_local = small_scatter(mod_terms, "dp", count) + ada_b[0].astype(F32)
-    mod_full = small_gather(mod_local, "tensor", members)
+    lane = Lane()
+    weights = []
+    qkv_shard = qkv_w[0].reshape(2, row_block, 3 * heads_width)
+    attn_shard = jnp.concatenate([qkv_shard, out_w[0].transpose(0, 2, 1)], axis=2)
+
+    def hold(operand, sent):
+        if len(sent) == 1:
+            weights.append(lane.add(ring.gather, later((attn_shard,), sent)[0]))
+        elif len(sent) == 2:
+            operand = later((operand,), weights[0][1][0])[0]
+        return operand
+
+    mod_local = small_scatter(mod_terms, "dp", count, hold)
+    mod_local = mod_local + ada_b[0].astype(F32)
+    mod_full = in_order(small_gather(mod_local[None], "tensor", members), "tensor")
     mods = mod_full.transpose(1, 0, 2).reshape(2, 6, 1, width)
+
+    up_shard = up_w[0]
+    down_shard = down_w[0].transpose(0, 2, 1)
+    w_both = weights[0][0]
+    w_qkv = w_both[:, :, : 3 * heads_width]
+    w_out = w_both[:, :, 3 * heads_width :]
+    w_up, up_marks = lane.add(ring.gather, up_shard)
+    w_down, down_marks = lane.add(ring.gather, down_shard)
 
     biases_out = out_b[0].astype(F32)
     biases_down = down_b[0].astype(F32)
@@ -417,7 +478,14 @@
         normed_one.append(normed)
         inv_one.append(inv_std)
         lowered.append((normed * (1.0 + mods[s, 1]) + mods[s, 0]).astype(BF16))
-    full_one = gather_rows(*lowered)
+    full_one, _ = gather_rows(*lowered)
+    gradients = [image_cot[0].astype(F32), text_cot[0].astype(F32)]
+    scaled = [mods[s, 5] * gradients[s] for s in both]
+    down_bias_grad = [jnp.sum(scaled[s], axis=0, keepdims=True) for s in both]
+    scaled = [value.astype(BF16) for value in scaled]
+    scaled = later(scaled, full_one)
+    dy_full, _ = gather_rows(*scaled)
+
     packed = []
     for s in both:
         bias = jnp.concatenate(
@@ -426,7 +494,8 @@
         packed.append((mm(full_one[s], w_qkv[s]) + bias).astype(BF16))
     attn_image, attn_text, lse = attend(*packed)
     attn = (attn_image, attn_text)
-    attn_sums = reduce_rows(attn, [lambda rows, s=s: mm_nt(rows, w_out[s]) for s in both])
+    attn_rows = later(attn, up_marks[0])
+    attn_sums, _ = reduce_rows(attn_rows, [lambda rows, s=s: mm_nt(rows, w_out[s]) for s in both])
     attn_bias, residuals, normed_two, inv_two, lowered = ([], [], [], [], [])
     for s in both:
         attn_bias.append(attn_sums[s] + biases_out[s])
@@ -435,101 +504,113 @@
         normed_two.append(normed)
         inv_two.append(inv_std)
         lowered.append((normed * (1.0 + mods[s, 4]) + mods[s, 3]).astype(BF16))
-    full_two = gather_rows(*lowered)
-
-    gradients = [image_cot[0].astype(F32), text_cot[0].astype(F32)]
-    scaled = [mods[s, 5] * gradients[s] for s in both]
-    down_bias_grad = [jnp.sum(scaled[s], axis=0) for s in both]
-    dy_full = gather_rows(*[value.astype(BF16) for value in scaled])
+    full_two, _ = gather_rows(*later(lowered, up_marks[1]))
+
     pre_acts, acts, down_w_grad = ([], [], [])
     for s in both:
         pre_acts.append(mm(full_two[s], w_up[s]) + biases_up[s])
         acts.append(gelu_tanh(pre_acts[s]).astype(BF16))
-    for s in both:
         down_w_grad.append(mm_tn(dy_full[s], acts[s]).astype(BF16))
-    down_grad = ring.scatter(jnp.stack(down_w_grad))
-
-    up_w_grad, up_b_grad, pre_grads = ([], [], [])
-    for s in both:
+    down_grad, marks = lane.add(ring.scatter, [(grad,) for grad in down_w_grad])
+    up_b_grad, pre_grads = ([None, None], [None, None])
+    for s in (1, 0):
         act_grad = mm(dy_full[s], w_down[s])
         gelu_back = jax.vjp(gelu_tanh, pre_acts[s])[1]
-        pre_grad = gelu_back(act_grad)[0].astype(BF16)
-        pre_grads.append(pre_grad)
-        up_b_grad.append(jnp.sum(pre_grad, axis=0, dtype=F32))
-    hidden_two = reduce_rows(pre_grads, [lambda rows, s=s: mm_nt(rows, w_up[s]) for s in both])
-    for s in both:
-        up_w_grad.append(mm_tn(full_two[s], pre_grads[s]).astype(BF16))
-    up_grad = ring.scatter(jnp.stack(up_w_grad))
-
-    mlp_sums = reduce_rows(acts, [lambda rows, s=s: mm_nt(rows, w_down[s]) for s in both])
+        pre_grads[s] = gelu_back(act_grad)[0].astype(BF16)
+        up_b_grad[s] = jnp.sum(pre_grads[s], axis=0, dtype=F32)
+    hidden_two, cross_two = reduce_rows(
+        later(pre_grads, marks[0]), [lambda rows, s=s: mm_nt(rows, w_up[s]) for s in both]
+    )
+    late_grads = later(pre_grads, (cross_two,))
+    up_w_grad = [mm_tn(full_two[s], late_grads[s]).astype(BF16) for s in both]
+    up_grad, up_marks = lane.add(ring.scatter, [(grad,) for grad in up_w_grad])
+    hidden_two = later(hidden_two, marks[1])
+
+    shift_two_grad, scale_two_grad, mid_grads = ([], [], [])
+    gate_one_grad, out_bias_grad, dz_lows = ([], [], [])
+    for s in both:
+        shift_two_grad.append(jnp.sum(hidden_two[s], axis=0, keepdims=True))
+        scale_two_grad.append(jnp.sum(hidden_two[s] * normed_two[s], axis=0, keepdims=True))
+        upstream = hidden_two[s] * (1.0 + mods[s, 4])
+        mid_grads.append(gradients[s] + norm_back(upstream, normed_two[s], inv_two[s]))
+        gate_one_grad.append(jnp.sum(mid_grads[s] * attn_bias[s], axis=0, keepdims=True))
+        scaled = mods[s, 2] * mid_grads[s]
+        out_bias_grad.append(jnp.sum(scaled, axis=0, keepdims=True))
+        dz_lows.append(scaled.astype(BF16))
+    dz_full, dz_sent = gather_rows(*dz_lows)
+    dz_rows = later(dz_full, marks[2])
+    attn_grads = [mm(dz_rows[s], w_out[s]).astype(BF16) for s in both]
+    packed_grad = attend_back(*packed, *attn_grads, lse)
+    hidden_one, cross_one = reduce_rows(
+        later(packed_grad, marks[3]), [lambda rows, s=s: mm_nt(rows, w_qkv[s]) for s in both]
+    )
+    late_grads = later(later(packed_grad, (cross_one,)), up_marks[0])
+    qkv_w_grad, qv_b_grad = ([], [])
+    for s in both:
+        qkv_w_grad.append(mm_tn(full_one[s], late_grads[s]).astype(BF16))
+        summed = jnp.sum(late_grads[s], axis=0, dtype=F32).reshape(3, heads_width)
+        qv_b_grad.append(jnp.stack([summed[0], summed[2]]))
+    late_dz = later(dz_full, up_marks[0])
+    out_w_grad = [mm_tn(late_dz[s], attn[s]).astype(BF16) for s in both]
+    shift_one_grad, scale_one_grad, new_grads = ([], [], [])
+    for s in both:
+        shift_one_grad.append(jnp.sum(hidden_one[s], axis=0, keepdims=True))
+        scale_one_grad.append(jnp.sum(hidden_one[s] * normed_one[s], axis=0, keepdims=True))
+        upstream = hidden_one[s] * (1.0 + mods[s, 1])
+        new_grads.append(mid_grads[s] + norm_back(upstream, normed_one[s], inv_one[s]))
+
+    late_acts = later(acts, (dz_sent,))
+    mlp_sums, cross_out = reduce_rows(
+        late_acts, [lambda rows, s=s: mm_nt(rows, w_down[s]) for s in both]
+    )
     outputs, gate_two_grad = ([], [])
     for s in both:
         mlp_bias = mlp_sums[s] + biases_down[s]
         outputs.append((residuals[s] + mods[s, 5] * mlp_bias).astype(BF16))
-        gate_two_grad.append(jnp.sum(gradients[s] * mlp_bias, axis=0))
-
-    shift_two_grad, scale_two_grad, mid_grads = ([], [], [])
-    gate_one_grad, out_bias_grad, dz_lows = ([], [], [])
-    for s in both:
-        shift_two_grad.append(jnp.sum(hidden_two[s], axis=0))
-        scale_two_grad.append(jnp.sum(hidden_two[s] * normed_two[s], axis=0))
-        upstream = hidden_two[s] * (1.0 + mods[s, 4])
-        mid_grads.append(gradients[s] + norm_back(upstream, normed_two[s], inv_two[s]))
-        gate_one_grad.append(jnp.sum(mid_grads[s] * attn_bias[s], axis=0))
-        scaled = mods[s, 2] * mid_grads[s]
-        out_bias_grad.append(jnp.sum(scaled, axis=0))
-        dz_lows.append(scaled.astype(BF16))
-    dz_full = gather_rows(*dz_lows)
-    attn_grads = [mm(dz_full[s], w_out[s]).astype(BF16) for s in both]
-    out_w_grad = [mm_tn(dz_full[s], attn[s]).astype(BF16) for s in both]
-    out_grad = ring.scatter(jnp.stack(out_w_grad))
-
-    packed_grad = attend_back(*packed, *attn_grads, lse)
-    hidden_one = reduce_rows(packed_grad, [lambda rows, s=s: mm_nt(rows, w_qkv[s]) for s in both])
-    qkv_w_grad, qv_b_grad = ([], [])
-    for s in both:
-        qkv_w_grad.append(mm_tn(full_one[s], packed_grad[s]).astype(BF16))
-        summed = jnp.sum(packed_grad[s], axis=0, dtype=F32).reshape(3, heads_width)
-        qv_b_grad.append(jnp.stack([summed[0], summed[2]]))
-    qkv_grad = ring.scatter(jnp.stack(qkv_w_grad))
-    shift_one_grad, scale_one_grad, new_grads = ([], [], [])
-    for s in both:
-        shift_one_grad.append(jnp.sum(hidden_one[s], axis=0))
-        scale_one_grad.append(jnp.sum(hidden_one[s] * normed_one[s], axis=0))
-        upstream = hidden_one[s] * (1.0 + mods[s, 1])
-        new_grads.append(mid_grads[s] + norm_back(upstream, normed_one[s], inv_one[s]))
-
-    mod_grad = jnp.stack(
-        [
-            jnp.concatenate(
-                [
-                    shift_one_grad[s],
-                    scale_one_grad[s],
-                    gate_one_grad[s],
-                    shift_two_grad[s],
-                    scale_two_grad[s],
-                    gate_two_grad[s],
-                ]
-            )
-            for s in both
+        gate_two_grad.append(jnp.sum(gradients[s] * mlp_bias, axis=0, keepdims=True))
+
+    rows = []
+    for s in both:
+        rows += [
+            shift_one_grad[s],
+            scale_one_grad[s],
+            gate_one_grad[s],
+            shift_two_grad[s],
+            scale_two_grad[s],
+            gate_two_grad[s],
         ]
-    )
-    bias_grad = jnp.stack(out_bias_grad + down_bias_grad)
-    mod_cols = mod_grad.shape[1] // members
+    rows = later(rows + out_bias_grad + down_bias_grad, up_marks[3])
+    total = small_sum(jnp.concatenate(rows), "tensor", members)
+    mod_cols = 6 * width // members
     bias_cols = width // members
-    by_member = jnp.concatenate(
-        [
-            mod_grad.reshape(2, members, mod_cols).transpose(1, 0, 2).reshape(members, -1),
-            bias_grad.reshape(4, members, bias_cols).transpose(1, 0, 2).reshape(members, -1),
-        ],
-        axis=1,
-    )
-    own_part = small_scatter(by_member, "tensor", members)
-    mod_part = own_part[: 2 * mod_cols].astype(BF16).astype(F32)
-    qv_part = jnp.stack(qv_b_grad).reshape(-1)
-    up_part = jnp.stack(up_b_grad).reshape(-1)
-    message = jnp.concatenate([mod_part, own_part[2 * mod_cols :], qv_part, up_part])
-    every = small_gather(message, "dp", count)
+    tensor_rank = lax.axis_index("tensor")
+    mod_part = lax.dynamic_slice_in_dim(
+        total[:12].reshape(2, 6 * width), tensor_rank * mod_cols, mod_cols, 1
+    )
+    mod_part = mod_part.astype(BF16).astype(F32).reshape(-1)
+    bias_part = lax.dynamic_slice_in_dim(total[12:], tensor_rank * bias_cols, bias_cols, 1)
+    qv_part = jnp.concatenate(qv_b_grad).reshape(-1)
+    up_part = jnp.concatenate(up_b_grad)
+    message = jnp.concatenate([mod_part, bias_part.reshape(-1), qv_part, up_part])[None]
+    kept = {}
+
+    def after_second(received):
+        kept["every"] = small_gather(later((message,), received)[0], "dp", count)
+        return received
+
+    def after_third(received):
+        every_low = kept["every"][:, : 2 * mod_cols].reshape(count, 2, mod_cols).astype(BF16)
+        cond_terms = jnp.einsum("skc,krc->sr", every_low, ada_w[0], preferred_element_type=F32)
+        cond_terms = small_sum(cond_terms, "tensor", members)
+        kept["cond"] = small_exchange(cond_terms, "dp", count)
+        return later(received, (cond_terms,))
+
+    attn_grad, _ = lane.add(
+        ring.scatter, list(zip(qkv_w_grad, out_w_grad)), {1: after_second, 2: after_third}
+    )
+    qkv_grad = attn_grad[:, :, : 3 * heads_width]
+    out_grad = attn_grad[:, :, 3 * heads_width :]
+    every = kept["every"]
     every_mod = every[:, : 2 * mod_cols].reshape(count, 2, mod_cols)
     every_low = every_mod.astype(BF16)
     summed = jnp.sum(every, axis=0)
@@ -546,9 +627,8 @@
     qv_sum = own_piece(summed[ends[1] : ends[2]].reshape(2, 2, heads_width))
     up_sum = own_piece(summed[ends[2] : ends[3]].reshape(2, -1))
 
-    ada_w_grad = jnp.einsum("sr,skc->krc", own_cols, every_low, preferred_element_type=F32)
-    cond_terms = jnp.einsum("skc,krc->sr", every_low, ada_w[0], preferred_element_type=F32)
-    cond_sum = small_exchange(small_sum(cond_terms, "tensor", members), "dp", count).reshape(1, width)
+    ada_w_grad = jnp.einsum("sr,skc->krc", near_cols, every_low, preferred_element_type=F32)
+    cond_sum = in_order(kept["cond"], "dp").reshape(1, width)
     sigmoid = jax.nn.sigmoid(own_cond)
     cond_grad = cond_sum * sigmoid * (1.0 + own_cond * (1.0 - sigmoid))
     return (

time: 778 us -> 688 us (0.88)
  waiting for transfers between devices: 387 us -> 234 us
  local copies, waits for them, and re-layouts: 79.3 us -> 117 us
  other arithmetic: 60 us -> 80 us
    ppermute x32 -> x24, waiting for transfers between devices: 222 us -> 147 us  [right(): return lax.ppermute(value, 'dp', self.right_pairs)]
    ppermute x32 -> x24, waiting for transfers between devices: 84.4 us -> 18.2 us  [left(): return lax.ppermute(value, 'dp', self.left_pairs)]
    slice x34 -> x11, local copies, waits for them, and re-layouts: 21.8 us -> 2.51 us  [the longest x1 0.89 us: after_third(): kept['every'][:, :2 * mod_cols].reshape(count, 2, mod_cols).astype(BF16)]
    ppermute x8 -> x17, starting transfers between devices: 9.76 us -> 25.5 us  [the longest x7 13.8 us: small_exchange(): lax.ppermute(value[count - offset:count - offset + 1], axis, shift_pairs(...]
    ppermute x5 -> x3, waiting for transfers between devices: 24.9 us -> 9.91 us  [small_scatter(): rest = mine + lax.ppermute(other, axis, flip_pairs(count, bit))]
    convert_element_type x3 -> x11, other arithmetic: 0.17 us -> 13.6 us  [the longest x9 13.5 us: scatter(): (block(-step).astype(F32) + backward).astype(BF16)]
    another operation x9 -> x10, local copies, waits for them, and re-layouts: 2.46 us -> 15 us
    unnamed x352 -> x388, local copies, waits for them, and re-layouts: 11.1 us -> 22.4 us
  transfers between devices with their start and end apart: 103 -> 96, of which waited for: 47 -> 47; matrix products, arithmetic and copies ran while one was open for 28% -> 40% of each run, Pallas kernels for 1% -> 4%
where the time goes in v2:
time: 688 us; the launch traced here: 679 us
  waiting for transfers between devices  234 us (34%)
  local copies, waits for them, and re-layouts  117 us (17%)
  matrix products  115 us (17%)
  starting transfers between devices  101 us (15%)
  other arithmetic  80 us (12%)
  Pallas kernels  28.5 us (4%)
    ppermute x24, waiting for transfers between devices, right(): return lax.ppermute(value, 'dp', self.right_pairs)  147 us
    dot_general x32, matrix products, dot(): lax.dot_general(left, right, (dims, ((), ())), preferred_element_type=F32)  112 us
    ppermute x8, waiting for transfers between devices, swap_y(): return lax.ppermute(value, 'tensor', flip_pairs(4, 2))  34.2 us
    dynamic_update_slice x27, local copies, waits for them, and re-layouts, put(): lax.dynamic_update_slice(whole, piece, (0, self.owner(offset) * rows + st...  33.9 us
    ppermute x24, starting transfers between devices, left(): return lax.ppermute(value, 'dp', self.left_pairs)  30.1 us
    unnamed x388, local copies, waits for them, and re-layouts  22.4 us
    ppermute x24, starting transfers between devices, right(): return lax.ppermute(value, 'dp', self.right_pairs)  21.5 us
    ppermute x24, waiting for transfers between devices, left(): return lax.ppermute(value, 'dp', self.left_pairs)  18.2 us
  transfers between devices with their start and end apart: 96, of which 47 were waited for; matrix products, arithmetic and copies ran while one was open for 40% of the time, Pallas kernels for 4%

profile of v2, /device:TPU:0, one launch (start us, length us, event | category | flops | bytes accessed | tf_op | source)
XLA Modules:
  0.0 679.4 jit_solution(11383269892315449197)
XLA Ops:
  16.6 4.1 broadcast.255.clone.1
  30.0 9.9 %collective-permute-done.1 = f32[2,2,2304]{2,1,0:T(2,128)} collective-permute-done((f32[2,2,2304]{2,1,0:T(2,128)}, f32[2,2,2304]{2,1,0:T(2,128)}, u32[]{:S(2)}, u32[]{:S(2)}) %collective-permute-start.1) | collective-permute-done | bytes 36896 | tf_op jit(solution)/shard_map/ppermute | solution.py:172
  60.2 12.9 %collective-permute-done.8.over_y = bf16[224,1536]{1,0:T(8,128)(2,1)S(1)} collective-permute-done((bf16[224,1536]{1,0:T(8,128)(2,1)S(1)}, bf16[224,1536]{1,0:T(8,128)(2,1)S(1)}, u32[]{:S(2)}, u32[]{:S(2)}) %collective-permute-start.8) | collective-permute-done | bytes 688160 | tf_op jit(solution)/shard_map/ppermute | solution.py:213
  80.7 21.0 %collective-permute-done.13 = bf16[2,192,1536]{2,1,0:T(8,128)(2,1)S(1)} collective-permute-done((bf16[2,192,1536]{2,1,0:T(8,128)(2,1)}, bf16[2,192,1536]{2,1,0:T(8,128)(2,1)S(1)}, u32[]{:S(2)}, u32[]{:S(2)}) %collective-permute-start.13) | collective-permute-done | bytes 1179680 | tf_op jit(solution)/shard_map/ppermute | solution.py:64
  108.3 9.0 %collective-permute-done.15 = bf16[2,96,1536]{2,1,0:T(8,128)(2,1)S(1)} collective-permute-done((bf16[2,96,1536]{2,1,0:T(8,128)(2,1)S(1)}, bf16[2,96,1536]{2,1,0:T(8,128)(2,1)S(1)}, u32[]{:S(2)}, u32[]{:S(2)}) %collective-permute-start.15) | collective-permute-done | bytes 589856 | tf_op jit(solution)/shard_map/ppermute | solution.py:64
  125.1 5.3 fusion.19.qi.ki.vi
  130.5 8.7 %shard_map.263 = (bf16[768,384]{1,0:T(8,128)(2,1)S(1)}, bf16[128,384]{1,0:T(8,128)(2,1)S(1)}, f32[3,2,896]{2,1,0:T(2,128)S(1)}) custom-call(bf16[768,1152]{1,0:T(8,128)(2,1)S(1)} %fusion.19.qi.ki.vi, bf16[128,1152]{1,0:T(8,128)(2,1)S(1)} %fusion.28.qt.kt.vt, bf16[768,1152]{1,0:T(8,128)(2,1)S(1)} %fusion.19.qi.ki.vi, bf16[128,1152]{1,0:T(8,128)(2,1)S(1)} %fusion.28.qt.kt.vt, ...), custom_call_target="tpu_custom_call" | custom-call | flops 4932501504 | bytes 3096576 | tf_op jit(solution)/shard_map/pallas_call | solution.py:310
  139.3 5.3 collective-permute-done.17
  147.4 3.5 fusion.65
  152.2 3.9 collective-permute-done.32.core
  158.7 12.6 %collective-permute-done.22 = bf16[2,192,1536]{2,1,0:T(8,128)(2,1)} collective-permute-done((bf16[2,192,1536]{2,1,0:T(8,128)(2,1)}, bf16[2,192,1536]{2,1,0:T(8,128)(2,1)}, u32[]{:S(2)}, u32[]{:S(2)}) %collective-permute-start.22) | collective-permute-done | bytes 1179680 | tf_op jit(solution)/shard_map/ppermute | solution.py:64
  173.7 4.3 broadcast.255.clone.2
  187.6 10.0 %collective-permute-done.27 = bf16[2,192,1536]{2,1,0:T(8,128)(2,1)S(1)} collective-permute-done((bf16[2,192,1536]{2,1,0:T(8,128)(2,1)}, bf16[2,192,1536]{2,1,0:T(8,128)(2,1)S(1)}, u32[]{:S(2)}, u32[]{:S(2)}) %collective-permute-start.27) | collective-permute-done | bytes 1179680 | tf_op jit(solution)/shard_map/ppermute | solution.py:64
  213.3 3.7 collective-permute-done.21
  224.9 5.3 collective-permute-done.24.over_y
  239.1 3.7 copy-done.29
  243.4 4.2 multiply_convert_fusion.2
  247.7 8.5 %multiply_convert_fusion = (bf16[768,1536]{1,0:T(8,128)(2,1)S(1)}, f32[768,1536]{1,0:T(8,128)}) fusion(f32[1536]{0:T(1024)S(1)} %copy-done.159, bf16[768,1536]{1,0:T(8,128)(2,1)S(1)} %get-tuple-element.154, bf16[2,1536,1536]{2,1,0:T(8,128)(2,1)} %constant_dynamic-update-slice_fusion.22), kind=kOutput, calls=%fused_computation.20 | convolution fusion | flops 3635675136 | bytes 14161920 | tf_op jit(solution)/shard_map/dot_general | solution.py:31
  256.2 4.2 collective-permute-done.36
  264.0 4.2 convolution_convert_fusion.3
  268.4 18.2 %collective-permute-done.38 = bf16[2,192,1536]{2,1,0:T(8,128)(2,1)S(1)} collective-permute-done((bf16[2,192,1536]{2,1,0:T(8,128)(2,1)S(1)}, bf16[2,192,1536]{2,1,0:T(8,128)(2,1)S(1)}, u32[]{:S(2)}, u32[]{:S(2)}) %collective-permute-start.38) | collective-permute-done | bytes 1179680 | tf_op jit(solution)/shard_map/ppermute | solution.py:64
  289.2 9.0 %collective-permute-done.40 = bf16[2,96,1536]{2,1,0:T(8,128)(2,1)S(1)} collective-permute-done((bf16[2,96,1536]{2,1,0:T(8,128)(2,1)S(1)}, bf16[2,96,1536]{2,1,0:T(8,128)(2,1)S(1)}, u32[]{:S(2)}, u32[]{:S(2)}) %collective-permute-start.40) | collective-permute-done | bytes 589856 | tf_op jit(solution)/shard_map/ppermute | solution.py:64
  303.8 7.5 %convert_reduce_fusion = (f32[1536]{0:T(1024)}, bf16[768,1536]{1,0:T(8,128)(2,1)S(1)}) fusion(f32[768,1536]{1,0:T(8,128)S(1)} %bitcast.380, f32[1536]{0:T(1024)S(1)} %copy-done.159, bf16[768,1536]{1,0:T(8,128)(2,1)S(1)} %get-tuple-element.162, bf16[2,1536,1536]{2,1,0:T(8,128)(2,1)S(1)} %constant_dynamic-update-slice_fusion.13), kind=kOutput, calls=%fused_computation.19 | convolution fusion | flops 3651009024 | bytes 14170112 | tf_op jit(solution)/shard_map/dot_general | solution.py:31
  314.8 5.9 fusion.7
  325.2 4.6 fusion.10
  332.5 4.1 fusion.31
  336.6 14.0 %collective-permute-done.47 = bf16[2,192,1536]{2,1,0:T(8,128)(2,1)} collective-permute-done((bf16[2,192,1536]{2,1,0:T(8,128)(2,1)}, bf16[2,192,1536]{2,1,0:T(8,128)(2,1)}, u32[]{:S(2)}, u32[]{:S(2)}) %collective-permute-start.47) | collective-permute-done | bytes 1179680 | tf_op jit(solution)/shard_map/ppermute | solution.py:64
  357.7 5.2 fusion.21
  366.1 4.2 convolution_convert_fusion.2
  370.3 10.6 %collective-permute-done.55 = bf16[2,192,1536]{2,1,0:T(8,128)(2,1)S(1)} collective-permute-done((bf16[2,192,1536]{2,1,0:T(8,128)(2,1)S(1)}, bf16[2,192,1536]{2,1,0:T(8,128)(2,1)S(1)}, u32[]{:S(2)}, u32[]{:S(2)}) %collective-permute-start.55) | collective-permute-done | bytes 1179680 | tf_op jit(solution)/shard_map/ppermute | solution.py:64
  380.9 3.1 collective-permute-done.56
  398.8 3.4 fusion.13
  405.2 5.4 collective-permute-done.57
  420.8 3.9 collective-permute-done.62
  435.7 16.4 %shard_map.267 = (bf16[768,1152]{1,0:T(8,128)(2,1)S(1)}, bf16[128,1152]{1,0:T(8,128)(2,1)S(1)}) custom-call(bf16[768,1152]{1,0:T(8,128)(2,1)S(1)} %copy-done.14, bf16[128,1152]{1,0:T(8,128)(2,1)S(1)} %copy-done.12, bf16[768,1152]{1,0:T(8,128)(2,1)S(1)} %copy-done.14, bf16[128,1152]{1,0:T(8,128)(2,1)S(1)} %copy-done.12, bf16[768,1152]{1,0:T(8,128)(2,1)S(1)} %copy-done.14, ...), custom_call_target="tpu_custom_call" | custom-call | flops 12331253760 | bytes 5160960 | tf_op jit(solution)/shard_map/pallas_call | solution.py:381
  452.2 3.3 fusion.23
  455.7 3.9 fusion.22
  465.3 3.7 fusion.20
  474.9 3.3 fusion.29
  478.9 7.3 %collective-permute-done.51 = bf16[224,1536]{1,0:T(8,128)(2,1)S(1)} collective-permute-done((bf16[224,1536]{1,0:T(8,128)(2,1)S(1)}, bf16[224,1536]{1,0:T(8,128)(2,1)S(1)}, u32[]{:S(2)}, u32[]{:S(2)}) %collective-permute-start.51) | collective-permute-done | bytes 688160 | tf_op jit(solution)/shard_map/ppermute | solution.py:213
  496.9 3.7 convolution_add_fusion.2
  507.9 5.1 convolution_convert_fusion.1
  513.1 4.9 collective-permute-done.61
  546.1 3.5 add_bitcast_fusion.1
  574.4 9.2 %collective-permute-done.74 = bf16[2,192,1536]{2,1,0:T(8,128)(2,1)} collective-permute-done((bf16[2,192,1536]{2,1,0:T(8,128)(2,1)}, bf16[2,192,1536]{2,1,0:T(8,128)(2,1)}, u32[]{:S(2)}, u32[]{:S(2)}) %collective-permute-start.74) | collective-permute-done | bytes 1179680 | tf_op jit(solution)/shard_map/ppermute | solution.py:64
  617.3 9.0 %collective-permute-done.92 = bf16[2,192,1536]{2,1,0:T(8,128)(2,1)} collective-permute-done((bf16[2,192,1536]{2,1,0:T(8,128)(2,1)}, bf16[2,192,1536]{2,1,0:T(8,128)(2,1)}, u32[]{:S(2)}, u32[]{:S(2)}) %collective-permute-start.92) | collective-permute-done | bytes 1179680 | tf_op jit(solution)/shard_map/ppermute | solution.py:64
  642.2 11.8 %collective-permute-done.85 = f32[1,192]{1,0:T(1,128)S(1)} collective-permute-done((f32[1,192]{1,0:T(1,128)S(1)}, f32[1,192]{1,0:T(1,128)S(1)}, u32[]{:S(2)}, u32[]{:S(2)}) %collective-permute-start.85) | collective-permute-done | bytes 800 | tf_op jit(solution)/shard_map/ppermute | solution.py:202
  654.1 3.5 collective-permute-start.88
  (825 shorter events, 343.1 us)
Async XLA Ops:
  3.2 19.1 %collective-permute-start = (f32[4,2,2304]{2,0,1:T(4,128)}, f32[4,2,2304]{2,0,1:T(4,128)}, u32[]{:S(2)}, u32[]{:S(2)}) collective-permute-start(f32[4,2,2304]{2,0,1:T(4,128)} %select_bitcast_fusion), channel_id=1, source_target_pairs={{0,4},{4,0},{8,12},{12,8},{16,20},{20,16},{24,28},{28,24},{1,5},{5... | collective-permute-start | bytes 221192 | tf_op jit(solution)/shard_map/ppermute | solution.py:172
  10.2 31.2 %collective-permute-start.2 = (bf16[2,192,1536]{2,1,0:T(8,128)(2,1)S(1)}, bf16[2,192,1536]{2,1,0:T(8,128)(2,1)}, u32[]{:S(2)}, u32[]{:S(2)}) collective-permute-start(bf16[2,192,1536]{2,1,0:T(8,128)(2,1)S(1)} %pad_maximum_fusion), channel_id=1, source_target_pairs={{0,8},{8,16},{16,24},{24,28},{28,20},{20,12},{12,4},{4,0},{1,9},{9... | collective-permute-start | bytes 3538952 | tf_op jit(solution)/shard_map/ppermute | solution.py:64
  11.9 29.5 %collective-permute-start.3 = (bf16[2,192,1536]{2,1,0:T(8,128)(2,1)S(1)}, bf16[2,192,1536]{2,1,0:T(8,128)(2,1)}, u32[]{:S(2)}, u32[]{:S(2)}) collective-permute-start(bf16[2,192,1536]{2,1,0:T(8,128)(2,1)S(1)} %pad_maximum_fusion), channel_id=1, source_target_pairs={{0,4},{8,0},{16,8},{24,16},{28,24},{20,28},{12,20},{4,12},{1,5},{9... | collective-permute-start | bytes 3538952 | tf_op jit(solution)/shard_map/ppermute | solution.py:67
  45.0 28.1 %collective-permute-start.11 = (bf16[2,192,1536]{2,1,0:T(8,128)(2,1)}, bf16[2,192,1536]{2,1,0:T(8,128)(2,1)}, u32[]{:S(2)}, u32[]{:S(2)}) collective-permute-start(bf16[2,192,1536]{2,1,0:T(8,128)(2,1)} %collective-permute-done.2), channel_id=1, source_target_pairs={{0,8},{8,16},{16,24},{24,28},{28,20},{20,12},{12,4},{4,0},{1,9},{9... | collective-permute-start | bytes 3538952 | tf_op jit(solution)/shard_map/ppermute | solution.py:64
  45.3 27.8 %collective-permute-start.12 = (bf16[2,192,1536]{2,1,0:T(8,128)(2,1)}, bf16[2,192,1536]{2,1,0:T(8,128)(2,1)}, u32[]{:S(2)}, u32[]{:S(2)}) collective-permute-start(bf16[2,192,1536]{2,1,0:T(8,128)(2,1)} %collective-permute-done.3), channel_id=1, source_target_pairs={{0,4},{8,0},{16,8},{24,16},{28,24},{20,28},{12,20},{4,12},{1,5},{9... | collective-permute-start | bytes 3538952 | tf_op jit(solution)/shard_map/ppermute | solution.py:67
  60.1 20.0 %collective-permute-start.9 = (bf16[224,1536]{1,0:T(8,128)(2,1)S(1)}, bf16[224,1536]{1,0:T(8,128)(2,1)S(1)}, u32[]{:S(2)}, u32[]{:S(2)}) collective-permute-start(bf16[224,1536]{1,0:T(8,128)(2,1)S(1)} %pad_maximum_fusion.1.own), channel_id=1, source_target_pairs={{0,1},{1,0},{2,3},{3,2},{4,5},{5,4},{6,7},{7,6},{8,9},{9,8},{10,11... | collective-permute-start | bytes 2064392 | tf_op jit(solution)/shard_map/ppermute | solution.py:209
  73.1 28.6 %collective-permute-start.13 = (bf16[2,192,1536]{2,1,0:T(8,128)(2,1)}, bf16[2,192,1536]{2,1,0:T(8,128)(2,1)S(1)}, u32[]{:S(2)}, u32[]{:S(2)}) collective-permute-start(bf16[2,192,1536]{2,1,0:T(8,128)(2,1)} %collective-permute-done.11), channel_id=1, source_target_pairs={{0,8},{8,16},{16,24},{24,28},{28,20},{20,12},{12,4},{4,0},{1,9},{9... | collective-permute-start | bytes 3538952 | tf_op jit(solution)/shard_map/ppermute | solution.py:64
  73.4 28.8 %collective-permute-start.14 = (bf16[2,192,1536]{2,1,0:T(8,128)(2,1)}, bf16[2,192,1536]{2,1,0:T(8,128)(2,1)S(1)}, u32[]{:S(2)}, u32[]{:S(2)}) collective-permute-start(bf16[2,192,1536]{2,1,0:T(8,128)(2,1)} %collective-permute-done.12), channel_id=1, source_target_pairs={{0,4},{8,0},{16,8},{24,16},{28,24},{20,28},{12,20},{4,12},{1,5},{9... | collective-permute-start | bytes 3538952 | tf_op jit(solution)/shard_map/ppermute | solution.py:67
  104.5 46.9 %collective-permute-start.31 = (bf16[224,1536]{1,0:T(8,128)(2,1)S(1)}, bf16[224,1536]{1,0:T(8,128)(2,1)S(1)}, u32[]{:S(2)}, u32[]{:S(2)}) collective-permute-start(bf16[224,1536]{1,0:T(8,128)(2,1)S(1)} %constant_dynamic-update-slice_fusion.10.own), channel_id=1, source_target_pairs={{0,2},{1,3},{2,0},{3,1},{4,6},{5,7},{6,4},{7,5},{8,10},{9,11},{10,... | collective-permute-start | bytes 2064392 | tf_op jit(solution)/shard_map/ppermute | solution.py:213
  118.5 26.1 %collective-permute-start.17 = (bf16[2,192,1536]{2,1,0:T(8,128)(2,1)S(1)}, bf16[2,192,1536]{2,1,0:T(8,128)(2,1)}, u32[]{:S(2)}, u32[]{:S(2)}) collective-permute-start(bf16[2,192,1536]{2,1,0:T(8,128)(2,1)S(1)} %bitcast.372), channel_id=1, source_target_pairs={{0,8},{8,16},{16,24},{24,28},{28,20},{20,12},{12,4},{4,0},{1,9},{9... | collective-permute-start | bytes 3538952 | tf_op jit(solution)/shard_map/ppermute | solution.py:64
  119.1 26.3 %collective-permute-start.18 = (bf16[2,192,1536]{2,1,0:T(8,128)(2,1)S(1)}, bf16[2,192,1536]{2,1,0:T(8,128)(2,1)}, u32[]{:S(2)}, u32[]{:S(2)}) collective-permute-start(bf16[2,192,1536]{2,1,0:T(8,128)(2,1)S(1)} %bitcast.373), channel_id=1, source_target_pairs={{0,4},{8,0},{16,8},{24,16},{28,24},{20,28},{12,20},{4,12},{1,5},{9... | collective-permute-start | bytes 3538952 | tf_op jit(solution)/shard_map/ppermute | solution.py:67
  145.4 26.0 %collective-permute-start.22 = (bf16[2,192,1536]{2,1,0:T(8,128)(2,1)}, bf16[2,192,1536]{2,1,0:T(8,128)(2,1)}, u32[]{:S(2)}, u32[]{:S(2)}) collective-permute-start(bf16[2,192,1536]{2,1,0:T(8,128)(2,1)} %collective-permute-done.17), channel_id=1, source_target_pairs={{0,8},{8,16},{16,24},{24,28},{28,20},{20,12},{12,4},{4,0},{1,9},{9... | collective-permute-start | bytes 3538952 | tf_op jit(solution)/shard_map/ppermute | solution.py:64
  145.8 25.8 %collective-permute-start.23 = (bf16[2,192,1536]{2,1,0:T(8,128)(2,1)}, bf16[2,192,1536]{2,1,0:T(8,128)(2,1)}, u32[]{:S(2)}, u32[]{:S(2)}) collective-permute-start(bf16[2,192,1536]{2,1,0:T(8,128)(2,1)} %collective-permute-done.18), channel_id=1, source_target_pairs={{0,4},{8,0},{16,8},{24,16},{28,24},{20,28},{12,20},{4,12},{1,5},{9... | collective-permute-start | bytes 3538952 | tf_op jit(solution)/shard_map/ppermute | solution.py:67
  150.9 49.2 %collective-permute-start.19 = (f32[384,1536]{1,0:T(8,128)}, f32[384,1536]{1,0:T(8,128)}, u32[]{:S(2)}, u32[]{:S(2)}) collective-permute-start(f32[384,1536]{1,0:T(8,128)} %fusion.65), channel_id=1, source_target_pairs={{0,1},{1,0},{2,3},{3,2},{4,5},{5,4},{6,7},{7,6},{8,9},{9,8},{10,11... | collective-permute-start | bytes 7077896 | tf_op jit(solution)/shard_map/ppermute | solution.py:209
  171.7 25.9 %collective-permute-start.27 = (bf16[2,192,1536]{2,1,0:T(8,128)(2,1)}, bf16[2,192,1536]{2,1,0:T(8,128)(2,1)S(1)}, u32[]{:S(2)}, u32[]{:S(2)}) collective-permute-start(bf16[2,192,1536]{2,1,0:T(8,128)(2,1)} %collective-permute-done.22), channel_id=1, source_target_pairs={{0,8},{8,16},{16,24},{24,28},{28,20},{20,12},{12,4},{4,0},{1,9},{9... | collective-permute-start | bytes 3538952 | tf_op jit(solution)/shard_map/ppermute | solution.py:64
  172.0 25.9 %collective-permute-start.28 = (bf16[2,192,1536]{2,1,0:T(8,128)(2,1)}, bf16[2,192,1536]{2,1,0:T(8,128)(2,1)S(1)}, u32[]{:S(2)}, u32[]{:S(2)}) collective-permute-start(bf16[2,192,1536]{2,1,0:T(8,128)(2,1)} %collective-permute-done.23), channel_id=1, source_target_pairs={{0,4},{8,0},{16,8},{24,16},{28,24},{20,28},{12,20},{4,12},{1,5},{9... | collective-permute-start | bytes 3538952 | tf_op jit(solution)/shard_map/ppermute | solution.py:67
  211.0 22.9 %collective-permute-start.34 = (bf16[2,192,1536]{2,1,0:T(8,128)(2,1)}, bf16[2,192,1536]{2,1,0:T(8,128)(2,1)}, u32[]{:S(2)}, u32[]{:S(2)}) collective-permute-start(bf16[2,192,1536]{2,1,0:T(8,128)(2,1)} %bitcast.28), channel_id=1, source_target_pairs={{0,8},{8,16},{16,24},{24,28},{28,20},{20,12},{12,4},{4,0},{1,9},{9... | collective-permute-start | bytes 3538952 | tf_op jit(solution)/shard_map/ppermute | solution.py:64
  211.5 22.8 %collective-permute-start.35 = (bf16[2,192,1536]{2,1,0:T(8,128)(2,1)}, bf16[2,192,1536]{2,1,0:T(8,128)(2,1)}, u32[]{:S(2)}, u32[]{:S(2)}) collective-permute-start(bf16[2,192,1536]{2,1,0:T(8,128)(2,1)} %bitcast.28), channel_id=1, source_target_pairs={{0,4},{8,0},{16,8},{24,16},{28,24},{20,28},{12,20},{4,12},{1,5},{9... | collective-permute-start | bytes 3538952 | tf_op jit(solution)/shard_map/ppermute | solution.py:67
  234.3 26.1 %collective-permute-start.36 = (bf16[2,192,1536]{2,1,0:T(8,128)(2,1)}, bf16[2,192,1536]{2,1,0:T(8,128)(2,1)S(1)}, u32[]{:S(2)}, u32[]{:S(2)}) collective-permute-start(bf16[2,192,1536]{2,1,0:T(8,128)(2,1)} %collective-permute-done.34), channel_id=1, source_target_pairs={{0,8},{8,16},{16,24},{24,28},{28,20},{20,12},{12,4},{4,0},{1,9},{9... | collective-permute-start | bytes 3538952 | tf_op jit(solution)/shard_map/ppermute | solution.py:64
  234.8 25.8 %collective-permute-start.37 = (bf16[2,192,1536]{2,1,0:T(8,128)(2,1)}, bf16[2,192,1536]{2,1,0:T(8,128)(2,1)S(1)}, u32[]{:S(2)}, u32[]{:S(2)}) collective-permute-start(bf16[2,192,1536]{2,1,0:T(8,128)(2,1)} %collective-permute-done.35), channel_id=1, source_target_pairs={{0,4},{8,0},{16,8},{24,16},{28,24},{20,28},{12,20},{4,12},{1,5},{9... | collective-permute-start | bytes 3538952 | tf_op jit(solution)/shard_map/ppermute | solution.py:67
  260.6 26.0 %collective-permute-start.38 = (bf16[2,192,1536]{2,1,0:T(8,128)(2,1)S(1)}, bf16[2,192,1536]{2,1,0:T(8,128)(2,1)S(1)}, u32[]{:S(2)}, u32[]{:S(2)}) collective-permute-start(bf16[2,192,1536]{2,1,0:T(8,128)(2,1)S(1)} %collective-permute-done.36), channel_id=1, source_target_pairs={{0,8},{8,16},{16,24},{24,28},{28,20},{20,12},{12,4},{4,0},{1,9},{9... | collective-permute-start | bytes 3538952 | tf_op jit(solution)/shard_map/ppermute | solution.py:64
  260.9 25.7 %collective-permute-start.39 = (bf16[2,192,1536]{2,1,0:T(8,128)(2,1)S(1)}, bf16[2,192,1536]{2,1,0:T(8,128)(2,1)S(1)}, u32[]{:S(2)}, u32[]{:S(2)}) collective-permute-start(bf16[2,192,1536]{2,1,0:T(8,128)(2,1)S(1)} %collective-permute-done.37), channel_id=1, source_target_pairs={{0,4},{8,0},{16,8},{24,16},{28,24},{20,28},{12,20},{4,12},{1,5},{9... | collective-permute-start | bytes 3538952 | tf_op jit(solution)/shard_map/ppermute | solution.py:67
  320.8 36.9 %collective-permute-start.44 = (f32[384,1536]{1,0:T(8,128)}, f32[384,1536]{1,0:T(8,128)}, u32[]{:S(2)}, u32[]{:S(2)}) collective-permute-start(f32[384,1536]{1,0:T(8,128)} %fusion.7), channel_id=1, source_target_pairs={{0,1},{1,0},{2,3},{3,2},{4,5},{5,4},{6,7},{7,6},{8,9},{9,8},{10,11... | collective-permute-start | bytes 7077896 | tf_op jit(solution)/shard_map/ppermute | solution.py:209
  322.0 28.7 %collective-permute-start.47 = (bf16[2,192,1536]{2,1,0:T(8,128)(2,1)}, bf16[2,192,1536]{2,1,0:T(8,128)(2,1)}, u32[]{:S(2)}, u32[]{:S(2)}) collective-permute-start(bf16[2,192,1536]{2,1,0:T(8,128)(2,1)} %add_convert_fusion.17), channel_id=1, source_target_pairs={{0,8},{8,16},{16,24},{24,28},{28,20},{20,12},{12,4},{4,0},{1,9},{9... | collective-permute-start | bytes 3538952 | tf_op jit(solution)/shard_map/ppermute | solution.py:64
  323.6 28.4 %collective-permute-start.48 = (bf16[2,192,1536]{2,1,0:T(8,128)(2,1)}, bf16[2,192,1536]{2,1,0:T(8,128)(2,1)}, u32[]{:S(2)}, u32[]{:S(2)}) collective-permute-start(bf16[2,192,1536]{2,1,0:T(8,128)(2,1)} %add_convert_fusion.16), channel_id=1, source_target_pairs={{0,4},{8,0},{16,8},{24,16},{28,24},{20,28},{12,20},{4,12},{1,5},{9... | collective-permute-start | bytes 3538952 | tf_op jit(solution)/shard_map/ppermute | solution.py:67
  353.6 27.3 %collective-permute-start.55 = (bf16[2,192,1536]{2,1,0:T(8,128)(2,1)S(1)}, bf16[2,192,1536]{2,1,0:T(8,128)(2,1)S(1)}, u32[]{:S(2)}, u32[]{:S(2)}) collective-permute-start(bf16[2,192,1536]{2,1,0:T(8,128)(2,1)S(1)} %add_convert_fusion.15), channel_id=1, source_target_pairs={{0,8},{8,16},{16,24},{24,28},{28,20},{20,12},{12,4},{4,0},{1,9},{9... | collective-permute-start | bytes 3538952 | tf_op jit(solution)/shard_map/ppermute | solution.py:64
  356.8 27.3 %collective-permute-start.56 = (bf16[2,192,1536]{2,1,0:T(8,128)(2,1)S(1)}, bf16[2,192,1536]{2,1,0:T(8,128)(2,1)S(1)}, u32[]{:S(2)}, u32[]{:S(2)}) collective-permute-start(bf16[2,192,1536]{2,1,0:T(8,128)(2,1)S(1)} %add_convert_fusion.14), channel_id=1, source_target_pairs={{0,4},{8,0},{16,8},{24,16},{28,24},{20,28},{12,20},{4,12},{1,5},{9... | collective-permute-start | bytes 3538952 | tf_op jit(solution)/shard_map/ppermute | solution.py:67
  363.0 23.8 %collective-permute-start.46 = (bf16[224,1536]{1,0:T(8,128)(2,1)S(1)}, bf16[224,1536]{1,0:T(8,128)(2,1)S(1)}, u32[]{:S(2)}, u32[]{:S(2)}) collective-permute-start(bf16[224,1536]{1,0:T(8,128)(2,1)S(1)} %pad_maximum_fusion.3), channel_id=1, source_target_pairs={{0,2},{1,3},{2,0},{3,1},{4,6},{5,7},{6,4},{7,5},{8,10},{9,11},{10,... | collective-permute-start | bytes 2064392 | tf_op jit(solution)/shard_map/ppermute | solution.py:213
  384.4 26.2 %collective-permute-start.57 = (bf16[2,192,1536]{2,1,0:T(8,128)(2,1)S(1)}, bf16[2,192,1536]{2,1,0:T(8,128)(2,1)S(1)}, u32[]{:S(2)}, u32[]{:S(2)}) collective-permute-start(bf16[2,192,1536]{2,1,0:T(8,128)(2,1)S(1)} %add_convert_fusion.13), channel_id=1, source_target_pairs={{0,8},{8,16},{16,24},{24,28},{28,20},{20,12},{12,4},{4,0},{1,9},{9... | collective-permute-start | bytes 3538952 | tf_op jit(solution)/shard_map/ppermute | solution.py:64
  386.4 25.9 %collective-permute-start.58 = (bf16[2,192,1536]{2,1,0:T(8,128)(2,1)S(1)}, bf16[2,192,1536]{2,1,0:T(8,128)(2,1)S(1)}, u32[]{:S(2)}, u32[]{:S(2)}) collective-permute-start(bf16[2,192,1536]{2,1,0:T(8,128)(2,1)S(1)} %add_convert_fusion.12), channel_id=1, source_target_pairs={{0,4},{8,0},{16,8},{24,16},{28,24},{20,28},{12,20},{4,12},{1,5},{9... | collective-permute-start | bytes 3538952 | tf_op jit(solution)/shard_map/ppermute | solution.py:67
  390.9 26.0 %collective-permute-start.52 = (bf16[224,1536]{1,0:T(8,128)(2,1)S(1)}, bf16[224,1536]{1,0:T(8,128)(2,1)S(1)}, u32[]{:S(2)}, u32[]{:S(2)}) collective-permute-start(bf16[224,1536]{1,0:T(8,128)(2,1)S(1)} %pad_maximum_fusion.4.own), channel_id=1, source_target_pairs={{0,2},{1,3},{2,0},{3,1},{4,6},{5,7},{6,4},{7,5},{8,10},{9,11},{10,... | collective-permute-start | bytes 2064392 | tf_op jit(solution)/shard_map/ppermute | solution.py:213
  392.4 38.2 %collective-permute-start.53 = (bf16[224,1536]{1,0:T(8,128)(2,1)S(1)}, bf16[224,1536]{1,0:T(8,128)(2,1)S(1)}, u32[]{:S(2)}, u32[]{:S(2)}) collective-permute-start(bf16[224,1536]{1,0:T(8,128)(2,1)S(1)} %pad_maximum_fusion.4.own), channel_id=1, source_target_pairs={{0,1},{1,0},{2,3},{3,2},{4,5},{5,4},{6,7},{7,6},{8,9},{9,8},{10,11... | collective-permute-start | bytes 2064392 | tf_op jit(solution)/shard_map/ppermute | solution.py:209
  402.2 63.1 %collective-permute-start.49 = (f32[384,1536]{1,0:T(8,128)}, f32[384,1536]{1,0:T(8,128)}, u32[]{:S(2)}, u32[]{:S(2)}) collective-permute-start(f32[384,1536]{1,0:T(8,128)} %fusion.13), channel_id=1, source_target_pairs={{0,1},{1,0},{2,3},{3,2},{4,5},{5,4},{6,7},{7,6},{8,9},{9,8},{10,11... | collective-permute-start | bytes 7077896 | tf_op jit(solution)/shard_map/ppermute | solution.py:209
  427.3 32.6 %collective-permute-start.64 = (bf16[2,192,1536]{2,1,0:T(8,128)(2,1)}, bf16[2,192,1536]{2,1,0:T(8,128)(2,1)}, u32[]{:S(2)}, u32[]{:S(2)}) collective-permute-start(bf16[2,192,1536]{2,1,0:T(8,128)(2,1)} %add_convert_fusion.11), channel_id=1, source_target_pairs={{0,8},{8,16},{16,24},{24,28},{28,20},{20,12},{12,4},{4,0},{1,9},{9... | collective-permute-start | bytes 3538952 | tf_op jit(solution)/shard_map/ppermute | solution.py:64
  429.6 30.4 %collective-permute-start.65 = (bf16[2,192,1536]{2,1,0:T(8,128)(2,1)}, bf16[2,192,1536]{2,1,0:T(8,128)(2,1)}, u32[]{:S(2)}, u32[]{:S(2)}) collective-permute-start(bf16[2,192,1536]{2,1,0:T(8,128)(2,1)} %add_convert_fusion.10), channel_id=1, source_target_pairs={{0,4},{8,0},{16,8},{24,16},{28,24},{20,28},{12,20},{4,12},{1,5},{9... | collective-permute-start | bytes 3538952 | tf_op jit(solution)/shard_map/ppermute | solution.py:67
  455.6 19.3 %collective-permute-start.60 = (f32[64,1536]{1,0:T(8,128)S(1)}, f32[64,1536]{1,0:T(8,128)S(1)}, u32[]{:S(2)}, u32[]{:S(2)}) collective-permute-start(f32[64,1536]{1,0:T(8,128)S(1)} %fusion.23), channel_id=1, source_target_pairs={{0,1},{1,0},{2,3},{3,2},{4,5},{5,4},{6,7},{7,6},{8,9},{9,8},{10,11... | collective-permute-start | bytes 1179656 | tf_op jit(solution)/shard_map/ppermute | solution.py:209
  459.5 37.4 %collective-permute-start.59 = (f32[384,1536]{1,0:T(8,128)S(1)}, f32[384,1536]{1,0:T(8,128)S(1)}, u32[]{:S(2)}, u32[]{:S(2)}) collective-permute-start(f32[384,1536]{1,0:T(8,128)S(1)} %fusion.22), channel_id=1, source_target_pairs={{0,1},{1,0},{2,3},{3,2},{4,5},{5,4},{6,7},{7,6},{8,9},{9,8},{10,11... | collective-permute-start | bytes 7077896 | tf_op jit(solution)/shard_map/ppermute | solution.py:209
  461.5 28.2 %collective-permute-start.66 = (bf16[2,192,1536]{2,1,0:T(8,128)(2,1)S(1)}, bf16[2,192,1536]{2,1,0:T(8,128)(2,1)S(1)}, u32[]{:S(2)}, u32[]{:S(2)}) collective-permute-start(bf16[2,192,1536]{2,1,0:T(8,128)(2,1)S(1)} %add_convert_fusion.9), channel_id=1, source_target_pairs={{0,8},{8,16},{16,24},{24,28},{28,20},{20,12},{12,4},{4,0},{1,9},{9... | collective-permute-start | bytes 3538952 | tf_op jit(solution)/shard_map/ppermute | solution.py:64
  464.2 27.9 %collective-permute-start.67 = (bf16[2,192,1536]{2,1,0:T(8,128)(2,1)S(1)}, bf16[2,192,1536]{2,1,0:T(8,128)(2,1)S(1)}, u32[]{:S(2)}, u32[]{:S(2)}) collective-permute-start(bf16[2,192,1536]{2,1,0:T(8,128)(2,1)S(1)} %add_convert_fusion.8), channel_id=1, source_target_pairs={{0,4},{8,0},{16,8},{24,16},{28,24},{20,28},{12,20},{4,12},{1,5},{9... | collective-permute-start | bytes 3538952 | tf_op jit(solution)/shard_map/ppermute | solution.py:67
  493.4 31.2 %collective-permute-start.68 = (bf16[2,192,1536]{2,1,0:T(8,128)(2,1)}, bf16[2,192,1536]{2,1,0:T(8,128)(2,1)}, u32[]{:S(2)}, u32[]{:S(2)}) collective-permute-start(bf16[2,192,1536]{2,1,0:T(8,128)(2,1)} %add_convert_fusion.7), channel_id=1, source_target_pairs={{0,8},{8,16},{16,24},{24,28},{28,20},{20,12},{12,4},{4,0},{1,9},{9... | collective-permute-start | bytes 3538952 | tf_op jit(solution)/shard_map/ppermute | solution.py:64
  495.7 28.9 %collective-permute-start.69 = (bf16[2,192,1536]{2,1,0:T(8,128)(2,1)}, bf16[2,192,1536]{2,1,0:T(8,128)(2,1)}, u32[]{:S(2)}, u32[]{:S(2)}) collective-permute-start(bf16[2,192,1536]{2,1,0:T(8,128)(2,1)} %add_convert_fusion.6), channel_id=1, source_target_pairs={{0,4},{8,0},{16,8},{24,16},{28,24},{20,28},{12,20},{4,12},{1,5},{9... | collective-permute-start | bytes 3538952 | tf_op jit(solution)/shard_map/ppermute | solution.py:67
  556.0 27.6 %collective-permute-start.74 = (bf16[2,192,1536]{2,1,0:T(8,128)(2,1)}, bf16[2,192,1536]{2,1,0:T(8,128)(2,1)}, u32[]{:S(2)}, u32[]{:S(2)}) collective-permute-start(bf16[2,192,1536]{2,1,0:T(8,128)(2,1)} %add_convert_fusion.5), channel_id=1, source_target_pairs={{0,8},{8,16},{16,24},{24,28},{28,20},{20,12},{12,4},{4,0},{1,9},{9... | collective-permute-start | bytes 3538952 | tf_op jit(solution)/shard_map/ppermute | solution.py:64
  558.4 27.5 %collective-permute-start.75 = (bf16[2,192,1536]{2,1,0:T(8,128)(2,1)}, bf16[2,192,1536]{2,1,0:T(8,128)(2,1)}, u32[]{:S(2)}, u32[]{:S(2)}) collective-permute-start(bf16[2,192,1536]{2,1,0:T(8,128)(2,1)} %add_convert_fusion.4), channel_id=1, source_target_pairs={{0,4},{8,0},{16,8},{24,16},{28,24},{20,28},{12,20},{4,12},{1,5},{9... | collective-permute-start | bytes 3538952 | tf_op jit(solution)/shard_map/ppermute | solution.py:67
  601.4 24.9 %collective-permute-start.92 = (bf16[2,192,1536]{2,1,0:T(8,128)(2,1)}, bf16[2,192,1536]{2,1,0:T(8,128)(2,1)}, u32[]{:S(2)}, u32[]{:S(2)}) collective-permute-start(bf16[2,192,1536]{2,1,0:T(8,128)(2,1)} %add_convert_fusion.3), channel_id=1, source_target_pairs={{0,8},{8,16},{16,24},{24,28},{28,20},{20,12},{12,4},{4,0},{1,9},{9... | collective-permute-start | bytes 3538952 | tf_op jit(solution)/shard_map/ppermute | solution.py:64
  602.6 24.8 %collective-permute-start.93 = (bf16[2,192,1536]{2,1,0:T(8,128)(2,1)}, bf16[2,192,1536]{2,1,0:T(8,128)(2,1)}, u32[]{:S(2)}, u32[]{:S(2)}) collective-permute-start(bf16[2,192,1536]{2,1,0:T(8,128)(2,1)} %add_convert_fusion.2), channel_id=1, source_target_pairs={{0,4},{8,0},{16,8},{24,16},{28,24},{20,28},{12,20},{4,12},{1,5},{9... | collective-permute-start | bytes 3538952 | tf_op jit(solution)/shard_map/ppermute | solution.py:67
  630.2 40.7 %collective-permute-start.94 = (bf16[2,192,1536]{2,1,0:T(8,128)(2,1)}, bf16[2,192,1536]{2,1,0:T(8,128)(2,1)}, u32[]{:S(2)}, u32[]{:S(2)}) collective-permute-start(bf16[2,192,1536]{2,1,0:T(8,128)(2,1)} %add_convert_fusion.1), channel_id=1, source_target_pairs={{0,8},{8,16},{16,24},{24,28},{28,20},{20,12},{12,4},{4,0},{1,9},{9... | collective-permute-start | bytes 3538952 | tf_op jit(solution)/shard_map/ppermute | solution.py:64
  634.5 36.3 %collective-permute-start.95 = (bf16[2,192,1536]{2,1,0:T(8,128)(2,1)}, bf16[2,192,1536]{2,1,0:T(8,128)(2,1)}, u32[]{:S(2)}, u32[]{:S(2)}) collective-permute-start(bf16[2,192,1536]{2,1,0:T(8,128)(2,1)} %add_convert_fusion), channel_id=1, source_target_pairs={{0,4},{8,0},{16,8},{24,16},{28,24},{20,28},{12,20},{4,12},{1,5},{9... | collective-permute-start | bytes 3538952 | tf_op jit(solution)/shard_map/ppermute | solution.py:67
  640.1 20.0 %collective-permute-start.87 = (f32[1,192]{1,0:T(1,128)S(1)}, f32[1,192]{1,0:T(1,128)S(1)}, u32[]{:S(2)}, u32[]{:S(2)}) collective-permute-start(f32[1,192]{1,0:T(1,128)S(1)} %get-tuple-element.424), channel_id=1, source_target_pairs={{0,20},{4,24},{8,28},{12,0},{16,4},{20,8},{24,12},{28,16},{1,21},{... | collective-permute-start | bytes 2312 | tf_op jit(solution)/shard_map/ppermute | solution.py:202
  (235 other events, 2707.7 us)

commit v3 on v2

--- a/solution.py
+++ b/solution.py
@@ -1,3 +1,5 @@
+import functools
+
 import jax
 import jax.numpy as jnp
 from jax import lax
@@ -48,6 +50,10 @@
     if isinstance(position, int):
         return 2 * position if position < count // 2 else 2 * (count - 1 - position) + 1
     return jnp.where(position < count // 2, 2 * position, 2 * (count - 1 - position) + 1)
+
+
+def add_three(own, forward, backward):
+    return own.astype(F32) + forward.astype(F32) + backward.astype(F32)
 
 
 class Ring:
@@ -80,14 +86,14 @@
         whole = put(whole, shard, 0)
         forward, backward = (shard, shard)
         for step in range(1, self.half):
-            forward, backward = yield (self.right(forward), self.left(backward))
+            forward, backward = yield (forward, backward)
             whole = put(whole, forward, -step)
             whole = put(whole, backward, step)
-        forward, backward = yield (self.right(forward[:, :cut]), self.left(backward[:, cut:]))
+        forward, backward = yield (forward[:, :cut], backward[:, cut:])
         whole = put(whole, forward, -self.half)
         return put(whole, backward, self.half, cut)
 
-    def scatter(self, wholes):
+    def scatter(self, wholes, finish=add_three):
         rows = wholes[0][0].shape[0] // self.count
         cut = rows // 2
 
@@ -103,19 +109,15 @@
                 ]
             )
 
-        forward, backward = yield (
-            self.right(block(self.half, 0, cut)),
-            self.left(block(-self.half, cut, rows - cut)),
-        )
+        forward, backward = yield (block(self.half, 0, cut), block(-self.half, cut, rows - cut))
         forward = jnp.pad(forward.astype(F32), ((0, 0), (0, rows - cut), (0, 0)))
         backward = jnp.pad(backward.astype(F32), ((0, 0), (cut, 0), (0, 0)))
         for step in range(self.half - 1, 0, -1):
             forward, backward = yield (
-                self.right((block(step).astype(F32) + forward).astype(BF16)),
-                self.left((block(-step).astype(F32) + backward).astype(BF16)),
+                (block(step).astype(F32) + forward.astype(F32)).astype(BF16),
+                (block(-step).astype(F32) + backward.astype(F32)).astype(BF16),
             )
-            forward, backward = (forward.astype(F32), backward.astype(F32))
-        return block(0).astype(F32) + forward + backward
+        return finish(block(0), forward, backward)
 
 
 def fence(pending, values):
@@ -128,18 +130,23 @@
 
 
 class Lane:
-    def __init__(self):
+    def __init__(self, ring):
+        self.ring = ring
         self.last = ()
+        self.sent = []
 
     def add(self, make, source, hooks=None):
         if self.last:
             source = lax.optimization_barrier((self.last, source))[1]
         steps = make(source)
         received = None
+        self.sent = []
         marks = []
         try:
             while True:
-                received = lax.optimization_barrier(steps.send(received))
+                right, left = lax.optimization_barrier(steps.send(received))
+                self.sent.append((right, left))
+                received = lax.optimization_barrier((self.ring.right(right), self.ring.left(left)))
                 if hooks and len(marks) in hooks:
                     received = hooks[len(marks)](received)
                 marks.append(received)
@@ -197,12 +204,39 @@
     return value
 
 
-def small_exchange(value, axis, count):
-    pieces = [value[:1]] + [
-        lax.ppermute(value[count - offset : count - offset + 1], axis, shift_pairs(count, -offset))
-        for offset in range(1, count)
-    ]
-    return jnp.concatenate(pieces)
+class Column:
+    def __init__(self, count):
+        self.count = count
+        self.size = count // 2
+        self.high = lax.axis_index("dp") // 2
+        self.low = lax.axis_index("dp") % 2
+
+    def swap_low(self, value):
+        return lax.ppermute(value, "dp", flip_pairs(self.count, 1))
+
+    def shift(self, value, offset):
+        pairs = [
+            (2 * h + l, 2 * ((h + offset) % self.size) + l)
+            for h in range(self.size)
+            for l in range(2)
+        ]
+        return lax.ppermute(value, "dp", pairs)
+
+    def paired(self, value, other):
+        return jnp.where(self.low == 0, jnp.stack([value, other]), jnp.stack([other, value]))
+
+    def shifts_from(self, value):
+        return [value] + [self.shift(value, -k) for k in range(1, self.size)]
+
+    def shifts_to(self, values):
+        return [values[0]] + [self.shift(values[k], k) for k in range(1, self.size)]
+
+    def near(self, value):
+        return jnp.roll(value.reshape((self.size, 2) + value.shape[1:]), -self.high, axis=0)
+
+    def from_back(self, value):
+        reverse = jnp.stack([value[-k % self.size] for k in range(self.size)])
+        return jnp.roll(reverse, self.high, axis=0)
 
 
 def swap_core(value):
@@ -245,26 +279,128 @@
 
 
 def gather_rows(first, second):
-    split = first.shape[0]
-    own = jnp.concatenate([first, second])
+    return gather_own(jnp.concatenate([first, second]), first.shape[0])
+
+
+def gather_own(own, split):
     over_y = swap_y(own)
     core = swap_core(own)
     both = swap_core(over_y)
     return (assemble((own, over_y, core, both), split), own)
 
 
-def reduce_rows(factors, products):
+def reduce_parts(factors, products):
     away, kept = ([], [])
     for factor, product in zip(factors, products):
         rows = factor.shape[0] // 2
         away.append(product(factor[rows:]))
         kept.append(product(factor[:rows]))
     sums = [keep + swap_core(piece) for keep, piece in zip(kept, away)]
-    quarter = [total.shape[0] // 2 for total in sums]
-    crossing = jnp.concatenate([total[size:].astype(BF16) for total, size in zip(sums, quarter)])
-    got = swap_y(crossing).astype(F32)
-    size = quarter[0]
-    return ([sums[0][:size] + got[:size], sums[1][:quarter[1]] + got[size:]], crossing)
+    crossing = jnp.concatenate([total[total.shape[0] // 2 :].astype(BF16) for total in sums])
+    return (sums, swap_y(crossing), crossing)
+
+
+def reduce_rows(factors, products):
+    sums, got, crossing = reduce_parts(factors, products)
+    got = got.astype(F32)
+    size = sums[0].shape[0] // 2
+    rest = sums[1].shape[0] // 2
+    return ([sums[0][:size] + got[:size], sums[1][:rest] + got[size:]], crossing)
+
+
+def norm_back_rows(total, got, normed, inv_std, scale, base):
+    hidden = total + got.astype(F32)
+    upstream = hidden * (1.0 + scale)
+    grad = base + norm_back(upstream, normed, inv_std)
+    return (
+        grad,
+        jnp.sum(hidden, axis=0, keepdims=True),
+        jnp.sum(hidden * normed, axis=0, keepdims=True),
+    )
+
+
+def middle_kernel(si, st, got, ni, nt, vi, vt, mods, ci, ct, ai, at, gi, gt, dz, sums):
+    size = gi.shape[0]
+    parts = ((si, ni, vi, ci, ai, gi, 0), (st, nt, vt, ct, at, gt, 1))
+    for total, normed, inv_std, cot, bias, out, s in parts:
+        rows = slice(0, size) if s == 0 else slice(size, size + gt.shape[0])
+        grad, shift, scale = norm_back_rows(
+            total[...], got[rows], normed[...], inv_std[...], mods[s, 4:5], cot[...].astype(F32)
+        )
+        scaled = mods[s, 2:3] * grad
+        out[...] = grad
+        dz[rows] = scaled.astype(BF16)
+        sums[4 * s : 4 * s + 1] = shift
+        sums[4 * s + 1 : 4 * s + 2] = scale
+        sums[4 * s + 2 : 4 * s + 3] = jnp.sum(grad * bias[...], axis=0, keepdims=True)
+        sums[4 * s + 3 : 4 * s + 4] = jnp.sum(scaled, axis=0, keepdims=True)
+
+
+def first_kernel(si, st, got, ni, nt, vi, vt, mods, bi, bt, known, extra, gi, gt, rows_out):
+    size = gi.shape[0]
+    for total, normed, inv_std, base, out, s in (
+        (si, ni, vi, bi, gi, 0),
+        (st, nt, vt, bt, gt, 1),
+    ):
+        rows = slice(0, size) if s == 0 else slice(size, size + gt.shape[0])
+        grad, shift, scale = norm_back_rows(
+            total[...], got[rows], normed[...], inv_std[...], mods[s, 1:2], base[...]
+        )
+        out[...] = grad
+        at = 6 * s
+        rows_out[at : at + 1] = shift
+        rows_out[at + 1 : at + 2] = scale
+        rows_out[at + 2 : at + 3] = known[4 * s + 2 : 4 * s + 3]
+        rows_out[at + 3 : at + 4] = known[4 * s : 4 * s + 1]
+        rows_out[at + 4 : at + 5] = known[4 * s + 1 : 4 * s + 2]
+        rows_out[at + 5 : at + 6] = extra[s : s + 1]
+        rows_out[12 + s : 13 + s] = known[4 * s + 3 : 4 * s + 4]
+        rows_out[14 + s : 15 + s] = extra[2 + s : 3 + s]
+
+
+def whole(shape):
+    return pl.BlockSpec(shape, lambda i: (0,) * len(shape))
+
+
+def norm_call(kernel, sums, others, out_shapes):
+    halves = [whole((total.shape[0] // 2, total.shape[1])) for total in sums]
+    return pl.pallas_call(
+        kernel,
+        grid=(1,),
+        in_specs=halves + [whole(other.shape) for other in others],
+        out_specs=[whole(shape.shape) for shape in out_shapes],
+        out_shape=out_shapes,
+        compiler_params=pltpu.CompilerParams(vmem_limit_bytes=40 * 2**20),
+        cost_estimate=pl.CostEstimate(flops=0, bytes_accessed=8 * 2**20, transcendentals=0),
+    )(*sums, *others)
+
+
+def split_kernel(own, forward, backward, qkv, out):
+    total = add_three(own[0], forward[0], backward[0])
+    width = qkv.shape[3]
+    for part in range(3):
+        qkv[0, :, part, :] = total[:, part * width : (part + 1) * width]
+    out[0] = total[:, 3 * width :].T
+
+
+def split_grads(own, forward, backward):
+    streams, rows, width = own.shape
+    quarter = width // 4
+    block = pl.BlockSpec((1, rows, width), lambda i: (i, 0, 0))
+    return pl.pallas_call(
+        split_kernel,
+        grid=(streams,),
+        in_specs=[block] * 3,
+        out_specs=[
+            pl.BlockSpec((1, rows, 3, quarter), lambda i: (i, 0, 0, 0)),
+            pl.BlockSpec((1, quarter, rows), lambda i: (i, 0, 0)),
+        ],
+        out_shape=[
+            jax.ShapeDtypeStruct((streams, rows, 3, quarter), F32),
+            jax.ShapeDtypeStruct((streams, quarter, rows), F32),
+        ],
+        compiler_params=pltpu.CompilerParams(vmem_limit_bytes=32 * 2**20),
+    )(own, forward, backward)
 
 
 CHUNK = 128
@@ -439,9 +575,10 @@
     silu_low = jax.nn.silu(cond_full).astype(BF16)
     own_cond = lax.dynamic_slice_in_dim(cond_full, dp_rank, 1, 0)
     own_cols = lax.dynamic_slice_in_dim(silu_low, dp_rank * row_block, row_block, 1)
-    near_cols = jnp.roll(own_cols, -dp_rank, axis=0)
+    column = Column(count)
+    near_cols = column.near(own_cols).reshape(count, row_block)
     mod_terms = jnp.einsum("sr,krc->skc", own_cols, ada_w[0], preferred_element_type=F32)
-    lane = Lane()
+    lane = Lane(ring)
     weights = []
     qkv_shard = qkv_w[0].reshape(2, row_block, 3 * heads_width)
     attn_shard = jnp.concatenate([qkv_shard, out_w[0].transpose(0, 2, 1)], axis=2)
@@ -512,37 +649,36 @@
         acts.append(gelu_tanh(pre_acts[s]).astype(BF16))
         down_w_grad.append(mm_tn(dy_full[s], acts[s]).astype(BF16))
     down_grad, marks = lane.add(ring.scatter, [(grad,) for grad in down_w_grad])
+    sent = lane.sent
     up_b_grad, pre_grads = ([None, None], [None, None])
     for s in (1, 0):
         act_grad = mm(dy_full[s], w_down[s])
         gelu_back = jax.vjp(gelu_tanh, pre_acts[s])[1]
         pre_grads[s] = gelu_back(act_grad)[0].astype(BF16)
         up_b_grad[s] = jnp.sum(pre_grads[s], axis=0, dtype=F32)
-    hidden_two, cross_two = reduce_rows(
-        later(pre_grads, marks[0]), [lambda rows, s=s: mm_nt(rows, w_up[s]) for s in both]
+    sums_two, got_two, cross_two = reduce_parts(
+        later(pre_grads, sent[1]), [lambda rows, s=s: mm_nt(rows, w_up[s]) for s in both]
     )
     late_grads = later(pre_grads, (cross_two,))
     up_w_grad = [mm_tn(full_two[s], late_grads[s]).astype(BF16) for s in both]
     up_grad, up_marks = lane.add(ring.scatter, [(grad,) for grad in up_w_grad])
-    hidden_two = later(hidden_two, marks[1])
-
-    shift_two_grad, scale_two_grad, mid_grads = ([], [], [])
-    gate_one_grad, out_bias_grad, dz_lows = ([], [], [])
-    for s in both:
-        shift_two_grad.append(jnp.sum(hidden_two[s], axis=0, keepdims=True))
-        scale_two_grad.append(jnp.sum(hidden_two[s] * normed_two[s], axis=0, keepdims=True))
-        upstream = hidden_two[s] * (1.0 + mods[s, 4])
-        mid_grads.append(gradients[s] + norm_back(upstream, normed_two[s], inv_two[s]))
-        gate_one_grad.append(jnp.sum(mid_grads[s] * attn_bias[s], axis=0, keepdims=True))
-        scaled = mods[s, 2] * mid_grads[s]
-        out_bias_grad.append(jnp.sum(scaled, axis=0, keepdims=True))
-        dz_lows.append(scaled.astype(BF16))
-    dz_full, dz_sent = gather_rows(*dz_lows)
-    dz_rows = later(dz_full, marks[2])
+    up_sent = lane.sent
+    got_two = later((got_two,), sent[2])[0]
+    size, rest = (streams[0].shape[0], streams[1].shape[0])
+    full_mods = mods.reshape(2, 6, width)
+    like = [jax.ShapeDtypeStruct((rows, width), F32) for rows in (size, rest, 8, 16)]
+    mid_image, mid_text, dz_sent, middle_rows = norm_call(
+        middle_kernel,
+        sums_two,
+        (got_two, *normed_two, *inv_two, full_mods, image_cot[0], text_cot[0], *attn_bias),
+        [like[0], like[1], jax.ShapeDtypeStruct((size + rest, width), BF16), like[2]],
+    )
+    dz_full, _ = gather_own(dz_sent, size)
+    dz_rows = later(dz_full, sent[3])
     attn_grads = [mm(dz_rows[s], w_out[s]).astype(BF16) for s in both]
     packed_grad = attend_back(*packed, *attn_grads, lse)
-    hidden_one, cross_one = reduce_rows(
-        later(packed_grad, marks[3]), [lambda rows, s=s: mm_nt(rows, w_qkv[s]) for s in both]
+    sums_one, got_one, cross_one = reduce_parts(
+        later(packed_grad, up_sent[2]), [lambda rows, s=s: mm_nt(rows, w_qkv[s]) for s in both]
     )
     late_grads = later(later(packed_grad, (cross_one,)), up_marks[0])
     qkv_w_grad, qv_b_grad = ([], [])
@@ -552,13 +688,6 @@
         qv_b_grad.append(jnp.stack([summed[0], summed[2]]))
     late_dz = later(dz_full, up_marks[0])
     out_w_grad = [mm_tn(late_dz[s], attn[s]).astype(BF16) for s in both]
-    shift_one_grad, scale_one_grad, new_grads = ([], [], [])
-    for s in both:
-        shift_one_grad.append(jnp.sum(hidden_one[s], axis=0, keepdims=True))
-        scale_one_grad.append(jnp.sum(hidden_one[s] * normed_one[s], axis=0, keepdims=True))
-        upstream = hidden_one[s] * (1.0 + mods[s, 1])
-        new_grads.append(mid_grads[s] + norm_back(upstream, normed_one[s], inv_one[s]))
-
     late_acts = later(acts, (dz_sent,))
     mlp_sums, cross_out = reduce_rows(
         late_acts, [lambda rows, s=s: mm_nt(rows, w_down[s]) for s in both]
@@ -569,58 +698,70 @@
         outputs.append((residuals[s] + mods[s, 5] * mlp_bias).astype(BF16))
         gate_two_grad.append(jnp.sum(gradients[s] * mlp_bias, axis=0, keepdims=True))
 
-    rows = []
-    for s in both:
-        rows += [
-            shift_one_grad[s],
-            scale_one_grad[s],
-            gate_one_grad[s],
-            shift_two_grad[s],
-            scale_two_grad[s],
-            gate_two_grad[s],
-        ]
-    rows = later(rows + out_bias_grad + down_bias_grad, up_marks[3])
-    total = small_sum(jnp.concatenate(rows), "tensor", members)
+    got_one = later((got_one,), up_marks[2])[0]
+    image_grad, text_grad, rows = norm_call(
+        first_kernel,
+        sums_one,
+        (
+            got_one,
+            *normed_one,
+            *inv_one,
+            full_mods,
+            mid_image,
+            mid_text,
+            middle_rows,
+            jnp.concatenate(gate_two_grad + down_bias_grad),
+        ),
+        [like[0], like[1], like[3]],
+    )
+    total = small_sum(rows, "tensor", members)
     mod_cols = 6 * width // members
     bias_cols = width // members
     tensor_rank = lax.axis_index("tensor")
+    lines = mod_cols // bias_cols
     mod_part = lax.dynamic_slice_in_dim(
-        total[:12].reshape(2, 6 * width), tensor_rank * mod_cols, mod_cols, 1
-    )
-    mod_part = mod_part.astype(BF16).astype(F32).reshape(-1)
+        total[:12].reshape(2, members * lines, bias_cols), tensor_rank * lines, lines, 1
+    )
+    mod_part = mod_part.astype(BF16).astype(F32).reshape(2 * lines, bias_cols)
     bias_part = lax.dynamic_slice_in_dim(total[12:], tensor_rank * bias_cols, bias_cols, 1)
-    qv_part = jnp.concatenate(qv_b_grad).reshape(-1)
-    up_part = jnp.concatenate(up_b_grad)
-    message = jnp.concatenate([mod_part, bias_part.reshape(-1), qv_part, up_part])[None]
+    qv_part = jnp.concatenate(qv_b_grad)
+    up_part = jnp.concatenate(up_b_grad).reshape(-1, bias_cols)
+    message = jnp.concatenate([mod_part, bias_part, qv_part, up_part])[None]
     kept = {}
 
+    def after_first(received):
+        kept["other"] = column.swap_low(message[0])
+        return received
+
     def after_second(received):
-        kept["every"] = small_gather(later((message,), received)[0], "dp", count)
-        return received
+        pair = column.paired(message[0], later((kept["other"],), received)[0])
+        kept["pairs"] = column.shifts_from(pair)
+        return later(received, (pair,))
 
     def after_third(received):
-        every_low = kept["every"][:, : 2 * mod_cols].reshape(count, 2, mod_cols).astype(BF16)
+        pairs = later(kept["pairs"], received)
+        every = jnp.stack(pairs).reshape((count,) + message.shape[1:])
+        kept["every"] = every
+        every_low = every[:, : 2 * lines].astype(BF16).reshape(count, 2, mod_cols)
         cond_terms = jnp.einsum("skc,krc->sr", every_low, ada_w[0], preferred_element_type=F32)
-        cond_terms = small_sum(cond_terms, "tensor", members)
-        kept["cond"] = small_exchange(cond_terms, "dp", count)
+        cond_terms = small_sum(cond_terms, "tensor", members).reshape(column.size, 2, row_block)
+        kept["cond"] = column.shifts_to(cond_terms)
         return later(received, (cond_terms,))
 
-    attn_grad, _ = lane.add(
-        ring.scatter, list(zip(qkv_w_grad, out_w_grad)), {1: after_second, 2: after_third}
-    )
-    qkv_grad = attn_grad[:, :, : 3 * heads_width]
-    out_grad = attn_grad[:, :, 3 * heads_width :]
+    attn_grad, attn_marks = lane.add(
+        functools.partial(ring.scatter, finish=split_grads), list(zip(qkv_w_grad, out_w_grad)), {0: after_first, 1: after_second, 2: after_third}
+    )
+    qkv_grad, out_grad = attn_grad
     every = kept["every"]
-    every_mod = every[:, : 2 * mod_cols].reshape(count, 2, mod_cols)
-    every_low = every_mod.astype(BF16)
+    every_low = every[:, : 2 * lines].astype(BF16).reshape(count, 2, mod_cols)
     summed = jnp.sum(every, axis=0)
 
     def own_piece(value):
         piece = value.shape[-1] // count
         return lax.dynamic_slice_in_dim(value, dp_rank * piece, piece, value.ndim - 1)
 
-    ends = [2 * mod_cols]
-    for size in (4 * bias_cols, qv_part.shape[0], up_part.shape[0]):
+    ends = [2 * lines]
+    for size in (4, qv_part.shape[0], up_part.shape[0]):
         ends.append(ends[-1] + size)
     ada_b_grad = own_piece(summed[: ends[0]].reshape(2, mod_cols))
     bias_sum = own_piece(summed[ends[0] : ends[1]].reshape(2, 2, bias_cols))
@@ -628,20 +769,24 @@
     up_sum = own_piece(summed[ends[2] : ends[3]].reshape(2, -1))
 
     ada_w_grad = jnp.einsum("sr,skc->krc", near_cols, every_low, preferred_element_type=F32)
-    cond_sum = in_order(kept["cond"], "dp").reshape(1, width)
+    cond = jnp.stack(kept["cond"])
+    mine = jnp.where(column.low == 0, cond[:, 0], cond[:, 1])
+    other = jnp.where(column.low == 0, cond[:, 1], cond[:, 0])
+    cond_sum = column.paired(mine, column.swap_low(other))
+    cond_sum = column.from_back(cond_sum.transpose(1, 0, 2)).reshape(1, width)
     sigmoid = jax.nn.sigmoid(own_cond)
     cond_grad = cond_sum * sigmoid * (1.0 + own_cond * (1.0 - sigmoid))
     return (
         outputs[0][None],
         outputs[1][None],
-        new_grads[0][None],
-        new_grads[1][None],
+        image_grad[None],
+        text_grad[None],
         cond_grad,
         ada_w_grad[None],
         ada_b_grad[None],
-        qkv_grad.reshape(1, 2, row_block, 3, heads_width),
+        qkv_grad[None],
         qv_sum[None],
-        out_grad.transpose(0, 2, 1)[None],
+        out_grad[None],
         bias_sum[0][None],
         up_grad[None],
         up_sum[None],

time: 688 us -> 660 us (0.959)
  local copies, waits for them, and re-layouts: 117 us -> 89.6 us
  waiting for transfers between devices: 234 us -> 256 us
  other arithmetic: 80 us -> 62.7 us
  starting transfers between devices: 101 us -> 86 us
    ppermute x7 -> x8, waiting for transfers between devices: 16.6 us -> 28.5 us  [the longest x2 24.5 us: swap_low(): return lax.ppermute(value, 'dp', flip_pairs(self.count, 1))]
    ppermute x10 -> x3, starting transfers between devices: 11.7 us -> 1.79 us  [small_gather(): lax.ppermute(value, axis, shift_pairs(count, -offset))]
    ppermute x24, waiting for transfers between devices: 147 us -> 156 us  [right(): return lax.ppermute(value, 'dp', self.right_pairs)]
    unnamed x388 -> x234, local copies, waits for them, and re-layouts: 22.4 us -> 13.4 us
    ppermute x3, waiting for transfers between devices: 9.91 us -> 17 us  [small_scatter(): rest = mine + lax.ppermute(other, axis, flip_pairs(count, bit))]
    ppermute x7 -> x8, starting transfers between devices: 13.8 us -> 8.77 us  [the longest x6 7.51 us: shift(): return lax.ppermute(value, 'dp', pairs)]
    convert_element_type x26 -> x20, other arithmetic: 31.6 us -> 28 us  [the longest x9 14 us: scatter(): (block(step).astype(F32) + forward.astype(F32)).astype(BF16)]
  transfers between devices with their start and end apart: 96 -> 90, of which waited for: 47 -> 51; matrix products, arithmetic and copies ran while one was open for 40% -> 38% of each run, Pallas kernels for 4% -> 5%
where the time goes in v3:
time: 660 us; the launch traced here: 653 us
  waiting for transfers between devices  256 us (39%)
  matrix products  120 us (18%)
  local copies, waits for them, and re-layouts  89.6 us (14%)
  starting transfers between devices  86 us (13%)
  other arithmetic  62.7 us (10%)
  Pallas kernels  34.3 us (5%)
    ppermute x24, waiting for transfers between devices, right(): return lax.ppermute(value, 'dp', self.right_pairs)  156 us
    dot_general x32, matrix products, dot(): lax.dot_general(left, right, (dims, ((), ())), preferred_element_type=F32)  115 us
    dynamic_update_slice x27, local copies, waits for them, and re-layouts, put(): lax.dynamic_update_slice(whole, piece, (0, self.owner(offset) * rows + st...  35.2 us
    ppermute x24, starting transfers between devices, left(): return lax.ppermute(value, 'dp', self.left_pairs)  31 us
    ppermute x8, waiting for transfers between devices, swap_y(): return lax.ppermute(value, 'tensor', flip_pairs(4, 2))  27.9 us
    ppermute x2, waiting for transfers between devices, swap_low(): return lax.ppermute(value, 'dp', flip_pairs(self.count, 1))  24.5 us
    ppermute x24, starting transfers between devices, right(): return lax.ppermute(value, 'dp', self.right_pairs)  20.6 us
    ppermute x3, waiting for transfers between devices, small_scatter(): rest = mine + lax.ppermute(other, axis, flip_pairs(count, bit))  17 us
  transfers between devices with their start and end apart: 90, of which 51 were waited for; matrix products, arithmetic and copies ran while one was open for 38% of the time, Pallas kernels for 5%

profile of v3, /device:TPU:0, one launch (start us, length us, event | category | flops | bytes accessed | tf_op | source)
XLA Modules:
  0.0 652.9 jit_solution(9091338409944132549)
XLA Ops:
  15.4 4.1 broadcast.262.clone.1
  25.3 17.0 %collective-permute-done.1 = f32[2,2,2304]{2,1,0:T(2,128)S(1)} collective-permute-done((f32[2,2,2304]{2,1,0:T(2,128)S(1)}, f32[2,2,2304]{2,1,0:T(2,128)S(1)}, u32[]{:S(2)}, u32[]{:S(2)}) %collective-permute-start.1) | collective-permute-done | bytes 36896 | tf_op jit(solution)/shard_map/ppermute | solution.py:179
  61.1 12.9 %collective-permute-done.8.over_y = bf16[224,1536]{1,0:T(8,128)(2,1)S(1)} collective-permute-done((bf16[224,1536]{1,0:T(8,128)(2,1)S(1)}, bf16[224,1536]{1,0:T(8,128)(2,1)S(1)}, u32[]{:S(2)}, u32[]{:S(2)}) %collective-permute-start.8) | collective-permute-done | bytes 688160 | tf_op jit(solution)/shard_map/ppermute | solution.py:247
  81.6 21.0 %collective-permute-done.13 = bf16[2,192,1536]{2,1,0:T(8,128)(2,1)S(1)} collective-permute-done((bf16[2,192,1536]{2,1,0:T(8,128)(2,1)}, bf16[2,192,1536]{2,1,0:T(8,128)(2,1)S(1)}, u32[]{:S(2)}, u32[]{:S(2)}) %collective-permute-start.13) | collective-permute-done | bytes 1179680 | tf_op jit(solution)/shard_map/ppermute | solution.py:70
  109.7 9.1 %collective-permute-done.15 = bf16[2,96,1536]{2,1,0:T(8,128)(2,1)S(1)} collective-permute-done((bf16[2,96,1536]{2,1,0:T(8,128)(2,1)S(1)}, bf16[2,96,1536]{2,1,0:T(8,128)(2,1)S(1)}, u32[]{:S(2)}, u32[]{:S(2)}) %collective-permute-start.15) | collective-permute-done | bytes 589856 | tf_op jit(solution)/shard_map/ppermute | solution.py:70
  126.9 5.3 fusion.19.qi.ki.vi
  132.3 8.7 %shard_map.263 = (bf16[768,384]{1,0:T(8,128)(2,1)S(1)}, bf16[128,384]{1,0:T(8,128)(2,1)S(1)}, f32[3,2,896]{2,1,0:T(2,128)S(1)}) custom-call(bf16[768,1152]{1,0:T(8,128)(2,1)S(1)} %fusion.19.qi.ki.vi, bf16[128,1152]{1,0:T(8,128)(2,1)S(1)} %fusion.28.qt.kt.vt, bf16[768,1152]{1,0:T(8,128)(2,1)S(1)} %fusion.19.qi.ki.vi, bf16[128,1152]{1,0:T(8,128)(2,1)S(1)} %fusion.28.qt.kt.vt, ...), custom_call_target="tpu_custom_call" | custom-call | flops 4932501504 | bytes 3096576 | tf_op jit(solution)/shard_map/pallas_call | solution.py:446
  141.1 5.1 collective-permute-done.17
  149.2 3.5 fusion.53
  153.4 5.5 collective-permute-done.32.core
  161.3 11.6 %collective-permute-done.22 = bf16[2,192,1536]{2,1,0:T(8,128)(2,1)} collective-permute-done((bf16[2,192,1536]{2,1,0:T(8,128)(2,1)}, bf16[2,192,1536]{2,1,0:T(8,128)(2,1)}, u32[]{:S(2)}, u32[]{:S(2)}) %collective-permute-start.22) | collective-permute-done | bytes 1179680 | tf_op jit(solution)/shard_map/ppermute | solution.py:70
  175.6 4.3 broadcast.262.clone.2
  189.5 9.6 %collective-permute-done.27 = bf16[2,192,1536]{2,1,0:T(8,128)(2,1)S(1)} collective-permute-done((bf16[2,192,1536]{2,1,0:T(8,128)(2,1)}, bf16[2,192,1536]{2,1,0:T(8,128)(2,1)S(1)}, u32[]{:S(2)}, u32[]{:S(2)}) %collective-permute-start.27) | collective-permute-done | bytes 1179680 | tf_op jit(solution)/shard_map/ppermute | solution.py:70
  226.3 5.3 collective-permute-done.24.over_y
  232.5 3.4 collective-permute-done.34
  241.6 3.7 copy-done.37
  245.9 4.3 multiply_convert_fusion.1
  250.3 8.5 %multiply_convert_fusion = (bf16[768,1536]{1,0:T(8,128)(2,1)S(1)}, f32[768,1536]{1,0:T(8,128)}) fusion(f32[1536]{0:T(1024)S(1)} %get-tuple-element.386, bf16[768,1536]{1,0:T(8,128)(2,1)S(1)} %get-tuple-element.211, bf16[2,1536,1536]{2,1,0:T(8,128)(2,1)} %constant_dynamic-update-slice_fusion.9), kind=kOutput, calls=%fused_computation.20 | convolution fusion | flops 3635675136 | bytes 14161920 | tf_op jit(solution)/shard_map/dot_general | solution.py:33
  258.8 3.7 collective-permute-done.36
  266.6 4.1 convolution_convert_fusion.3
  270.9 17.5 %collective-permute-done.38 = bf16[2,192,1536]{2,1,0:T(8,128)(2,1)S(1)} collective-permute-done((bf16[2,192,1536]{2,1,0:T(8,128)(2,1)S(1)}, bf16[2,192,1536]{2,1,0:T(8,128)(2,1)S(1)}, u32[]{:S(2)}, u32[]{:S(2)}) %collective-permute-start.38) | collective-permute-done | bytes 1179680 | tf_op jit(solution)/shard_map/ppermute | solution.py:70
  291.6 10.1 %collective-permute-done.40 = bf16[2,96,1536]{2,1,0:T(8,128)(2,1)S(1)} collective-permute-done((bf16[2,96,1536]{2,1,0:T(8,128)(2,1)S(1)}, bf16[2,96,1536]{2,1,0:T(8,128)(2,1)S(1)}, u32[]{:S(2)}, u32[]{:S(2)}) %collective-permute-start.40) | collective-permute-done | bytes 589856 | tf_op jit(solution)/shard_map/ppermute | solution.py:70
  305.9 8.7 %convert_reduce_fusion = (f32[1536]{0:T(1024)}, bf16[768,1536]{1,0:T(8,128)(2,1)S(1)}) fusion(f32[768,1536]{1,0:T(8,128)} %get-tuple-element.517, f32[1536]{0:T(1024)S(1)} %get-tuple-element.386, bf16[768,1536]{1,0:T(8,128)(2,1)S(1)} %get-tuple-element.223, bf16[2,1536,1536]{2,1,0:T(8,128)(2,1)S(1)} %constant_dynamic-update-slice_fusion), kind=kOutput, calls=%fused_computation.19 | convolution fusion | flops 3651009024 | bytes 14170112 | tf_op jit(solution)/shard_map/dot_general | solution.py:33
  317.4 4.1 convert_reduce_fusion.3
  324.0 5.8 fusion.7
  331.9 4.6 fusion.10
  349.5 4.1 fusion.31.st
  353.6 4.8 collective-permute-done.47
  365.4 5.2 fusion.21.si
  372.3 3.6 convolution_convert_fusion.4
  375.9 5.6 convolution_convert_fusion.2
  381.6 8.6 %collective-permute-done.55 = bf16[2,192,1536]{2,1,0:T(8,128)(2,1)S(1)} collective-permute-done((bf16[2,192,1536]{2,1,0:T(8,128)(2,1)S(1)}, bf16[2,192,1536]{2,1,0:T(8,128)(2,1)S(1)}, u32[]{:S(2)}, u32[]{:S(2)}) %collective-permute-start.55) | collective-permute-done | bytes 1179680 | tf_op jit(solution)/shard_map/ppermute | solution.py:70
  402.4 3.4 fusion.13
  407.4 14.5 %collective-permute-done.57 = bf16[2,192,1536]{2,1,0:T(8,128)(2,1)} collective-permute-done((bf16[2,192,1536]{2,1,0:T(8,128)(2,1)}, bf16[2,192,1536]{2,1,0:T(8,128)(2,1)}, u32[]{:S(2)}, u32[]{:S(2)}) %collective-permute-start.57) | collective-permute-done | bytes 1179680 | tf_op jit(solution)/shard_map/ppermute | solution.py:70
  425.1 3.5 add_bitcast_fusion
  430.4 4.9 collective-permute-done.59
  448.0 16.4 %shard_map.268 = (bf16[768,1152]{1,0:T(8,128)(2,1)S(1)}, bf16[128,1152]{1,0:T(8,128)(2,1)S(1)}) custom-call(bf16[768,1152]{1,0:T(8,128)(2,1)S(1)} %copy-done.31, bf16[128,1152]{1,0:T(8,128)(2,1)S(1)} %copy-done.29, bf16[768,1152]{1,0:T(8,128)(2,1)S(1)} %copy-done.31, bf16[128,1152]{1,0:T(8,128)(2,1)S(1)} %copy-done.29, bf16[768,1152]{1,0:T(8,128)(2,1)S(1)} %copy-done.31, ...), custom_call_target="tpu_custom_call" | custom-call | flops 12331253760 | bytes 5160960 | tf_op jit(solution)/shard_map/pallas_call | solution.py:517
  473.3 5.1 fusion.20
  480.1 3.7 fusion.22
  484.6 3.2 fusion.29.st
  487.9 8.5 %collective-permute-done.51 = bf16[224,1536]{1,0:T(8,128)(2,1)S(1)} collective-permute-done((bf16[224,1536]{1,0:T(8,128)(2,1)S(1)}, bf16[224,1536]{1,0:T(8,128)(2,1)S(1)}, u32[]{:S(2)}, u32[]{:S(2)}) %collective-permute-start.51) | collective-permute-done | bytes 688160 | tf_op jit(solution)/shard_map/ppermute | solution.py:247
  501.5 3.7 convolution_add_fusion.2.si
  508.9 3.5 convolution_convert_fusion.1
  512.4 14.6 %collective-permute-done.71 = bf16[2,192,1536]{2,1,0:T(8,128)(2,1)S(1)} collective-permute-done((bf16[2,192,1536]{2,1,0:T(8,128)(2,1)S(1)}, bf16[2,192,1536]{2,1,0:T(8,128)(2,1)S(1)}, u32[]{:S(2)}, u32[]{:S(2)}) %collective-permute-start.71) | collective-permute-done | bytes 1179680 | tf_op jit(solution)/shard_map/ppermute | solution.py:70
  539.6 5.7 collective-permute-done.73
  563.0 11.7 %collective-permute-done.75 = bf16[2,192,1536]{2,1,0:T(8,128)(2,1)} collective-permute-done((bf16[2,192,1536]{2,1,0:T(8,128)(2,1)}, bf16[2,192,1536]{2,1,0:T(8,128)(2,1)}, u32[]{:S(2)}, u32[]{:S(2)}) %collective-permute-start.75) | collective-permute-done | bytes 1179680 | tf_op jit(solution)/shard_map/ppermute | solution.py:70
  592.9 3.3 convolution_bitcast_fusion
  620.7 24.1 %collective-permute-done.85 = f32[4,192]{1,0:T(4,128)S(1)} collective-permute-done((f32[4,192]{1,0:T(4,128)S(1)}, f32[4,192]{1,0:T(4,128)S(1)}, u32[]{:S(2)}, u32[]{:S(2)}) %collective-permute-start.85) | collective-permute-done | bytes 3104 | tf_op jit(solution)/shard_map/ppermute | solution.py:215
  (642 shorter events, 285.9 us)
Async XLA Ops:
  3.1 19.3 %collective-permute-start = (f32[4,2,2304]{2,0,1:T(4,128)}, f32[4,2,2304]{2,0,1:T(4,128)}, u32[]{:S(2)}, u32[]{:S(2)}) collective-permute-start(f32[4,2,2304]{2,0,1:T(4,128)} %select_bitcast_fusion), channel_id=1, source_target_pairs={{0,4},{4,0},{8,12},{12,8},{16,20},{20,16},{24,28},{28,24},{1,5},{5... | collective-permute-start | bytes 221192 | tf_op jit(solution)/shard_map/ppermute | solution.py:179
  12.5 29.8 %collective-permute-start.2 = (bf16[2,192,1536]{2,1,0:T(8,128)(2,1)}, bf16[2,192,1536]{2,1,0:T(8,128)(2,1)}, u32[]{:S(2)}, u32[]{:S(2)}) collective-permute-start(bf16[2,192,1536]{2,1,0:T(8,128)(2,1)} %pad_maximum_fusion), channel_id=1, source_target_pairs={{0,8},{8,16},{16,24},{24,28},{28,20},{20,12},{12,4},{4,0},{1,9},{9... | collective-permute-start | bytes 3538952 | tf_op jit(solution)/shard_map/ppermute | solution.py:70
  14.1 28.2 %collective-permute-start.3 = (bf16[2,192,1536]{2,1,0:T(8,128)(2,1)}, bf16[2,192,1536]{2,1,0:T(8,128)(2,1)}, u32[]{:S(2)}, u32[]{:S(2)}) collective-permute-start(bf16[2,192,1536]{2,1,0:T(8,128)(2,1)} %pad_maximum_fusion), channel_id=1, source_target_pairs={{0,4},{8,0},{16,8},{24,16},{28,24},{20,28},{12,20},{4,12},{1,5},{9... | collective-permute-start | bytes 3538952 | tf_op jit(solution)/shard_map/ppermute | solution.py:73
  45.3 28.8 %collective-permute-start.11 = (bf16[2,192,1536]{2,1,0:T(8,128)(2,1)}, bf16[2,192,1536]{2,1,0:T(8,128)(2,1)}, u32[]{:S(2)}, u32[]{:S(2)}) collective-permute-start(bf16[2,192,1536]{2,1,0:T(8,128)(2,1)} %collective-permute-done.2), channel_id=1, source_target_pairs={{0,8},{8,16},{16,24},{24,28},{28,20},{20,12},{12,4},{4,0},{1,9},{9... | collective-permute-start | bytes 3538952 | tf_op jit(solution)/shard_map/ppermute | solution.py:70
  45.6 28.4 %collective-permute-start.12 = (bf16[2,192,1536]{2,1,0:T(8,128)(2,1)}, bf16[2,192,1536]{2,1,0:T(8,128)(2,1)}, u32[]{:S(2)}, u32[]{:S(2)}) collective-permute-start(bf16[2,192,1536]{2,1,0:T(8,128)(2,1)} %collective-permute-done.3), channel_id=1, source_target_pairs={{0,4},{8,0},{16,8},{24,16},{28,24},{20,28},{12,20},{4,12},{1,5},{9... | collective-permute-start | bytes 3538952 | tf_op jit(solution)/shard_map/ppermute | solution.py:73
  61.0 19.9 %collective-permute-start.9 = (bf16[224,1536]{1,0:T(8,128)(2,1)S(1)}, bf16[224,1536]{1,0:T(8,128)(2,1)S(1)}, u32[]{:S(2)}, u32[]{:S(2)}) collective-permute-start(bf16[224,1536]{1,0:T(8,128)(2,1)S(1)} %pad_maximum_fusion.2.own), channel_id=1, source_target_pairs={{0,1},{1,0},{2,3},{3,2},{4,5},{5,4},{6,7},{7,6},{8,9},{9,8},{10,11... | collective-permute-start | bytes 2064392 | tf_op jit(solution)/shard_map/ppermute | solution.py:243
  74.0 28.6 %collective-permute-start.13 = (bf16[2,192,1536]{2,1,0:T(8,128)(2,1)}, bf16[2,192,1536]{2,1,0:T(8,128)(2,1)S(1)}, u32[]{:S(2)}, u32[]{:S(2)}) collective-permute-start(bf16[2,192,1536]{2,1,0:T(8,128)(2,1)} %collective-permute-done.11), channel_id=1, source_target_pairs={{0,8},{8,16},{16,24},{24,28},{28,20},{20,12},{12,4},{4,0},{1,9},{9... | collective-permute-start | bytes 3538952 | tf_op jit(solution)/shard_map/ppermute | solution.py:70
  74.6 29.1 %collective-permute-start.14 = (bf16[2,192,1536]{2,1,0:T(8,128)(2,1)}, bf16[2,192,1536]{2,1,0:T(8,128)(2,1)S(1)}, u32[]{:S(2)}, u32[]{:S(2)}) collective-permute-start(bf16[2,192,1536]{2,1,0:T(8,128)(2,1)} %collective-permute-done.12), channel_id=1, source_target_pairs={{0,4},{8,0},{16,8},{24,16},{28,24},{20,28},{12,20},{4,12},{1,5},{9... | collective-permute-start | bytes 3538952 | tf_op jit(solution)/shard_map/ppermute | solution.py:73
  105.9 47.3 %collective-permute-start.31 = (bf16[224,1536]{1,0:T(8,128)(2,1)S(1)}, bf16[224,1536]{1,0:T(8,128)(2,1)}, u32[]{:S(2)}, u32[]{:S(2)}) collective-permute-start(bf16[224,1536]{1,0:T(8,128)(2,1)S(1)} %constant_dynamic-update-slice_fusion.37.own), channel_id=1, source_target_pairs={{0,2},{1,3},{2,0},{3,1},{4,6},{5,7},{6,4},{7,5},{8,10},{9,11},{10,... | collective-permute-start | bytes 2064392 | tf_op jit(solution)/shard_map/ppermute | solution.py:247
  119.9 26.2 %collective-permute-start.17 = (bf16[2,192,1536]{2,1,0:T(8,128)(2,1)S(1)}, bf16[2,192,1536]{2,1,0:T(8,128)(2,1)}, u32[]{:S(2)}, u32[]{:S(2)}) collective-permute-start(bf16[2,192,1536]{2,1,0:T(8,128)(2,1)S(1)} %bitcast.365), channel_id=1, source_target_pairs={{0,8},{8,16},{16,24},{24,28},{28,20},{20,12},{12,4},{4,0},{1,9},{9... | collective-permute-start | bytes 3538952 | tf_op jit(solution)/shard_map/ppermute | solution.py:70
  120.5 26.7 %collective-permute-start.18 = (bf16[2,192,1536]{2,1,0:T(8,128)(2,1)S(1)}, bf16[2,192,1536]{2,1,0:T(8,128)(2,1)}, u32[]{:S(2)}, u32[]{:S(2)}) collective-permute-start(bf16[2,192,1536]{2,1,0:T(8,128)(2,1)S(1)} %bitcast.366), channel_id=1, source_target_pairs={{0,4},{8,0},{16,8},{24,16},{28,24},{20,28},{12,20},{4,12},{1,5},{9... | collective-permute-start | bytes 3538952 | tf_op jit(solution)/shard_map/ppermute | solution.py:73
  147.2 25.7 %collective-permute-start.22 = (bf16[2,192,1536]{2,1,0:T(8,128)(2,1)}, bf16[2,192,1536]{2,1,0:T(8,128)(2,1)}, u32[]{:S(2)}, u32[]{:S(2)}) collective-permute-start(bf16[2,192,1536]{2,1,0:T(8,128)(2,1)} %collective-permute-done.17), channel_id=1, source_target_pairs={{0,8},{8,16},{16,24},{24,28},{28,20},{20,12},{12,4},{4,0},{1,9},{9... | collective-permute-start | bytes 3538952 | tf_op jit(solution)/shard_map/ppermute | solution.py:70
  147.8 25.8 %collective-permute-start.23 = (bf16[2,192,1536]{2,1,0:T(8,128)(2,1)}, bf16[2,192,1536]{2,1,0:T(8,128)(2,1)}, u32[]{:S(2)}, u32[]{:S(2)}) collective-permute-start(bf16[2,192,1536]{2,1,0:T(8,128)(2,1)} %collective-permute-done.18), channel_id=1, source_target_pairs={{0,4},{8,0},{16,8},{24,16},{28,24},{20,28},{12,20},{4,12},{1,5},{9... | collective-permute-start | bytes 3538952 | tf_op jit(solution)/shard_map/ppermute | solution.py:73
  152.7 49.3 %collective-permute-start.19 = (f32[384,1536]{1,0:T(8,128)}, f32[384,1536]{1,0:T(8,128)}, u32[]{:S(2)}, u32[]{:S(2)}) collective-permute-start(f32[384,1536]{1,0:T(8,128)} %fusion.53), channel_id=1, source_target_pairs={{0,1},{1,0},{2,3},{3,2},{4,5},{5,4},{6,7},{7,6},{8,9},{9,8},{10,11... | collective-permute-start | bytes 7077896 | tf_op jit(solution)/shard_map/ppermute | solution.py:243
  173.6 25.4 %collective-permute-start.27 = (bf16[2,192,1536]{2,1,0:T(8,128)(2,1)}, bf16[2,192,1536]{2,1,0:T(8,128)(2,1)S(1)}, u32[]{:S(2)}, u32[]{:S(2)}) collective-permute-start(bf16[2,192,1536]{2,1,0:T(8,128)(2,1)} %collective-permute-done.22), channel_id=1, source_target_pairs={{0,8},{8,16},{16,24},{24,28},{28,20},{20,12},{12,4},{4,0},{1,9},{9... | collective-permute-start | bytes 3538952 | tf_op jit(solution)/shard_map/ppermute | solution.py:70
  173.9 25.9 %collective-permute-start.28 = (bf16[2,192,1536]{2,1,0:T(8,128)(2,1)}, bf16[2,192,1536]{2,1,0:T(8,128)(2,1)S(1)}, u32[]{:S(2)}, u32[]{:S(2)}) collective-permute-start(bf16[2,192,1536]{2,1,0:T(8,128)(2,1)} %collective-permute-done.23), channel_id=1, source_target_pairs={{0,4},{8,0},{16,8},{24,16},{28,24},{20,28},{12,20},{4,12},{1,5},{9... | collective-permute-start | bytes 3538952 | tf_op jit(solution)/shard_map/ppermute | solution.py:73
  213.1 22.8 %collective-permute-start.34 = (bf16[2,192,1536]{2,1,0:T(8,128)(2,1)}, bf16[2,192,1536]{2,1,0:T(8,128)(2,1)}, u32[]{:S(2)}, u32[]{:S(2)}) collective-permute-start(bf16[2,192,1536]{2,1,0:T(8,128)(2,1)} %bitcast.27), channel_id=1, source_target_pairs={{0,8},{8,16},{16,24},{24,28},{28,20},{20,12},{12,4},{4,0},{1,9},{9... | collective-permute-start | bytes 3538952 | tf_op jit(solution)/shard_map/ppermute | solution.py:70
  213.5 23.2 %collective-permute-start.35 = (bf16[2,192,1536]{2,1,0:T(8,128)(2,1)}, bf16[2,192,1536]{2,1,0:T(8,128)(2,1)}, u32[]{:S(2)}, u32[]{:S(2)}) collective-permute-start(bf16[2,192,1536]{2,1,0:T(8,128)(2,1)} %bitcast.27), channel_id=1, source_target_pairs={{0,4},{8,0},{16,8},{24,16},{28,24},{20,28},{12,20},{4,12},{1,5},{9... | collective-permute-start | bytes 3538952 | tf_op jit(solution)/shard_map/ppermute | solution.py:73
  236.8 25.7 %collective-permute-start.36 = (bf16[2,192,1536]{2,1,0:T(8,128)(2,1)}, bf16[2,192,1536]{2,1,0:T(8,128)(2,1)S(1)}, u32[]{:S(2)}, u32[]{:S(2)}) collective-permute-start(bf16[2,192,1536]{2,1,0:T(8,128)(2,1)} %collective-permute-done.34), channel_id=1, source_target_pairs={{0,8},{8,16},{16,24},{24,28},{28,20},{20,12},{12,4},{4,0},{1,9},{9... | collective-permute-start | bytes 3538952 | tf_op jit(solution)/shard_map/ppermute | solution.py:70
  237.1 26.1 %collective-permute-start.37 = (bf16[2,192,1536]{2,1,0:T(8,128)(2,1)}, bf16[2,192,1536]{2,1,0:T(8,128)(2,1)S(1)}, u32[]{:S(2)}, u32[]{:S(2)}) collective-permute-start(bf16[2,192,1536]{2,1,0:T(8,128)(2,1)} %collective-permute-done.35), channel_id=1, source_target_pairs={{0,4},{8,0},{16,8},{24,16},{28,24},{20,28},{12,20},{4,12},{1,5},{9... | collective-permute-start | bytes 3538952 | tf_op jit(solution)/shard_map/ppermute | solution.py:73
  263.2 25.3 %collective-permute-start.38 = (bf16[2,192,1536]{2,1,0:T(8,128)(2,1)S(1)}, bf16[2,192,1536]{2,1,0:T(8,128)(2,1)S(1)}, u32[]{:S(2)}, u32[]{:S(2)}) collective-permute-start(bf16[2,192,1536]{2,1,0:T(8,128)(2,1)S(1)} %collective-permute-done.36), channel_id=1, source_target_pairs={{0,8},{8,16},{16,24},{24,28},{28,20},{20,12},{12,4},{4,0},{1,9},{9... | collective-permute-start | bytes 3538952 | tf_op jit(solution)/shard_map/ppermute | solution.py:70
  263.4 25.6 %collective-permute-start.39 = (bf16[2,192,1536]{2,1,0:T(8,128)(2,1)S(1)}, bf16[2,192,1536]{2,1,0:T(8,128)(2,1)S(1)}, u32[]{:S(2)}, u32[]{:S(2)}) collective-permute-start(bf16[2,192,1536]{2,1,0:T(8,128)(2,1)S(1)} %collective-permute-done.37), channel_id=1, source_target_pairs={{0,4},{8,0},{16,8},{24,16},{28,24},{20,28},{12,20},{4,12},{1,5},{9... | collective-permute-start | bytes 3538952 | tf_op jit(solution)/shard_map/ppermute | solution.py:73
  302.4 19.1 %collective-permute-start.42 = (bf16[2,96,1536]{2,1,0:T(8,128)(2,1)S(1)}, bf16[2,96,1536]{2,1,0:T(8,128)(2,1)S(1)}, u32[]{:S(2)}, u32[]{:S(2)}) collective-permute-start(bf16[2,96,1536]{2,1,0:T(8,128)(2,1)S(1)} %pad_maximum_fusion.7), channel_id=1, source_target_pairs={{0,8},{8,16},{16,24},{24,28},{28,20},{20,12},{12,4},{4,0},{1,9},{9... | collective-permute-start | bytes 1769480 | tf_op jit(solution)/shard_map/ppermute | solution.py:70
  329.8 35.6 %collective-permute-start.44 = (f32[384,1536]{1,0:T(8,128)}, f32[384,1536]{1,0:T(8,128)}, u32[]{:S(2)}, u32[]{:S(2)}) collective-permute-start(f32[384,1536]{1,0:T(8,128)} %fusion.7), channel_id=1, source_target_pairs={{0,1},{1,0},{2,3},{3,2},{4,5},{5,4},{6,7},{7,6},{8,9},{9,8},{10,11... | collective-permute-start | bytes 7077896 | tf_op jit(solution)/shard_map/ppermute | solution.py:243
  329.8 28.7 %collective-permute-start.47 = (bf16[2,192,1536]{2,1,0:T(8,128)(2,1)}, bf16[2,192,1536]{2,1,0:T(8,128)(2,1)}, u32[]{:S(2)}, u32[]{:S(2)}) collective-permute-start(bf16[2,192,1536]{2,1,0:T(8,128)(2,1)} %add_convert_fusion.17), channel_id=1, source_target_pairs={{0,8},{8,16},{16,24},{24,28},{28,20},{20,12},{12,4},{4,0},{1,9},{9... | collective-permute-start | bytes 3538952 | tf_op jit(solution)/shard_map/ppermute | solution.py:70
  330.3 29.0 %collective-permute-start.48 = (bf16[2,192,1536]{2,1,0:T(8,128)(2,1)}, bf16[2,192,1536]{2,1,0:T(8,128)(2,1)}, u32[]{:S(2)}, u32[]{:S(2)}) collective-permute-start(bf16[2,192,1536]{2,1,0:T(8,128)(2,1)} %add_convert_fusion.16), channel_id=1, source_target_pairs={{0,4},{8,0},{16,8},{24,16},{28,24},{20,28},{12,20},{4,12},{1,5},{9... | collective-permute-start | bytes 3538952 | tf_op jit(solution)/shard_map/ppermute | solution.py:73
  362.6 27.6 %collective-permute-start.55 = (bf16[2,192,1536]{2,1,0:T(8,128)(2,1)S(1)}, bf16[2,192,1536]{2,1,0:T(8,128)(2,1)S(1)}, u32[]{:S(2)}, u32[]{:S(2)}) collective-permute-start(bf16[2,192,1536]{2,1,0:T(8,128)(2,1)S(1)} %add_convert_fusion.15), channel_id=1, source_target_pairs={{0,8},{8,16},{16,24},{24,28},{28,20},{20,12},{12,4},{4,0},{1,9},{9... | collective-permute-start | bytes 3538952 | tf_op jit(solution)/shard_map/ppermute | solution.py:70
  365.0 27.6 %collective-permute-start.56 = (bf16[2,192,1536]{2,1,0:T(8,128)(2,1)S(1)}, bf16[2,192,1536]{2,1,0:T(8,128)(2,1)S(1)}, u32[]{:S(2)}, u32[]{:S(2)}) collective-permute-start(bf16[2,192,1536]{2,1,0:T(8,128)(2,1)S(1)} %add_convert_fusion.14), channel_id=1, source_target_pairs={{0,4},{8,0},{16,8},{24,16},{28,24},{20,28},{12,20},{4,12},{1,5},{9... | collective-permute-start | bytes 3538952 | tf_op jit(solution)/shard_map/ppermute | solution.py:73
  370.7 26.6 %collective-permute-start.46 = (bf16[224,1536]{1,0:T(8,128)(2,1)S(1)}, bf16[224,1536]{1,0:T(8,128)(2,1)S(1)}, u32[]{:S(2)}, u32[]{:S(2)}) collective-permute-start(bf16[224,1536]{1,0:T(8,128)(2,1)S(1)} %pad_maximum_fusion.4), channel_id=1, source_target_pairs={{0,2},{1,3},{2,0},{3,1},{4,6},{5,7},{6,4},{7,5},{8,10},{9,11},{10,... | collective-permute-start | bytes 2064392 | tf_op jit(solution)/shard_map/ppermute | solution.py:247
  395.3 26.7 %collective-permute-start.57 = (bf16[2,192,1536]{2,1,0:T(8,128)(2,1)}, bf16[2,192,1536]{2,1,0:T(8,128)(2,1)}, u32[]{:S(2)}, u32[]{:S(2)}) collective-permute-start(bf16[2,192,1536]{2,1,0:T(8,128)(2,1)} %add_convert_fusion.13), channel_id=1, source_target_pairs={{0,8},{8,16},{16,24},{24,28},{28,20},{20,12},{12,4},{4,0},{1,9},{9... | collective-permute-start | bytes 3538952 | tf_op jit(solution)/shard_map/ppermute | solution.py:70
  396.7 26.1 %collective-permute-start.58 = (bf16[2,192,1536]{2,1,0:T(8,128)(2,1)}, bf16[2,192,1536]{2,1,0:T(8,128)(2,1)}, u32[]{:S(2)}, u32[]{:S(2)}) collective-permute-start(bf16[2,192,1536]{2,1,0:T(8,128)(2,1)} %add_convert_fusion.12), channel_id=1, source_target_pairs={{0,4},{8,0},{16,8},{24,16},{28,24},{20,28},{12,20},{4,12},{1,5},{9... | collective-permute-start | bytes 3538952 | tf_op jit(solution)/shard_map/ppermute | solution.py:73
  398.6 30.4 %collective-permute-start.52 = (bf16[224,1536]{1,0:T(8,128)(2,1)S(1)}, bf16[224,1536]{1,0:T(8,128)(2,1)S(1)}, u32[]{:S(2)}, u32[]{:S(2)}) collective-permute-start(bf16[224,1536]{1,0:T(8,128)(2,1)S(1)} %get-tuple-element.257.own), channel_id=1, source_target_pairs={{0,2},{1,3},{2,0},{3,1},{4,6},{5,7},{6,4},{7,5},{8,10},{9,11},{10,... | collective-permute-start | bytes 2064392 | tf_op jit(solution)/shard_map/ppermute | solution.py:247
  400.2 40.2 %collective-permute-start.53 = (bf16[224,1536]{1,0:T(8,128)(2,1)S(1)}, bf16[224,1536]{1,0:T(8,128)(2,1)S(1)}, u32[]{:S(2)}, u32[]{:S(2)}) collective-permute-start(bf16[224,1536]{1,0:T(8,128)(2,1)S(1)} %get-tuple-element.257.own), channel_id=1, source_target_pairs={{0,1},{1,0},{2,3},{3,2},{4,5},{5,4},{6,7},{7,6},{8,9},{9,8},{10,11... | collective-permute-start | bytes 2064392 | tf_op jit(solution)/shard_map/ppermute | solution.py:243
  405.8 67.5 %collective-permute-start.49 = (f32[384,1536]{1,0:T(8,128)}, f32[384,1536]{1,0:T(8,128)}, u32[]{:S(2)}, u32[]{:S(2)}) collective-permute-start(f32[384,1536]{1,0:T(8,128)} %fusion.13), channel_id=1, source_target_pairs={{0,1},{1,0},{2,3},{3,2},{4,5},{5,4},{6,7},{7,6},{8,9},{9,8},{10,11... | collective-permute-start | bytes 7077896 | tf_op jit(solution)/shard_map/ppermute | solution.py:243
  438.3 26.1 %collective-permute-start.61 = (bf16[2,192,1536]{2,1,0:T(8,128)(2,1)}, bf16[2,192,1536]{2,1,0:T(8,128)(2,1)}, u32[]{:S(2)}, u32[]{:S(2)}) collective-permute-start(bf16[2,192,1536]{2,1,0:T(8,128)(2,1)} %add_convert_fusion.11), channel_id=1, source_target_pairs={{0,8},{8,16},{16,24},{24,28},{28,20},{20,12},{12,4},{4,0},{1,9},{9... | collective-permute-start | bytes 3538952 | tf_op jit(solution)/shard_map/ppermute | solution.py:70
  439.3 25.1 %collective-permute-start.62 = (bf16[2,192,1536]{2,1,0:T(8,128)(2,1)}, bf16[2,192,1536]{2,1,0:T(8,128)(2,1)}, u32[]{:S(2)}, u32[]{:S(2)}) collective-permute-start(bf16[2,192,1536]{2,1,0:T(8,128)(2,1)} %add_convert_fusion.10), channel_id=1, source_target_pairs={{0,4},{8,0},{16,8},{24,16},{28,24},{20,28},{12,20},{4,12},{1,5},{9... | collective-permute-start | bytes 3538952 | tf_op jit(solution)/shard_map/ppermute | solution.py:73
  467.7 31.1 %collective-permute-start.66 = (bf16[2,192,1536]{2,1,0:T(8,128)(2,1)S(1)}, bf16[2,192,1536]{2,1,0:T(8,128)(2,1)S(1)}, u32[]{:S(2)}, u32[]{:S(2)}) collective-permute-start(bf16[2,192,1536]{2,1,0:T(8,128)(2,1)S(1)} %add_convert_fusion.9), channel_id=1, source_target_pairs={{0,8},{8,16},{16,24},{24,28},{28,20},{20,12},{12,4},{4,0},{1,9},{9... | collective-permute-start | bytes 3538952 | tf_op jit(solution)/shard_map/ppermute | solution.py:70
  468.8 30.0 %collective-permute-start.67 = (bf16[2,192,1536]{2,1,0:T(8,128)(2,1)S(1)}, bf16[2,192,1536]{2,1,0:T(8,128)(2,1)S(1)}, u32[]{:S(2)}, u32[]{:S(2)}) collective-permute-start(bf16[2,192,1536]{2,1,0:T(8,128)(2,1)S(1)} %add_convert_fusion.8), channel_id=1, source_target_pairs={{0,4},{8,0},{16,8},{24,16},{28,24},{20,28},{12,20},{4,12},{1,5},{9... | collective-permute-start | bytes 3538952 | tf_op jit(solution)/shard_map/ppermute | solution.py:73
  499.4 27.6 %collective-permute-start.71 = (bf16[2,192,1536]{2,1,0:T(8,128)(2,1)S(1)}, bf16[2,192,1536]{2,1,0:T(8,128)(2,1)S(1)}, u32[]{:S(2)}, u32[]{:S(2)}) collective-permute-start(bf16[2,192,1536]{2,1,0:T(8,128)(2,1)S(1)} %add_convert_fusion.7), channel_id=1, source_target_pairs={{0,8},{8,16},{16,24},{24,28},{28,20},{20,12},{12,4},{4,0},{1,9},{9... | collective-permute-start | bytes 3538952 | tf_op jit(solution)/shard_map/ppermute | solution.py:70
  500.5 27.3 %collective-permute-start.72 = (bf16[2,192,1536]{2,1,0:T(8,128)(2,1)S(1)}, bf16[2,192,1536]{2,1,0:T(8,128)(2,1)S(1)}, u32[]{:S(2)}, u32[]{:S(2)}) collective-permute-start(bf16[2,192,1536]{2,1,0:T(8,128)(2,1)S(1)} %add_convert_fusion.6), channel_id=1, source_target_pairs={{0,4},{8,0},{16,8},{24,16},{28,24},{20,28},{12,20},{4,12},{1,5},{9... | collective-permute-start | bytes 3538952 | tf_op jit(solution)/shard_map/ppermute | solution.py:73
  505.4 46.2 %collective-permute-start.65 = (bf16[224,1536]{1,0:T(8,128)(2,1)S(1)}, bf16[224,1536]{1,0:T(8,128)(2,1)S(1)}, u32[]{:S(2)}, u32[]{:S(2)}) collective-permute-start(bf16[224,1536]{1,0:T(8,128)(2,1)S(1)} %pad_maximum_fusion.6), channel_id=1, source_target_pairs={{0,2},{1,3},{2,0},{3,1},{4,6},{5,7},{6,4},{7,5},{8,10},{9,11},{10,... | collective-permute-start | bytes 2064392 | tf_op jit(solution)/shard_map/ppermute | solution.py:247
  548.7 26.0 %collective-permute-start.75 = (bf16[2,192,1536]{2,1,0:T(8,128)(2,1)}, bf16[2,192,1536]{2,1,0:T(8,128)(2,1)}, u32[]{:S(2)}, u32[]{:S(2)}) collective-permute-start(bf16[2,192,1536]{2,1,0:T(8,128)(2,1)} %add_convert_fusion.5), channel_id=1, source_target_pairs={{0,8},{8,16},{16,24},{24,28},{28,20},{20,12},{12,4},{4,0},{1,9},{9... | collective-permute-start | bytes 3538952 | tf_op jit(solution)/shard_map/ppermute | solution.py:70
  549.4 25.3 %collective-permute-start.76 = (bf16[2,192,1536]{2,1,0:T(8,128)(2,1)}, bf16[2,192,1536]{2,1,0:T(8,128)(2,1)}, u32[]{:S(2)}, u32[]{:S(2)}) collective-permute-start(bf16[2,192,1536]{2,1,0:T(8,128)(2,1)} %add_convert_fusion.4), channel_id=1, source_target_pairs={{0,4},{8,0},{16,8},{24,16},{28,24},{20,28},{12,20},{4,12},{1,5},{9... | collective-permute-start | bytes 3538952 | tf_op jit(solution)/shard_map/ppermute | solution.py:73
  584.7 28.4 %collective-permute-start.86 = (bf16[2,192,1536]{2,1,0:T(8,128)(2,1)}, bf16[2,192,1536]{2,1,0:T(8,128)(2,1)}, u32[]{:S(2)}, u32[]{:S(2)}) collective-permute-start(bf16[2,192,1536]{2,1,0:T(8,128)(2,1)} %add_convert_fusion.3), channel_id=1, source_target_pairs={{0,8},{8,16},{16,24},{24,28},{28,20},{20,12},{12,4},{4,0},{1,9},{9... | collective-permute-start | bytes 3538952 | tf_op jit(solution)/shard_map/ppermute | solution.py:70
  587.0 26.0 %collective-permute-start.87 = (bf16[2,192,1536]{2,1,0:T(8,128)(2,1)}, bf16[2,192,1536]{2,1,0:T(8,128)(2,1)}, u32[]{:S(2)}, u32[]{:S(2)}) collective-permute-start(bf16[2,192,1536]{2,1,0:T(8,128)(2,1)} %add_convert_fusion.2), channel_id=1, source_target_pairs={{0,4},{8,0},{16,8},{24,16},{28,24},{20,28},{12,20},{4,12},{1,5},{9... | collective-permute-start | bytes 3538952 | tf_op jit(solution)/shard_map/ppermute | solution.py:73
  618.3 28.1 %collective-permute-start.88 = (bf16[2,192,1536]{2,1,0:T(8,128)(2,1)}, bf16[2,192,1536]{2,1,0:T(8,128)(2,1)}, u32[]{:S(2)}, u32[]{:S(2)}) collective-permute-start(bf16[2,192,1536]{2,1,0:T(8,128)(2,1)} %add_convert_fusion.1), channel_id=1, source_target_pairs={{0,8},{8,16},{16,24},{24,28},{28,20},{20,12},{12,4},{4,0},{1,9},{9... | collective-permute-start | bytes 3538952 | tf_op jit(solution)/shard_map/ppermute | solution.py:70
  618.3 28.1 %collective-permute-start.89 = (bf16[2,192,1536]{2,1,0:T(8,128)(2,1)}, bf16[2,192,1536]{2,1,0:T(8,128)(2,1)}, u32[]{:S(2)}, u32[]{:S(2)}) collective-permute-start(bf16[2,192,1536]{2,1,0:T(8,128)(2,1)} %add_convert_fusion), channel_id=1, source_target_pairs={{0,4},{8,0},{16,8},{24,16},{28,24},{20,28},{12,20},{4,12},{1,5},{9... | collective-permute-start | bytes 3538952 | tf_op jit(solution)/shard_map/ppermute | solution.py:73
  620.4 24.4 %collective-permute-start.85 = (f32[4,192]{1,0:T(4,128)S(1)}, f32[4,192]{1,0:T(4,128)S(1)}, u32[]{:S(2)}, u32[]{:S(2)}) collective-permute-start(f32[4,192]{1,0:T(4,128)S(1)} %bitcast.375), channel_id=1, source_target_pairs={{0,4},{4,0},{8,12},{12,8},{16,20},{20,16},{24,28},{28,24},{1,5},{5... | collective-permute-start | bytes 9224 | tf_op jit(solution)/shard_map/ppermute | solution.py:215
  (153 other events, 1864.6 us)

commit v4 on v3

--- a/solution.py
+++ b/solution.py
@@ -686,7 +686,7 @@
         qkv_w_grad.append(mm_tn(full_one[s], late_grads[s]).astype(BF16))
         summed = jnp.sum(late_grads[s], axis=0, dtype=F32).reshape(3, heads_width)
         qv_b_grad.append(jnp.stack([summed[0], summed[2]]))
-    late_dz = later(dz_full, up_marks[0])
+    late_dz = later(dz_full, up_sent[3])
     out_w_grad = [mm_tn(late_dz[s], attn[s]).astype(BF16) for s in both]
     late_acts = later(acts, (dz_sent,))
     mlp_sums, cross_out = reduce_rows(

time: 660 us -> 656 us (level)
  waiting for transfers between devices: 256 us -> 248 us
    ppermute x24, waiting for transfers between devices: 156 us -> 149 us  [right(): return lax.ppermute(value, 'dp', self.right_pairs)]
    unnamed x234 -> x240, local copies, waits for them, and re-layouts: 13.4 us -> 13.1 us
  transfers between devices with their start and end apart: 90 -> 90, of which waited for: 51 -> 50; matrix products, arithmetic and copies ran while one was open for 38% -> 38% of each run, Pallas kernels for 5% -> 5%
where the time goes in v4:
time: 656 us; the launch traced here: 647 us
  waiting for transfers between devices  248 us (38%)
  matrix products  126 us (19%)
  local copies, waits for them, and re-layouts  90.3 us (14%)
  starting transfers between devices  86 us (13%)
  other arithmetic  58.9 us (9%)
  Pallas kernels  34.4 us (5%)
    ppermute x24, waiting for transfers between devices, right(): return lax.ppermute(value, 'dp', self.right_pairs)  149 us
    dot_general x32, matrix products, dot(): lax.dot_general(left, right, (dims, ((), ())), preferred_element_type=F32)  121 us
    dynamic_update_slice x27, local copies, waits for them, and re-layouts, put(): lax.dynamic_update_slice(whole, piece, (0, self.owner(offset) * rows + st...  35.3 us
    ppermute x24, starting transfers between devices, left(): return lax.ppermute(value, 'dp', self.left_pairs)  31 us
    ppermute x8, waiting for transfers between devices, swap_y(): return lax.ppermute(value, 'tensor', flip_pairs(4, 2))  28.5 us
    ppermute x2, waiting for transfers between devices, swap_low(): return lax.ppermute(value, 'dp', flip_pairs(self.count, 1))  24.6 us
    ppermute x24, starting transfers between devices, right(): return lax.ppermute(value, 'dp', self.right_pairs)  20 us
    ppermute x3, waiting for transfers between devices, small_scatter(): rest = mine + lax.ppermute(other, axis, flip_pairs(count, bit))  17 us
  transfers between devices with their start and end apart: 90, of which 50 were waited for; matrix products, arithmetic and copies ran while one was open for 38% of the time, Pallas kernels for 5%

profile of v4, /device:TPU:0, one launch (start us, length us, event | category | flops | bytes accessed | tf_op | source)
XLA Modules:
  0.0 647.5 jit_solution(25563004047851952)
XLA Ops:
  15.4 4.1 broadcast.262.clone.1
  25.3 17.0 %collective-permute-done.1 = f32[2,2,2304]{2,1,0:T(2,128)S(1)} collective-permute-done((f32[2,2,2304]{2,1,0:T(2,128)S(1)}, f32[2,2,2304]{2,1,0:T(2,128)S(1)}, u32[]{:S(2)}, u32[]{:S(2)}) %collective-permute-start.1) | collective-permute-done | bytes 36896 | tf_op jit(solution)/shard_map/ppermute | solution.py:179
  61.1 12.9 %collective-permute-done.8.over_y = bf16[224,1536]{1,0:T(8,128)(2,1)S(1)} collective-permute-done((bf16[224,1536]{1,0:T(8,128)(2,1)S(1)}, bf16[224,1536]{1,0:T(8,128)(2,1)S(1)}, u32[]{:S(2)}, u32[]{:S(2)}) %collective-permute-start.8) | collective-permute-done | bytes 688160 | tf_op jit(solution)/shard_map/ppermute | solution.py:247
  81.6 21.0 %collective-permute-done.13 = bf16[2,192,1536]{2,1,0:T(8,128)(2,1)S(1)} collective-permute-done((bf16[2,192,1536]{2,1,0:T(8,128)(2,1)}, bf16[2,192,1536]{2,1,0:T(8,128)(2,1)S(1)}, u32[]{:S(2)}, u32[]{:S(2)}) %collective-permute-start.13) | collective-permute-done | bytes 1179680 | tf_op jit(solution)/shard_map/ppermute | solution.py:70
  109.7 9.1 %collective-permute-done.15 = bf16[2,96,1536]{2,1,0:T(8,128)(2,1)S(1)} collective-permute-done((bf16[2,96,1536]{2,1,0:T(8,128)(2,1)S(1)}, bf16[2,96,1536]{2,1,0:T(8,128)(2,1)S(1)}, u32[]{:S(2)}, u32[]{:S(2)}) %collective-permute-start.15) | collective-permute-done | bytes 589856 | tf_op jit(solution)/shard_map/ppermute | solution.py:70
  126.6 5.3 fusion.19.qi.ki.vi
  132.0 8.7 %shard_map.263 = (bf16[768,384]{1,0:T(8,128)(2,1)S(1)}, bf16[128,384]{1,0:T(8,128)(2,1)S(1)}, f32[3,2,896]{2,1,0:T(2,128)S(1)}) custom-call(bf16[768,1152]{1,0:T(8,128)(2,1)S(1)} %fusion.19.qi.ki.vi, bf16[128,1152]{1,0:T(8,128)(2,1)S(1)} %fusion.28.qt.kt.vt, bf16[768,1152]{1,0:T(8,128)(2,1)S(1)} %fusion.19.qi.ki.vi, bf16[128,1152]{1,0:T(8,128)(2,1)S(1)} %fusion.28.qt.kt.vt, ...), custom_call_target="tpu_custom_call" | custom-call | flops 4932501504 | bytes 3096576 | tf_op jit(solution)/shard_map/pallas_call | solution.py:446
  140.8 5.4 collective-permute-done.17
  148.9 3.5 fusion.53
  153.1 5.5 collective-permute-done.32.core
  161.0 11.6 %collective-permute-done.22 = bf16[2,192,1536]{2,1,0:T(8,128)(2,1)} collective-permute-done((bf16[2,192,1536]{2,1,0:T(8,128)(2,1)}, bf16[2,192,1536]{2,1,0:T(8,128)(2,1)}, u32[]{:S(2)}, u32[]{:S(2)}) %collective-permute-start.22) | collective-permute-done | bytes 1179680 | tf_op jit(solution)/shard_map/ppermute | solution.py:70
  175.3 4.3 broadcast.262.clone.2
  189.2 9.7 %collective-permute-done.27 = bf16[2,192,1536]{2,1,0:T(8,128)(2,1)S(1)} collective-permute-done((bf16[2,192,1536]{2,1,0:T(8,128)(2,1)}, bf16[2,192,1536]{2,1,0:T(8,128)(2,1)S(1)}, u32[]{:S(2)}, u32[]{:S(2)}) %collective-permute-start.27) | collective-permute-done | bytes 1179680 | tf_op jit(solution)/shard_map/ppermute | solution.py:70
  226.3 5.2 collective-permute-done.24.over_y
  241.0 3.7 copy-done.37
  245.4 4.3 multiply_convert_fusion.1
  249.7 8.5 %multiply_convert_fusion = (bf16[768,1536]{1,0:T(8,128)(2,1)S(1)}, f32[768,1536]{1,0:T(8,128)}) fusion(f32[1536]{0:T(1024)S(1)} %get-tuple-element.386, bf16[768,1536]{1,0:T(8,128)(2,1)S(1)} %get-tuple-element.211, bf16[2,1536,1536]{2,1,0:T(8,128)(2,1)} %constant_dynamic-update-slice_fusion.9), kind=kOutput, calls=%fused_computation.20 | convolution fusion | flops 3635675136 | bytes 14161920 | tf_op jit(solution)/shard_map/dot_general | solution.py:33
  258.2 4.2 collective-permute-done.36
  266.1 4.1 convolution_convert_fusion.3
  270.4 18.0 %collective-permute-done.38 = bf16[2,192,1536]{2,1,0:T(8,128)(2,1)S(1)} collective-permute-done((bf16[2,192,1536]{2,1,0:T(8,128)(2,1)S(1)}, bf16[2,192,1536]{2,1,0:T(8,128)(2,1)S(1)}, u32[]{:S(2)}, u32[]{:S(2)}) %collective-permute-start.38) | collective-permute-done | bytes 1179680 | tf_op jit(solution)/shard_map/ppermute | solution.py:70
  291.2 10.6 %collective-permute-done.40 = bf16[2,96,1536]{2,1,0:T(8,128)(2,1)S(1)} collective-permute-done((bf16[2,96,1536]{2,1,0:T(8,128)(2,1)S(1)}, bf16[2,96,1536]{2,1,0:T(8,128)(2,1)S(1)}, u32[]{:S(2)}, u32[]{:S(2)}) %collective-permute-start.40) | collective-permute-done | bytes 589856 | tf_op jit(solution)/shard_map/ppermute | solution.py:70
  305.6 8.7 %convert_reduce_fusion = (f32[1536]{0:T(1024)}, bf16[768,1536]{1,0:T(8,128)(2,1)S(1)}) fusion(f32[768,1536]{1,0:T(8,128)} %get-tuple-element.517, f32[1536]{0:T(1024)S(1)} %get-tuple-element.386, bf16[768,1536]{1,0:T(8,128)(2,1)S(1)} %get-tuple-element.223, bf16[2,1536,1536]{2,1,0:T(8,128)(2,1)S(1)} %constant_dynamic-update-slice_fusion), kind=kOutput, calls=%fused_computation.19 | convolution fusion | flops 3651009024 | bytes 14170112 | tf_op jit(solution)/shard_map/dot_general | solution.py:33
  317.1 4.1 convert_reduce_fusion.3
  323.7 5.8 fusion.7
  331.5 4.6 fusion.10
  349.2 4.1 fusion.31.st
  353.3 4.8 collective-permute-done.47
  364.0 5.1 fusion.21.si
  370.9 3.6 convolution_convert_fusion.4
  374.5 5.6 convolution_convert_fusion.2
  380.1 9.0 %collective-permute-done.55 = bf16[2,192,1536]{2,1,0:T(8,128)(2,1)S(1)} collective-permute-done((bf16[2,192,1536]{2,1,0:T(8,128)(2,1)S(1)}, bf16[2,192,1536]{2,1,0:T(8,128)(2,1)S(1)}, u32[]{:S(2)}, u32[]{:S(2)}) %collective-permute-start.55) | collective-permute-done | bytes 1179680 | tf_op jit(solution)/shard_map/ppermute | solution.py:70
  396.9 4.0 fusion.16
  401.5 5.8 fusion.13
  407.3 3.9 fusion.30
  412.0 6.3 collective-permute-done.57
  425.9 5.7 collective-permute-done.59
  442.3 16.4 %shard_map.268 = (bf16[768,1152]{1,0:T(8,128)(2,1)S(1)}, bf16[128,1152]{1,0:T(8,128)(2,1)S(1)}) custom-call(bf16[768,1152]{1,0:T(8,128)(2,1)S(1)} %copy-done.31, bf16[128,1152]{1,0:T(8,128)(2,1)S(1)} %copy-done.29, bf16[768,1152]{1,0:T(8,128)(2,1)S(1)} %copy-done.31, bf16[128,1152]{1,0:T(8,128)(2,1)S(1)} %copy-done.29, bf16[768,1152]{1,0:T(8,128)(2,1)S(1)} %copy-done.31, ...), custom_call_target="tpu_custom_call" | custom-call | flops 12331253760 | bytes 5160960 | tf_op jit(solution)/shard_map/pallas_call | solution.py:517
  468.2 5.1 fusion.20
  475.1 3.7 fusion.22
  479.1 3.2 fusion.29.st
  482.4 9.0 %collective-permute-done.51 = bf16[224,1536]{1,0:T(8,128)(2,1)S(1)} collective-permute-done((bf16[224,1536]{1,0:T(8,128)(2,1)S(1)}, bf16[224,1536]{1,0:T(8,128)(2,1)S(1)}, u32[]{:S(2)}, u32[]{:S(2)}) %collective-permute-start.51) | collective-permute-done | bytes 688160 | tf_op jit(solution)/shard_map/ppermute | solution.py:247
  498.6 3.7 convolution_add_fusion.2.si
  506.0 3.5 convolution_convert_fusion.1
  509.5 12.5 %collective-permute-done.71 = bf16[2,192,1536]{2,1,0:T(8,128)(2,1)S(1)} collective-permute-done((bf16[2,192,1536]{2,1,0:T(8,128)(2,1)S(1)}, bf16[2,192,1536]{2,1,0:T(8,128)(2,1)S(1)}, u32[]{:S(2)}, u32[]{:S(2)}) %collective-permute-start.71) | collective-permute-done | bytes 1179680 | tf_op jit(solution)/shard_map/ppermute | solution.py:70
  533.4 5.9 collective-permute-done.73
  556.8 12.0 %collective-permute-done.75 = bf16[2,192,1536]{2,1,0:T(8,128)(2,1)} collective-permute-done((bf16[2,192,1536]{2,1,0:T(8,128)(2,1)}, bf16[2,192,1536]{2,1,0:T(8,128)(2,1)}, u32[]{:S(2)}, u32[]{:S(2)}) %collective-permute-start.75) | collective-permute-done | bytes 1179680 | tf_op jit(solution)/shard_map/ppermute | solution.py:70
  587.8 3.3 convolution_bitcast_fusion
  614.9 24.6 %collective-permute-done.85 = f32[4,192]{1,0:T(4,128)S(1)} collective-permute-done((f32[4,192]{1,0:T(4,128)S(1)}, f32[4,192]{1,0:T(4,128)S(1)}, u32[]{:S(2)}, u32[]{:S(2)}) %collective-permute-start.85) | collective-permute-done | bytes 3104 | tf_op jit(solution)/shard_map/ppermute | solution.py:215
  (647 shorter events, 283.3 us)
Async XLA Ops:
  3.1 19.3 %collective-permute-start = (f32[4,2,2304]{2,0,1:T(4,128)}, f32[4,2,2304]{2,0,1:T(4,128)}, u32[]{:S(2)}, u32[]{:S(2)}) collective-permute-start(f32[4,2,2304]{2,0,1:T(4,128)} %select_bitcast_fusion), channel_id=1, source_target_pairs={{0,4},{4,0},{8,12},{12,8},{16,20},{20,16},{24,28},{28,24},{1,5},{5... | collective-permute-start | bytes 221192 | tf_op jit(solution)/shard_map/ppermute | solution.py:179
  12.5 29.8 %collective-permute-start.2 = (bf16[2,192,1536]{2,1,0:T(8,128)(2,1)}, bf16[2,192,1536]{2,1,0:T(8,128)(2,1)}, u32[]{:S(2)}, u32[]{:S(2)}) collective-permute-start(bf16[2,192,1536]{2,1,0:T(8,128)(2,1)} %pad_maximum_fusion), channel_id=1, source_target_pairs={{0,8},{8,16},{16,24},{24,28},{28,20},{20,12},{12,4},{4,0},{1,9},{9... | collective-permute-start | bytes 3538952 | tf_op jit(solution)/shard_map/ppermute | solution.py:70
  14.1 28.2 %collective-permute-start.3 = (bf16[2,192,1536]{2,1,0:T(8,128)(2,1)}, bf16[2,192,1536]{2,1,0:T(8,128)(2,1)}, u32[]{:S(2)}, u32[]{:S(2)}) collective-permute-start(bf16[2,192,1536]{2,1,0:T(8,128)(2,1)} %pad_maximum_fusion), channel_id=1, source_target_pairs={{0,4},{8,0},{16,8},{24,16},{28,24},{20,28},{12,20},{4,12},{1,5},{9... | collective-permute-start | bytes 3538952 | tf_op jit(solution)/shard_map/ppermute | solution.py:73
  45.3 28.8 %collective-permute-start.11 = (bf16[2,192,1536]{2,1,0:T(8,128)(2,1)}, bf16[2,192,1536]{2,1,0:T(8,128)(2,1)}, u32[]{:S(2)}, u32[]{:S(2)}) collective-permute-start(bf16[2,192,1536]{2,1,0:T(8,128)(2,1)} %collective-permute-done.2), channel_id=1, source_target_pairs={{0,8},{8,16},{16,24},{24,28},{28,20},{20,12},{12,4},{4,0},{1,9},{9... | collective-permute-start | bytes 3538952 | tf_op jit(solution)/shard_map/ppermute | solution.py:70
  45.6 28.4 %collective-permute-start.12 = (bf16[2,192,1536]{2,1,0:T(8,128)(2,1)}, bf16[2,192,1536]{2,1,0:T(8,128)(2,1)}, u32[]{:S(2)}, u32[]{:S(2)}) collective-permute-start(bf16[2,192,1536]{2,1,0:T(8,128)(2,1)} %collective-permute-done.3), channel_id=1, source_target_pairs={{0,4},{8,0},{16,8},{24,16},{28,24},{20,28},{12,20},{4,12},{1,5},{9... | collective-permute-start | bytes 3538952 | tf_op jit(solution)/shard_map/ppermute | solution.py:73
  61.0 19.9 %collective-permute-start.9 = (bf16[224,1536]{1,0:T(8,128)(2,1)S(1)}, bf16[224,1536]{1,0:T(8,128)(2,1)S(1)}, u32[]{:S(2)}, u32[]{:S(2)}) collective-permute-start(bf16[224,1536]{1,0:T(8,128)(2,1)S(1)} %pad_maximum_fusion.2.own), channel_id=1, source_target_pairs={{0,1},{1,0},{2,3},{3,2},{4,5},{5,4},{6,7},{7,6},{8,9},{9,8},{10,11... | collective-permute-start | bytes 2064392 | tf_op jit(solution)/shard_map/ppermute | solution.py:243
  74.0 28.6 %collective-permute-start.13 = (bf16[2,192,1536]{2,1,0:T(8,128)(2,1)}, bf16[2,192,1536]{2,1,0:T(8,128)(2,1)S(1)}, u32[]{:S(2)}, u32[]{:S(2)}) collective-permute-start(bf16[2,192,1536]{2,1,0:T(8,128)(2,1)} %collective-permute-done.11), channel_id=1, source_target_pairs={{0,8},{8,16},{16,24},{24,28},{28,20},{20,12},{12,4},{4,0},{1,9},{9... | collective-permute-start | bytes 3538952 | tf_op jit(solution)/shard_map/ppermute | solution.py:70
  74.6 29.1 %collective-permute-start.14 = (bf16[2,192,1536]{2,1,0:T(8,128)(2,1)}, bf16[2,192,1536]{2,1,0:T(8,128)(2,1)S(1)}, u32[]{:S(2)}, u32[]{:S(2)}) collective-permute-start(bf16[2,192,1536]{2,1,0:T(8,128)(2,1)} %collective-permute-done.12), channel_id=1, source_target_pairs={{0,4},{8,0},{16,8},{24,16},{28,24},{20,28},{12,20},{4,12},{1,5},{9... | collective-permute-start | bytes 3538952 | tf_op jit(solution)/shard_map/ppermute | solution.py:73
  105.9 47.0 %collective-permute-start.31 = (bf16[224,1536]{1,0:T(8,128)(2,1)S(1)}, bf16[224,1536]{1,0:T(8,128)(2,1)}, u32[]{:S(2)}, u32[]{:S(2)}) collective-permute-start(bf16[224,1536]{1,0:T(8,128)(2,1)S(1)} %constant_dynamic-update-slice_fusion.37.own), channel_id=1, source_target_pairs={{0,2},{1,3},{2,0},{3,1},{4,6},{5,7},{6,4},{7,5},{8,10},{9,11},{10,... | collective-permute-start | bytes 2064392 | tf_op jit(solution)/shard_map/ppermute | solution.py:247
  119.9 26.2 %collective-permute-start.17 = (bf16[2,192,1536]{2,1,0:T(8,128)(2,1)S(1)}, bf16[2,192,1536]{2,1,0:T(8,128)(2,1)}, u32[]{:S(2)}, u32[]{:S(2)}) collective-permute-start(bf16[2,192,1536]{2,1,0:T(8,128)(2,1)S(1)} %bitcast.363), channel_id=1, source_target_pairs={{0,8},{8,16},{16,24},{24,28},{28,20},{20,12},{12,4},{4,0},{1,9},{9... | collective-permute-start | bytes 3538952 | tf_op jit(solution)/shard_map/ppermute | solution.py:70
  120.5 26.4 %collective-permute-start.18 = (bf16[2,192,1536]{2,1,0:T(8,128)(2,1)S(1)}, bf16[2,192,1536]{2,1,0:T(8,128)(2,1)}, u32[]{:S(2)}, u32[]{:S(2)}) collective-permute-start(bf16[2,192,1536]{2,1,0:T(8,128)(2,1)S(1)} %bitcast.364), channel_id=1, source_target_pairs={{0,4},{8,0},{16,8},{24,16},{28,24},{20,28},{12,20},{4,12},{1,5},{9... | collective-permute-start | bytes 3538952 | tf_op jit(solution)/shard_map/ppermute | solution.py:73
  146.9 25.7 %collective-permute-start.22 = (bf16[2,192,1536]{2,1,0:T(8,128)(2,1)}, bf16[2,192,1536]{2,1,0:T(8,128)(2,1)}, u32[]{:S(2)}, u32[]{:S(2)}) collective-permute-start(bf16[2,192,1536]{2,1,0:T(8,128)(2,1)} %collective-permute-done.17), channel_id=1, source_target_pairs={{0,8},{8,16},{16,24},{24,28},{28,20},{20,12},{12,4},{4,0},{1,9},{9... | collective-permute-start | bytes 3538952 | tf_op jit(solution)/shard_map/ppermute | solution.py:70
  147.5 25.8 %collective-permute-start.23 = (bf16[2,192,1536]{2,1,0:T(8,128)(2,1)}, bf16[2,192,1536]{2,1,0:T(8,128)(2,1)}, u32[]{:S(2)}, u32[]{:S(2)}) collective-permute-start(bf16[2,192,1536]{2,1,0:T(8,128)(2,1)} %collective-permute-done.18), channel_id=1, source_target_pairs={{0,4},{8,0},{16,8},{24,16},{28,24},{20,28},{12,20},{4,12},{1,5},{9... | collective-permute-start | bytes 3538952 | tf_op jit(solution)/shard_map/ppermute | solution.py:73
  152.4 49.4 %collective-permute-start.19 = (f32[384,1536]{1,0:T(8,128)}, f32[384,1536]{1,0:T(8,128)}, u32[]{:S(2)}, u32[]{:S(2)}) collective-permute-start(f32[384,1536]{1,0:T(8,128)} %fusion.53), channel_id=1, source_target_pairs={{0,1},{1,0},{2,3},{3,2},{4,5},{5,4},{6,7},{7,6},{8,9},{9,8},{10,11... | collective-permute-start | bytes 7077896 | tf_op jit(solution)/shard_map/ppermute | solution.py:243
  173.3 25.5 %collective-permute-start.27 = (bf16[2,192,1536]{2,1,0:T(8,128)(2,1)}, bf16[2,192,1536]{2,1,0:T(8,128)(2,1)S(1)}, u32[]{:S(2)}, u32[]{:S(2)}) collective-permute-start(bf16[2,192,1536]{2,1,0:T(8,128)(2,1)} %collective-permute-done.22), channel_id=1, source_target_pairs={{0,8},{8,16},{16,24},{24,28},{28,20},{20,12},{12,4},{4,0},{1,9},{9... | collective-permute-start | bytes 3538952 | tf_op jit(solution)/shard_map/ppermute | solution.py:70
  173.7 25.9 %collective-permute-start.28 = (bf16[2,192,1536]{2,1,0:T(8,128)(2,1)}, bf16[2,192,1536]{2,1,0:T(8,128)(2,1)S(1)}, u32[]{:S(2)}, u32[]{:S(2)}) collective-permute-start(bf16[2,192,1536]{2,1,0:T(8,128)(2,1)} %collective-permute-done.23), channel_id=1, source_target_pairs={{0,4},{8,0},{16,8},{24,16},{28,24},{20,28},{12,20},{4,12},{1,5},{9... | collective-permute-start | bytes 3538952 | tf_op jit(solution)/shard_map/ppermute | solution.py:73
  212.8 22.8 %collective-permute-start.34 = (bf16[2,192,1536]{2,1,0:T(8,128)(2,1)}, bf16[2,192,1536]{2,1,0:T(8,128)(2,1)}, u32[]{:S(2)}, u32[]{:S(2)}) collective-permute-start(bf16[2,192,1536]{2,1,0:T(8,128)(2,1)} %bitcast.27), channel_id=1, source_target_pairs={{0,8},{8,16},{16,24},{24,28},{28,20},{20,12},{12,4},{4,0},{1,9},{9... | collective-permute-start | bytes 3538952 | tf_op jit(solution)/shard_map/ppermute | solution.py:70
  213.3 22.9 %collective-permute-start.35 = (bf16[2,192,1536]{2,1,0:T(8,128)(2,1)}, bf16[2,192,1536]{2,1,0:T(8,128)(2,1)}, u32[]{:S(2)}, u32[]{:S(2)}) collective-permute-start(bf16[2,192,1536]{2,1,0:T(8,128)(2,1)} %bitcast.27), channel_id=1, source_target_pairs={{0,4},{8,0},{16,8},{24,16},{28,24},{20,28},{12,20},{4,12},{1,5},{9... | collective-permute-start | bytes 3538952 | tf_op jit(solution)/shard_map/ppermute | solution.py:73
  236.2 26.2 %collective-permute-start.36 = (bf16[2,192,1536]{2,1,0:T(8,128)(2,1)}, bf16[2,192,1536]{2,1,0:T(8,128)(2,1)S(1)}, u32[]{:S(2)}, u32[]{:S(2)}) collective-permute-start(bf16[2,192,1536]{2,1,0:T(8,128)(2,1)} %collective-permute-done.34), channel_id=1, source_target_pairs={{0,8},{8,16},{16,24},{24,28},{28,20},{20,12},{12,4},{4,0},{1,9},{9... | collective-permute-start | bytes 3538952 | tf_op jit(solution)/shard_map/ppermute | solution.py:70
  236.6 26.1 %collective-permute-start.37 = (bf16[2,192,1536]{2,1,0:T(8,128)(2,1)}, bf16[2,192,1536]{2,1,0:T(8,128)(2,1)S(1)}, u32[]{:S(2)}, u32[]{:S(2)}) collective-permute-start(bf16[2,192,1536]{2,1,0:T(8,128)(2,1)} %collective-permute-done.35), channel_id=1, source_target_pairs={{0,4},{8,0},{16,8},{24,16},{28,24},{20,28},{12,20},{4,12},{1,5},{9... | collective-permute-start | bytes 3538952 | tf_op jit(solution)/shard_map/ppermute | solution.py:73
  262.6 25.8 %collective-permute-start.38 = (bf16[2,192,1536]{2,1,0:T(8,128)(2,1)S(1)}, bf16[2,192,1536]{2,1,0:T(8,128)(2,1)S(1)}, u32[]{:S(2)}, u32[]{:S(2)}) collective-permute-start(bf16[2,192,1536]{2,1,0:T(8,128)(2,1)S(1)} %collective-permute-done.36), channel_id=1, source_target_pairs={{0,8},{8,16},{16,24},{24,28},{28,20},{20,12},{12,4},{4,0},{1,9},{9... | collective-permute-start | bytes 3538952 | tf_op jit(solution)/shard_map/ppermute | solution.py:70
  262.9 25.7 %collective-permute-start.39 = (bf16[2,192,1536]{2,1,0:T(8,128)(2,1)S(1)}, bf16[2,192,1536]{2,1,0:T(8,128)(2,1)S(1)}, u32[]{:S(2)}, u32[]{:S(2)}) collective-permute-start(bf16[2,192,1536]{2,1,0:T(8,128)(2,1)S(1)} %collective-permute-done.37), channel_id=1, source_target_pairs={{0,4},{8,0},{16,8},{24,16},{28,24},{20,28},{12,20},{4,12},{1,5},{9... | collective-permute-start | bytes 3538952 | tf_op jit(solution)/shard_map/ppermute | solution.py:73
  329.5 34.5 %collective-permute-start.44 = (f32[384,1536]{1,0:T(8,128)}, f32[384,1536]{1,0:T(8,128)}, u32[]{:S(2)}, u32[]{:S(2)}) collective-permute-start(f32[384,1536]{1,0:T(8,128)} %fusion.7), channel_id=1, source_target_pairs={{0,1},{1,0},{2,3},{3,2},{4,5},{5,4},{6,7},{7,6},{8,9},{9,8},{10,11... | collective-permute-start | bytes 7077896 | tf_op jit(solution)/shard_map/ppermute | solution.py:243
  329.5 28.7 %collective-permute-start.47 = (bf16[2,192,1536]{2,1,0:T(8,128)(2,1)}, bf16[2,192,1536]{2,1,0:T(8,128)(2,1)}, u32[]{:S(2)}, u32[]{:S(2)}) collective-permute-start(bf16[2,192,1536]{2,1,0:T(8,128)(2,1)} %add_convert_fusion.17), channel_id=1, source_target_pairs={{0,8},{8,16},{16,24},{24,28},{28,20},{20,12},{12,4},{4,0},{1,9},{9... | collective-permute-start | bytes 3538952 | tf_op jit(solution)/shard_map/ppermute | solution.py:70
  330.0 28.4 %collective-permute-start.48 = (bf16[2,192,1536]{2,1,0:T(8,128)(2,1)}, bf16[2,192,1536]{2,1,0:T(8,128)(2,1)}, u32[]{:S(2)}, u32[]{:S(2)}) collective-permute-start(bf16[2,192,1536]{2,1,0:T(8,128)(2,1)} %add_convert_fusion.16), channel_id=1, source_target_pairs={{0,4},{8,0},{16,8},{24,16},{28,24},{20,28},{12,20},{4,12},{1,5},{9... | collective-permute-start | bytes 3538952 | tf_op jit(solution)/shard_map/ppermute | solution.py:73
  361.6 27.4 %collective-permute-start.55 = (bf16[2,192,1536]{2,1,0:T(8,128)(2,1)S(1)}, bf16[2,192,1536]{2,1,0:T(8,128)(2,1)S(1)}, u32[]{:S(2)}, u32[]{:S(2)}) collective-permute-start(bf16[2,192,1536]{2,1,0:T(8,128)(2,1)S(1)} %add_convert_fusion.15), channel_id=1, source_target_pairs={{0,8},{8,16},{16,24},{24,28},{28,20},{20,12},{12,4},{4,0},{1,9},{9... | collective-permute-start | bytes 3538952 | tf_op jit(solution)/shard_map/ppermute | solution.py:70
  363.8 27.4 %collective-permute-start.56 = (bf16[2,192,1536]{2,1,0:T(8,128)(2,1)S(1)}, bf16[2,192,1536]{2,1,0:T(8,128)(2,1)S(1)}, u32[]{:S(2)}, u32[]{:S(2)}) collective-permute-start(bf16[2,192,1536]{2,1,0:T(8,128)(2,1)S(1)} %add_convert_fusion.14), channel_id=1, source_target_pairs={{0,4},{8,0},{16,8},{24,16},{28,24},{20,28},{12,20},{4,12},{1,5},{9... | collective-permute-start | bytes 3538952 | tf_op jit(solution)/shard_map/ppermute | solution.py:73
  369.3 24.7 %collective-permute-start.46 = (bf16[224,1536]{1,0:T(8,128)(2,1)S(1)}, bf16[224,1536]{1,0:T(8,128)(2,1)S(1)}, u32[]{:S(2)}, u32[]{:S(2)}) collective-permute-start(bf16[224,1536]{1,0:T(8,128)(2,1)S(1)} %pad_maximum_fusion.4), channel_id=1, source_target_pairs={{0,2},{1,3},{2,0},{3,1},{4,6},{5,7},{6,4},{7,5},{8,10},{9,11},{10,... | collective-permute-start | bytes 2064392 | tf_op jit(solution)/shard_map/ppermute | solution.py:247
  391.9 26.4 %collective-permute-start.57 = (bf16[2,192,1536]{2,1,0:T(8,128)(2,1)S(1)}, bf16[2,192,1536]{2,1,0:T(8,128)(2,1)S(1)}, u32[]{:S(2)}, u32[]{:S(2)}) collective-permute-start(bf16[2,192,1536]{2,1,0:T(8,128)(2,1)S(1)} %add_convert_fusion.13), channel_id=1, source_target_pairs={{0,8},{8,16},{16,24},{24,28},{28,20},{20,12},{12,4},{4,0},{1,9},{9... | collective-permute-start | bytes 3538952 | tf_op jit(solution)/shard_map/ppermute | solution.py:70
  393.4 25.7 %collective-permute-start.58 = (bf16[2,192,1536]{2,1,0:T(8,128)(2,1)S(1)}, bf16[2,192,1536]{2,1,0:T(8,128)(2,1)S(1)}, u32[]{:S(2)}, u32[]{:S(2)}) collective-permute-start(bf16[2,192,1536]{2,1,0:T(8,128)(2,1)S(1)} %add_convert_fusion.12), channel_id=1, source_target_pairs={{0,4},{8,0},{16,8},{24,16},{28,24},{20,28},{12,20},{4,12},{1,5},{9... | collective-permute-start | bytes 3538952 | tf_op jit(solution)/shard_map/ppermute | solution.py:73
  395.3 29.2 %collective-permute-start.52 = (bf16[224,1536]{1,0:T(8,128)(2,1)S(1)}, bf16[224,1536]{1,0:T(8,128)(2,1)S(1)}, u32[]{:S(2)}, u32[]{:S(2)}) collective-permute-start(bf16[224,1536]{1,0:T(8,128)(2,1)S(1)} %get-tuple-element.257.own), channel_id=1, source_target_pairs={{0,2},{1,3},{2,0},{3,1},{4,6},{5,7},{6,4},{7,5},{8,10},{9,11},{10,... | collective-permute-start | bytes 2064392 | tf_op jit(solution)/shard_map/ppermute | solution.py:247
  396.9 40.3 %collective-permute-start.53 = (bf16[224,1536]{1,0:T(8,128)(2,1)S(1)}, bf16[224,1536]{1,0:T(8,128)(2,1)S(1)}, u32[]{:S(2)}, u32[]{:S(2)}) collective-permute-start(bf16[224,1536]{1,0:T(8,128)(2,1)S(1)} %get-tuple-element.257.own), channel_id=1, source_target_pairs={{0,1},{1,0},{2,3},{3,2},{4,5},{5,4},{6,7},{7,6},{8,9},{9,8},{10,11... | collective-permute-start | bytes 2064392 | tf_op jit(solution)/shard_map/ppermute | solution.py:243
  407.3 61.0 %collective-permute-start.49 = (f32[384,1536]{1,0:T(8,128)}, f32[384,1536]{1,0:T(8,128)}, u32[]{:S(2)}, u32[]{:S(2)}) collective-permute-start(f32[384,1536]{1,0:T(8,128)} %fusion.13), channel_id=1, source_target_pairs={{0,1},{1,0},{2,3},{3,2},{4,5},{5,4},{6,7},{7,6},{8,9},{9,8},{10,11... | collective-permute-start | bytes 7077896 | tf_op jit(solution)/shard_map/ppermute | solution.py:243
  434.7 24.0 %collective-permute-start.61 = (bf16[2,192,1536]{2,1,0:T(8,128)(2,1)}, bf16[2,192,1536]{2,1,0:T(8,128)(2,1)}, u32[]{:S(2)}, u32[]{:S(2)}) collective-permute-start(bf16[2,192,1536]{2,1,0:T(8,128)(2,1)} %add_convert_fusion.11), channel_id=1, source_target_pairs={{0,8},{8,16},{16,24},{24,28},{28,20},{20,12},{12,4},{4,0},{1,9},{9... | collective-permute-start | bytes 3538952 | tf_op jit(solution)/shard_map/ppermute | solution.py:70
  435.5 24.0 %collective-permute-start.62 = (bf16[2,192,1536]{2,1,0:T(8,128)(2,1)}, bf16[2,192,1536]{2,1,0:T(8,128)(2,1)}, u32[]{:S(2)}, u32[]{:S(2)}) collective-permute-start(bf16[2,192,1536]{2,1,0:T(8,128)(2,1)} %add_convert_fusion.10), channel_id=1, source_target_pairs={{0,4},{8,0},{16,8},{24,16},{28,24},{20,28},{12,20},{4,12},{1,5},{9... | collective-permute-start | bytes 3538952 | tf_op jit(solution)/shard_map/ppermute | solution.py:73
  462.9 30.9 %collective-permute-start.66 = (bf16[2,192,1536]{2,1,0:T(8,128)(2,1)S(1)}, bf16[2,192,1536]{2,1,0:T(8,128)(2,1)S(1)}, u32[]{:S(2)}, u32[]{:S(2)}) collective-permute-start(bf16[2,192,1536]{2,1,0:T(8,128)(2,1)S(1)} %add_convert_fusion.9), channel_id=1, source_target_pairs={{0,8},{8,16},{16,24},{24,28},{28,20},{20,12},{12,4},{4,0},{1,9},{9... | collective-permute-start | bytes 3538952 | tf_op jit(solution)/shard_map/ppermute | solution.py:70
  463.8 29.9 %collective-permute-start.67 = (bf16[2,192,1536]{2,1,0:T(8,128)(2,1)S(1)}, bf16[2,192,1536]{2,1,0:T(8,128)(2,1)S(1)}, u32[]{:S(2)}, u32[]{:S(2)}) collective-permute-start(bf16[2,192,1536]{2,1,0:T(8,128)(2,1)S(1)} %add_convert_fusion.8), channel_id=1, source_target_pairs={{0,4},{8,0},{16,8},{24,16},{28,24},{20,28},{12,20},{4,12},{1,5},{9... | collective-permute-start | bytes 3538952 | tf_op jit(solution)/shard_map/ppermute | solution.py:73
  478.9 19.7 %collective-permute-start.63 = (f32[384,1536]{1,0:T(8,128)S(1)}, f32[384,1536]{1,0:T(8,128)S(1)}, u32[]{:S(2)}, u32[]{:S(2)}) collective-permute-start(f32[384,1536]{1,0:T(8,128)S(1)} %fusion.22), channel_id=1, source_target_pairs={{0,1},{1,0},{2,3},{3,2},{4,5},{5,4},{6,7},{7,6},{8,9},{9,8},{10,11... | collective-permute-start | bytes 7077896 | tf_op jit(solution)/shard_map/ppermute | solution.py:243
  494.4 27.6 %collective-permute-start.71 = (bf16[2,192,1536]{2,1,0:T(8,128)(2,1)S(1)}, bf16[2,192,1536]{2,1,0:T(8,128)(2,1)S(1)}, u32[]{:S(2)}, u32[]{:S(2)}) collective-permute-start(bf16[2,192,1536]{2,1,0:T(8,128)(2,1)S(1)} %add_convert_fusion.7), channel_id=1, source_target_pairs={{0,8},{8,16},{16,24},{24,28},{28,20},{20,12},{12,4},{4,0},{1,9},{9... | collective-permute-start | bytes 3538952 | tf_op jit(solution)/shard_map/ppermute | solution.py:70
  495.4 27.4 %collective-permute-start.72 = (bf16[2,192,1536]{2,1,0:T(8,128)(2,1)S(1)}, bf16[2,192,1536]{2,1,0:T(8,128)(2,1)S(1)}, u32[]{:S(2)}, u32[]{:S(2)}) collective-permute-start(bf16[2,192,1536]{2,1,0:T(8,128)(2,1)S(1)} %add_convert_fusion.6), channel_id=1, source_target_pairs={{0,4},{8,0},{16,8},{24,16},{28,24},{20,28},{12,20},{4,12},{1,5},{9... | collective-permute-start | bytes 3538952 | tf_op jit(solution)/shard_map/ppermute | solution.py:73
  502.4 43.2 %collective-permute-start.65 = (bf16[224,1536]{1,0:T(8,128)(2,1)S(1)}, bf16[224,1536]{1,0:T(8,128)(2,1)S(1)}, u32[]{:S(2)}, u32[]{:S(2)}) collective-permute-start(bf16[224,1536]{1,0:T(8,128)(2,1)S(1)} %pad_maximum_fusion.6), channel_id=1, source_target_pairs={{0,2},{1,3},{2,0},{3,1},{4,6},{5,7},{6,4},{7,5},{8,10},{9,11},{10,... | collective-permute-start | bytes 2064392 | tf_op jit(solution)/shard_map/ppermute | solution.py:247
  542.8 26.0 %collective-permute-start.75 = (bf16[2,192,1536]{2,1,0:T(8,128)(2,1)}, bf16[2,192,1536]{2,1,0:T(8,128)(2,1)}, u32[]{:S(2)}, u32[]{:S(2)}) collective-permute-start(bf16[2,192,1536]{2,1,0:T(8,128)(2,1)} %add_convert_fusion.5), channel_id=1, source_target_pairs={{0,8},{8,16},{16,24},{24,28},{28,20},{20,12},{12,4},{4,0},{1,9},{9... | collective-permute-start | bytes 3538952 | tf_op jit(solution)/shard_map/ppermute | solution.py:70
  543.7 25.7 %collective-permute-start.76 = (bf16[2,192,1536]{2,1,0:T(8,128)(2,1)}, bf16[2,192,1536]{2,1,0:T(8,128)(2,1)}, u32[]{:S(2)}, u32[]{:S(2)}) collective-permute-start(bf16[2,192,1536]{2,1,0:T(8,128)(2,1)} %add_convert_fusion.4), channel_id=1, source_target_pairs={{0,4},{8,0},{16,8},{24,16},{28,24},{20,28},{12,20},{4,12},{1,5},{9... | collective-permute-start | bytes 3538952 | tf_op jit(solution)/shard_map/ppermute | solution.py:73
  579.6 27.8 %collective-permute-start.86 = (bf16[2,192,1536]{2,1,0:T(8,128)(2,1)}, bf16[2,192,1536]{2,1,0:T(8,128)(2,1)}, u32[]{:S(2)}, u32[]{:S(2)}) collective-permute-start(bf16[2,192,1536]{2,1,0:T(8,128)(2,1)} %add_convert_fusion.3), channel_id=1, source_target_pairs={{0,8},{8,16},{16,24},{24,28},{28,20},{20,12},{12,4},{4,0},{1,9},{9... | collective-permute-start | bytes 3538952 | tf_op jit(solution)/shard_map/ppermute | solution.py:70
  581.0 26.4 %collective-permute-start.87 = (bf16[2,192,1536]{2,1,0:T(8,128)(2,1)}, bf16[2,192,1536]{2,1,0:T(8,128)(2,1)}, u32[]{:S(2)}, u32[]{:S(2)}) collective-permute-start(bf16[2,192,1536]{2,1,0:T(8,128)(2,1)} %add_convert_fusion.2), channel_id=1, source_target_pairs={{0,4},{8,0},{16,8},{24,16},{28,24},{20,28},{12,20},{4,12},{1,5},{9... | collective-permute-start | bytes 3538952 | tf_op jit(solution)/shard_map/ppermute | solution.py:73
  612.7 28.4 %collective-permute-start.88 = (bf16[2,192,1536]{2,1,0:T(8,128)(2,1)}, bf16[2,192,1536]{2,1,0:T(8,128)(2,1)}, u32[]{:S(2)}, u32[]{:S(2)}) collective-permute-start(bf16[2,192,1536]{2,1,0:T(8,128)(2,1)} %add_convert_fusion.1), channel_id=1, source_target_pairs={{0,8},{8,16},{16,24},{24,28},{28,20},{20,12},{12,4},{4,0},{1,9},{9... | collective-permute-start | bytes 3538952 | tf_op jit(solution)/shard_map/ppermute | solution.py:70
  612.7 28.4 %collective-permute-start.89 = (bf16[2,192,1536]{2,1,0:T(8,128)(2,1)}, bf16[2,192,1536]{2,1,0:T(8,128)(2,1)}, u32[]{:S(2)}, u32[]{:S(2)}) collective-permute-start(bf16[2,192,1536]{2,1,0:T(8,128)(2,1)} %add_convert_fusion), channel_id=1, source_target_pairs={{0,4},{8,0},{16,8},{24,16},{28,24},{20,28},{12,20},{4,12},{1,5},{9... | collective-permute-start | bytes 3538952 | tf_op jit(solution)/shard_map/ppermute | solution.py:73
  614.7 24.7 %collective-permute-start.85 = (f32[4,192]{1,0:T(4,128)S(1)}, f32[4,192]{1,0:T(4,128)S(1)}, u32[]{:S(2)}, u32[]{:S(2)}) collective-permute-start(f32[4,192]{1,0:T(4,128)S(1)} %bitcast.373), channel_id=1, source_target_pairs={{0,4},{4,0},{8,12},{12,8},{16,20},{20,16},{24,28},{28,24},{1,5},{5... | collective-permute-start | bytes 9224 | tf_op jit(solution)/shard_map/ppermute | solution.py:215
  (156 other events, 1793.0 us)
